TPU v7x, 32 devices: a whole 2x2x4 slice. The times are simulated.
32 devices in a mesh: space: 8 (over z, x), rep: 4 (over y, core).
Axes of the slice: x: 2, y: 2, z: 4, core: 2. Of those that a mesh axis runs over, the one named last changes fastest.
Arguments:
- atom_features: float32 [32768, 64], P('space'), may hold values from -6 to 6
- bond_features: bfloat16 [32768, 1024], P(('space', 'rep')), may hold values from -6 to 6
- offsets: int32 [32768, 16], P(('space', 'rep')), may hold values from -2048 to 2048, as said below
- counts: int32 [32768], P(('space', 'rep')), may hold values from 8 to 16
- cosines: float32 [32768, 256], P(('space', 'rep')), may hold values from -1 to 1
- weight_core: bfloat16 [2, 192, 192], replicated, may hold values from -0.4375 to 0.4375
- weight_atom: bfloat16 [2, 64, 64], replicated, may hold values from -0.75 to 0.75
- weight_pair: bfloat16 [2, 64, 128], replicated, may hold values from -0.75 to 0.75
- weight_cosine: float32 [2, 64], replicated, may hold values from -6 to 6
- weight_bond: bfloat16 [2, 64, 64], replicated, may hold values from -0.75 to 0.75
- weight_energy: float32 [64], replicated, may hold values from -0.75 to 0.75
Outputs:
- atoms_out: float32 [32768, 64], P(('space', 'rep'))
- bonds_out: bfloat16 [32768, 1024], P(('space', 'rep'))
- energy: float32 [], replicated
Inputs may be any that keep to these rules, and one draw needn't show every extreme that they name: `offsets`: never zero; |offset| is at most 2048.
All inputs are finite; a program needn't handle non-finite values.
Results may differ from a plain program's by a relative error of at most 0.0045.
Values may be sent and summed in bfloat16 or wider, within the bound.
No kernel may reach another device: no remote copies, remote signals or barrier semaphores. Data moves between devices by JAX's collectives and lax.ppermute only.
A program may use at most 64 MiB of HBM per device.

v0:
```python
import math

import jax
import jax.numpy as jnp
from jax import lax
from jax.sharding import PartitionSpec as P

LAYERS = 2


def padded_2(cells, sides, width):
    for axis, dim in sides:
        count = lax.axis_size(axis)
        head = lax.slice_in_dim(cells, 0, width, axis=dim)
        tail = lax.slice_in_dim(cells, cells.shape[dim] - width, cells.shape[dim], axis=dim)
        cells = jnp.concatenate(
            [
                lax.ppermute(tail, axis, [(i, (i + 1) % count) for i in range(count)]),
                cells,
                lax.ppermute(head, axis, [((i + 1) % count, i) for i in range(count)]),
            ],
            axis=dim,
        )
    return cells


def passed_along(value, axis, steps):
    count = lax.axis_size(axis)
    pairs = [(source, (source + steps) % count) for source in range(count)]
    return lax.ppermute(value, axis, pairs)


def interact(
    h_rows,
    neighbours,
    e_rows,
    cnt_rows,
    cos_rows,
    weight_core,
    weight_atom,
    weight_pair,
    weight_cosine,
    weight_bond,
):
    row_count = h_rows.shape[0]
    channels = h_rows.shape[1]
    slot_count = e_rows.shape[1] // channels
    bond_rows = e_rows.reshape(row_count, slot_count, channels)
    centre = jnp.broadcast_to(
        h_rows.astype(jnp.bfloat16)[:, None, :], (row_count, slot_count, channels)
    )
    joined = jnp.concatenate([centre, neighbours, bond_rows], axis=2).reshape(
        row_count * slot_count, 3 * channels
    )
    mixed_all = jnp.dot(joined, weight_core, preferred_element_type=jnp.float32).reshape(
        row_count, slot_count, 3 * channels
    )
    live_mask = (jnp.arange(slot_count, dtype=jnp.int32)[None, :] < cnt_rows[:, None]).astype(
        jnp.float32
    )
    inverse_count = 1.0 / cnt_rows.astype(jnp.float32)
    message = (
        jax.nn.sigmoid(mixed_all[..., :channels])
        * jax.nn.silu(mixed_all[..., channels : 2 * channels])
        * live_mask[..., None]
    )
    summed = (jnp.sum(message, axis=1) * inverse_count[:, None]).astype(jnp.bfloat16)
    atom_next = h_rows + jnp.dot(summed, weight_atom, preferred_element_type=jnp.float32)
    paired = jnp.dot(
        bond_rows.reshape(row_count * slot_count, channels),
        weight_pair,
        preferred_element_type=jnp.float32,
    ).reshape(row_count, slot_count, 2 * channels)
    cosine_tile = cos_rows.reshape(row_count, slot_count, slot_count)
    angle_input = (
        paired[:, :, None, :channels]
        + paired[:, None, :, channels:]
        + cosine_tile[..., None] * weight_cosine
    )
    pair_mask = (
        live_mask[:, :, None]
        * live_mask[:, None, :]
        * (1.0 - jnp.eye(slot_count, dtype=jnp.float32))
    )
    angular = (
        jnp.sum(jax.nn.silu(angle_input) * pair_mask[..., None], axis=2)
        * inverse_count[:, None, None]
    ).astype(jnp.bfloat16)
    update = jnp.dot(
        angular.reshape(row_count * slot_count, channels),
        weight_bond,
        preferred_element_type=jnp.float32,
    ).reshape(row_count, slot_count, channels)
    update = update * jax.nn.sigmoid(mixed_all[..., 2 * channels :]) * live_mask[..., None]
    bond_next = (
        (bond_rows.astype(jnp.float32) + update)
        .astype(jnp.bfloat16)
        .reshape(row_count, slot_count * channels)
    )
    return (atom_next, bond_next)


def per_device(
    atom_features,
    bond_features,
    offsets,
    counts,
    cosines,
    weight_core,
    weight_atom,
    weight_pair,
    weight_cosine,
    weight_bond,
    weight_energy,
):
    rep_index = lax.axis_index("rep")
    quarter = bond_features.shape[0]
    domain = atom_features.shape[0]
    channels = atom_features.shape[1]
    slot_count = offsets.shape[1]
    rim = 2 * quarter
    block_rows = math.gcd(quarter, 128)
    number = quarter // block_rows
    window = block_rows + 2 * rim
    starts = jnp.arange(number, dtype=jnp.int32) * block_rows
    own_rows = lax.dynamic_slice_in_dim(atom_features, rep_index * quarter, quarter, 0)
    bonds_now = bond_features
    columns = jnp.arange(window, dtype=jnp.int32)
    inside = jnp.arange(block_rows, dtype=jnp.int32)[:, None] + rim
    for layer_index in range(LAYERS):
        own_table = own_rows.astype(jnp.bfloat16)
        near = padded_2(own_table, ((("space", "rep"), 0),), quarter)
        far_pieces = []
        for distance in (2, -2):
            far_pieces.append(passed_along(own_table, ("space", "rep"), distance))
        padded = jnp.concatenate([far_pieces[0], near, far_pieces[1]], axis=0)

        def block_step(items):
            block_start, h_rows, e_rows, off_rows, cnt_rows, cos_rows = items
            window_rows = lax.dynamic_slice_in_dim(padded, rim + block_start - rim, window, 0)
            local_ids = (inside + off_rows).reshape(block_rows * slot_count)
            one_hot = (local_ids[:, None] == columns[None, :]).astype(jnp.bfloat16)
            picked = jnp.dot(one_hot, window_rows, preferred_element_type=jnp.float32)
            neighbours = picked.astype(jnp.bfloat16).reshape(block_rows, slot_count, channels)
            return interact(
                h_rows,
                neighbours,
                e_rows,
                cnt_rows,
                cos_rows,
                weight_core[layer_index],
                weight_atom[layer_index],
                weight_pair[layer_index],
                weight_cosine[layer_index],
                weight_bond[layer_index],
            )

        atom_next, bond_next = lax.map(
            block_step,
            (
                starts,
                own_rows.reshape(number, block_rows, -1),
                bonds_now.reshape(number, block_rows, -1),
                offsets.reshape(number, block_rows, -1),
                counts.reshape(number, block_rows),
                cosines.reshape(number, block_rows, -1),
            ),
        )
        own_rows = atom_next.reshape(quarter, -1)
        bonds_now = bond_next.reshape(quarter, -1)
    energy_sum = lax.psum(jnp.sum(own_rows * weight_energy), ("space", "rep"))
    energy = energy_sum / math.sqrt(lax.axis_size("space") * domain)
    return (own_rows, bonds_now, energy)


def solution(mesh):
    return jax.shard_map(
        per_device,
        mesh=mesh,
        in_specs=(
            P("space", None),
            P(("space", "rep"), None),
            P(("space", "rep"), None),
            P(("space", "rep")),
            P(("space", "rep"), None),
            P(),
            P(),
            P(),
            P(),
            P(),
            P(),
        ),
        out_specs=(P(("space", "rep"), None), P(("space", "rep"), None), P()),
        check_vma=False,
    )
```

profile of v0, /device:TPU:0, one launch (start us, length us, event | category | flops | bytes accessed | tf_op | source)
XLA Modules:
  0.0 452.9 jit_solution(13015361954599620634)
XLA Ops:
  0.7 1.2 copy-done
  2.1 3.0 collective-permute-start
  5.2 5.3 %collective-permute-start.2 = (bf16[1024,64]{1,0:T(8,128)(2,1)S(1)}, bf16[1024,64]{1,0:T(8,128)(2,1)}, u32[]{:S(2)}, u32[]{:S(2)}) collective-permute-start(bf16[1024,64]{1,0:T(8,128)(2,1)S(1)} %convert_element_type.245), channel_id=1, source_target_pairs={{1,0},{2,1},{3,2},{4,3},{5,4},{6,5},{7,6},{8,7},{9,8},{10,9},{11,1... | collective-permute-start | bytes 393224 | tf_op jit(solution)/shard_map/ppermute | solution.py:20
  11.1 1.3 copy.127
  12.5 1.0 copy.138
  13.5 1.1 copy.126
  14.7 5.6 %collective-permute-done = bf16[1024,64]{1,0:T(8,128)(2,1)} collective-permute-done((bf16[1024,64]{1,0:T(8,128)(2,1)S(1)}, bf16[1024,64]{1,0:T(8,128)(2,1)}, u32[]{:S(2)}, u32[]{:S(2)}) %collective-permute-start) | collective-permute-done | bytes 131104 | tf_op jit(solution)/shard_map/ppermute | solution.py:30
  21.3 1.0 constant_dynamic-update-slice_fusion.5
  22.3 1.0 constant_dynamic-update-slice_fusion.3
  23.3 3.0 collective-permute-done.3
  26.3 1.0 constant_dynamic-update-slice_fusion.2
  28.4 172.6 %while.34 = (s32[]{:T(128)}, f32[8,128,64]{1,2,0:T(8,128)}, bf16[8,128,1024]{1,2,0:T(8,128)(2,1)}, f32[8,128,64]{1,2,0:T(8,128)S(1)}, s32[8,128,16]{2,1,0:T(8,12...) while((s32[]{:T(128)}, f32[8,128,64]{1,2,0:T(8,128)}, ...), condition=%wide.region_3.4_spmd.clone, body=%wide.region_0.3_spmd.clone.sunk | while | flops 1342266496 | bytes 15302635 | solution.py:158
  31.8 8.6 %fusion.130 = bf16[2048,64]{0,1:T(8,128)(2,1)S(1)} fusion(s32[2048]{0:T(1024)S(1)} %add.497, bf16[5120,64]{1,0:T(8,128)(2,1)} %get-tuple-element.1195, s32[]{:T(128)S(6)} %select_n.26), kind=kOutput, calls=%fused_computation.8.clone.1 | convolution fusion | flops 1116078080 | bytes 1351684 | tf_op jit(solution)/shard_map/while/body/eval_jaxpr/dot_general | solution.py:143
  44.9 2.9 multiply_reduce_fusion.5
  53.4 8.6 %fusion.130 = bf16[2048,64]{0,1:T(8,128)(2,1)S(1)} fusion(s32[2048]{0:T(1024)S(1)} %add.497, bf16[5120,64]{1,0:T(8,128)(2,1)} %get-tuple-element.1195, s32[]{:T(128)S(6)} %select_n.26), kind=kOutput, calls=%fused_computation.8.clone.1 | convolution fusion | flops 1116078080 | bytes 1351684 | tf_op jit(solution)/shard_map/while/body/eval_jaxpr/dot_general | solution.py:143
  66.5 2.9 multiply_reduce_fusion.5
  75.0 8.6 %fusion.130 = bf16[2048,64]{0,1:T(8,128)(2,1)S(1)} fusion(s32[2048]{0:T(1024)S(1)} %add.497, bf16[5120,64]{1,0:T(8,128)(2,1)} %get-tuple-element.1195, s32[]{:T(128)S(6)} %select_n.26), kind=kOutput, calls=%fused_computation.8.clone.1 | convolution fusion | flops 1116078080 | bytes 1351684 | tf_op jit(solution)/shard_map/while/body/eval_jaxpr/dot_general | solution.py:143
  88.1 2.9 multiply_reduce_fusion.5
  96.5 8.6 %fusion.130 = bf16[2048,64]{0,1:T(8,128)(2,1)S(1)} fusion(s32[2048]{0:T(1024)S(1)} %add.497, bf16[5120,64]{1,0:T(8,128)(2,1)} %get-tuple-element.1195, s32[]{:T(128)S(6)} %select_n.26), kind=kOutput, calls=%fused_computation.8.clone.1 | convolution fusion | flops 1116078080 | bytes 1351684 | tf_op jit(solution)/shard_map/while/body/eval_jaxpr/dot_general | solution.py:143
  109.7 2.9 multiply_reduce_fusion.5
  118.1 8.6 %fusion.130 = bf16[2048,64]{0,1:T(8,128)(2,1)S(1)} fusion(s32[2048]{0:T(1024)S(1)} %add.497, bf16[5120,64]{1,0:T(8,128)(2,1)} %get-tuple-element.1195, s32[]{:T(128)S(6)} %select_n.26), kind=kOutput, calls=%fused_computation.8.clone.1 | convolution fusion | flops 1116078080 | bytes 1351684 | tf_op jit(solution)/shard_map/while/body/eval_jaxpr/dot_general | solution.py:143
  131.3 2.9 multiply_reduce_fusion.5
  139.7 8.6 %fusion.130 = bf16[2048,64]{0,1:T(8,128)(2,1)S(1)} fusion(s32[2048]{0:T(1024)S(1)} %add.497, bf16[5120,64]{1,0:T(8,128)(2,1)} %get-tuple-element.1195, s32[]{:T(128)S(6)} %select_n.26), kind=kOutput, calls=%fused_computation.8.clone.1 | convolution fusion | flops 1116078080 | bytes 1351684 | tf_op jit(solution)/shard_map/while/body/eval_jaxpr/dot_general | solution.py:143
  152.8 2.9 multiply_reduce_fusion.5
  161.3 8.6 %fusion.130 = bf16[2048,64]{0,1:T(8,128)(2,1)S(1)} fusion(s32[2048]{0:T(1024)S(1)} %add.497, bf16[5120,64]{1,0:T(8,128)(2,1)} %get-tuple-element.1195, s32[]{:T(128)S(6)} %select_n.26), kind=kOutput, calls=%fused_computation.8.clone.1 | convolution fusion | flops 1116078080 | bytes 1351684 | tf_op jit(solution)/shard_map/while/body/eval_jaxpr/dot_general | solution.py:143
  174.4 2.9 multiply_reduce_fusion.5
  182.9 8.6 %fusion.130 = bf16[2048,64]{0,1:T(8,128)(2,1)S(1)} fusion(s32[2048]{0:T(1024)S(1)} %add.497, bf16[5120,64]{1,0:T(8,128)(2,1)} %get-tuple-element.1195, s32[]{:T(128)S(6)} %select_n.26), kind=kOutput, calls=%fused_computation.8.clone.1 | convolution fusion | flops 1116078080 | bytes 1351684 | tf_op jit(solution)/shard_map/while/body/eval_jaxpr/dot_general | solution.py:143
  196.0 2.9 multiply_reduce_fusion.5
  202.6 5.3 %collective-permute-start.6 = (bf16[1024,64]{1,0:T(8,128)(2,1)S(1)}, bf16[1024,64]{1,0:T(8,128)(2,1)S(1)}, u32[]{:S(2)}, u32[]{:S(2)}) collective-permute-start(bf16[1024,64]{1,0:T(8,128)(2,1)S(1)} %bitcast.158), channel_id=1, source_target_pairs={{1,0},{2,1},{3,2},{4,3},{5,4},{6,5},{7,6},{8,7},{9,8},{10,9},{11,1... | collective-permute-start | bytes 393224 | tf_op jit(solution)/shard_map/ppermute | solution.py:20
  207.9 1.7 collective-permute-start.7
  209.6 7.9 %collective-permute-done.4 = bf16[1024,64]{1,0:T(8,128)(2,1)S(1)} collective-permute-done((bf16[1024,64]{1,0:T(8,128)(2,1)S(1)}, bf16[1024,64]{1,0:T(8,128)(2,1)S(1)}, u32[]{:S(2)}, u32[]{:S(2)}) %collective-permute-start.4) | collective-permute-done | bytes 131104 | tf_op jit(solution)/shard_map/ppermute | solution.py:30
  220.4 2.6 collective-permute-done.7
  224.4 184.7 %while.35 = (s32[]{:T(128)}, f32[8,128,64]{1,2,0:T(8,128)}, bf16[8,128,1024]{2,1,0:T(8,128)(2,1)}, f32[8,128,64]{1,2,0:T(8,128)}, s32[8,128,16]{2,1,0:T(8,128)},...) while((s32[]{:T(128)}, f32[8,128,64]{1,2,0:T(8,128)}, ...), condition=%wide.region_7.8_spmd.clone, body=%wide.region_4.7_spmd.clone.sunk | while | flops 1342266496 | bytes 15302635 | solution.py:158
  227.9 8.6 %fusion.145 = bf16[2048,64]{0,1:T(8,128)(2,1)S(1)} fusion(s32[2048]{0:T(1024)S(1)} %add.514, bf16[5120,64]{1,0:T(8,128)(2,1)} %get-tuple-element.1249, s32[]{:T(128)S(6)} %select_n.27), kind=kOutput, calls=%fused_computation.68.clone.1 | convolution fusion | flops 1116078080 | bytes 1351684 | tf_op jit(solution)/shard_map/while/body/eval_jaxpr/dot_general | solution.py:143
  237.2 1.0 constant_dynamic-slice_fusion.18
  241.6 2.9 multiply_reduce_fusion.6
  246.0 1.6 fusion.149
  251.0 8.6 %fusion.145 = bf16[2048,64]{0,1:T(8,128)(2,1)S(1)} fusion(s32[2048]{0:T(1024)S(1)} %add.514, bf16[5120,64]{1,0:T(8,128)(2,1)} %get-tuple-element.1249, s32[]{:T(128)S(6)} %select_n.27), kind=kOutput, calls=%fused_computation.68.clone.1 | convolution fusion | flops 1116078080 | bytes 1351684 | tf_op jit(solution)/shard_map/while/body/eval_jaxpr/dot_general | solution.py:143
  264.6 2.9 multiply_reduce_fusion.6
  269.1 1.6 fusion.149
  274.0 8.6 %fusion.145 = bf16[2048,64]{0,1:T(8,128)(2,1)S(1)} fusion(s32[2048]{0:T(1024)S(1)} %add.514, bf16[5120,64]{1,0:T(8,128)(2,1)} %get-tuple-element.1249, s32[]{:T(128)S(6)} %select_n.27), kind=kOutput, calls=%fused_computation.68.clone.1 | convolution fusion | flops 1116078080 | bytes 1351684 | tf_op jit(solution)/shard_map/while/body/eval_jaxpr/dot_general | solution.py:143
  283.4 1.0 constant_dynamic-slice_fusion.18
  287.7 2.9 multiply_reduce_fusion.6
  292.1 1.6 fusion.149
  297.1 8.6 %fusion.145 = bf16[2048,64]{0,1:T(8,128)(2,1)S(1)} fusion(s32[2048]{0:T(1024)S(1)} %add.514, bf16[5120,64]{1,0:T(8,128)(2,1)} %get-tuple-element.1249, s32[]{:T(128)S(6)} %select_n.27), kind=kOutput, calls=%fused_computation.68.clone.1 | convolution fusion | flops 1116078080 | bytes 1351684 | tf_op jit(solution)/shard_map/while/body/eval_jaxpr/dot_general | solution.py:143
  310.8 2.9 multiply_reduce_fusion.6
  315.2 1.6 fusion.149
  320.2 8.6 %fusion.145 = bf16[2048,64]{0,1:T(8,128)(2,1)S(1)} fusion(s32[2048]{0:T(1024)S(1)} %add.514, bf16[5120,64]{1,0:T(8,128)(2,1)} %get-tuple-element.1249, s32[]{:T(128)S(6)} %select_n.27), kind=kOutput, calls=%fused_computation.68.clone.1 | convolution fusion | flops 1116078080 | bytes 1351684 | tf_op jit(solution)/shard_map/while/body/eval_jaxpr/dot_general | solution.py:143
  333.9 2.9 multiply_reduce_fusion.6
  338.3 1.6 fusion.149
  343.3 8.6 %fusion.145 = bf16[2048,64]{0,1:T(8,128)(2,1)S(1)} fusion(s32[2048]{0:T(1024)S(1)} %add.514, bf16[5120,64]{1,0:T(8,128)(2,1)} %get-tuple-element.1249, s32[]{:T(128)S(6)} %select_n.27), kind=kOutput, calls=%fused_computation.68.clone.1 | convolution fusion | flops 1116078080 | bytes 1351684 | tf_op jit(solution)/shard_map/while/body/eval_jaxpr/dot_general | solution.py:143
  352.6 1.0 constant_dynamic-slice_fusion.18
  357.0 2.9 multiply_reduce_fusion.6
  361.4 1.6 fusion.149
  366.4 8.6 %fusion.145 = bf16[2048,64]{0,1:T(8,128)(2,1)S(1)} fusion(s32[2048]{0:T(1024)S(1)} %add.514, bf16[5120,64]{1,0:T(8,128)(2,1)} %get-tuple-element.1249, s32[]{:T(128)S(6)} %select_n.27), kind=kOutput, calls=%fused_computation.68.clone.1 | convolution fusion | flops 1116078080 | bytes 1351684 | tf_op jit(solution)/shard_map/while/body/eval_jaxpr/dot_general | solution.py:143
  375.7 1.0 constant_dynamic-slice_fusion.18
  380.1 2.9 multiply_reduce_fusion.6
  384.5 1.6 fusion.149
  389.5 8.6 %fusion.145 = bf16[2048,64]{0,1:T(8,128)(2,1)S(1)} fusion(s32[2048]{0:T(1024)S(1)} %add.514, bf16[5120,64]{1,0:T(8,128)(2,1)} %get-tuple-element.1249, s32[]{:T(128)S(6)} %select_n.27), kind=kOutput, calls=%fused_computation.68.clone.1 | convolution fusion | flops 1116078080 | bytes 1351684 | tf_op jit(solution)/shard_map/while/body/eval_jaxpr/dot_general | solution.py:143
  403.2 2.9 multiply_reduce_fusion.6
  407.6 1.6 fusion.149
  409.1 1.7 multiply_reduce_fusion.2
  410.8 1.7 copy_bitcast_fusion
  412.5 38.6 %psum.7 = f32[]{:T(128)} all-reduce(f32[]{:T(128)} %multiply_reduce_fusion.2), channel_id=1, replica_groups=mesh['space'=8,'rep'=4] {'space','rep'}, use_global_device_ids=true, to_apply=%region_9.10 | all-reduce | flops 1 | bytes 8 | tf_op jit(solution)/shard_map/psum | solution.py:171
  (448 shorter events, 136.4 us)
Async XLA Ops:
  0.6 1.2 copy-start
  0.6 10.5 %copy-start.1 = (f32[1024,256]{1,0:T(8,128)S(1)}, f32[1024,256]{1,0:T(8,128)}, u32[]{:S(2)}) copy-start(f32[1024,256]{1,0:T(8,128)} %param.19) | copy-start | bytes 3145732
  2.1 10.3 %copy-start.4 = (s32[1024,16]{0,1:T(8,128)S(1)}, s32[1024,16]{0,1:T(8,128)}, u32[]{:S(2)}) copy-start(s32[1024,16]{0,1:T(8,128)} %param.17) | copy-start | bytes 196612
  2.1 18.2 %collective-permute-start = (bf16[1024,64]{1,0:T(8,128)(2,1)S(1)}, bf16[1024,64]{1,0:T(8,128)(2,1)}, u32[]{:S(2)}, u32[]{:S(2)}) collective-permute-start(bf16[1024,64]{1,0:T(8,128)(2,1)S(1)} %convert_element_type.245), channel_id=1, source_target_pairs={{0,2},{1,3},{2,4},{3,5},{4,6},{5,7},{6,8},{7,9},{8,10},{9,11},{10,... | collective-permute-start | bytes 393224 | tf_op jit(solution)/shard_map/ppermute | solution.py:30
  5.2 16.1 %collective-permute-start.1 = (bf16[1024,64]{1,0:T(8,128)(2,1)S(1)}, bf16[1024,64]{1,0:T(8,128)(2,1)}, u32[]{:S(2)}, u32[]{:S(2)}) collective-permute-start(bf16[1024,64]{1,0:T(8,128)(2,1)S(1)} %convert_element_type.245), channel_id=1, source_target_pairs={{0,1},{1,2},{2,3},{3,4},{4,5},{5,6},{6,7},{7,8},{8,9},{9,10},{10,1... | collective-permute-start | bytes 393224 | tf_op jit(solution)/shard_map/ppermute | solution.py:18
  5.2 17.2 %collective-permute-start.2 = (bf16[1024,64]{1,0:T(8,128)(2,1)S(1)}, bf16[1024,64]{1,0:T(8,128)(2,1)}, u32[]{:S(2)}, u32[]{:S(2)}) collective-permute-start(bf16[1024,64]{1,0:T(8,128)(2,1)S(1)} %convert_element_type.245), channel_id=1, source_target_pairs={{1,0},{2,1},{3,2},{4,3},{5,4},{6,5},{7,6},{8,7},{9,8},{10,9},{11,1... | collective-permute-start | bytes 393224 | tf_op jit(solution)/shard_map/ppermute | solution.py:20
  10.5 15.8 %collective-permute-start.3 = (bf16[1024,64]{1,0:T(8,128)(2,1)S(1)}, bf16[1024,64]{1,0:T(8,128)(2,1)}, u32[]{:S(2)}, u32[]{:S(2)}) collective-permute-start(bf16[1024,64]{1,0:T(8,128)(2,1)S(1)} %convert_element_type.245), channel_id=1, source_target_pairs={{0,30},{1,31},{2,0},{3,1},{4,2},{5,3},{6,4},{7,5},{8,6},{9,7},{10,... | collective-permute-start | bytes 393224 | tf_op jit(solution)/shard_map/ppermute | solution.py:30
  11.1 3.4 copy-start.6
  14.6 13.8 %copy-start.2 = (bf16[2,64,64]{2,1,0:T(8,128)(2,1)S(1)}, bf16[2,64,64]{2,1,0:T(8,128)(2,1)}, u32[]{:S(2)}) copy-start(bf16[2,64,64]{2,1,0:T(8,128)(2,1)} %param.21) | copy-start | bytes 49156
  14.7 13.8 %copy-start.3 = (bf16[2,64,128]{2,1,0:T(8,128)(2,1)S(1)}, bf16[2,64,128]{2,1,0:T(8,128)(2,1)}, u32[]{:S(2)}) copy-start(bf16[2,64,128]{2,1,0:T(8,128)(2,1)} %param.22) | copy-start | bytes 98308
  14.7 13.8 %copy-start.8 = (f32[2,64]{1,0:T(2,128)S(1)}, f32[2,64]{1,0:T(2,128)}, u32[]{:S(2)}) copy-start(f32[2,64]{1,0:T(2,128)} %param.23) | copy-start | bytes 1540
  27.3 1.1 copy-start.5
  202.2 15.3 %collective-permute-start.4 = (bf16[1024,64]{1,0:T(8,128)(2,1)S(1)}, bf16[1024,64]{1,0:T(8,128)(2,1)S(1)}, u32[]{:S(2)}, u32[]{:S(2)}) collective-permute-start(bf16[1024,64]{1,0:T(8,128)(2,1)S(1)} %bitcast.156), channel_id=1, source_target_pairs={{0,2},{1,3},{2,4},{3,5},{4,6},{5,7},{6,8},{7,9},{8,10},{9,11},{10,... | collective-permute-start | bytes 393224 | tf_op jit(solution)/shard_map/ppermute | solution.py:30
  202.6 15.7 %collective-permute-start.5 = (bf16[1024,64]{1,0:T(8,128)(2,1)S(1)}, bf16[1024,64]{1,0:T(8,128)(2,1)S(1)}, u32[]{:S(2)}, u32[]{:S(2)}) collective-permute-start(bf16[1024,64]{1,0:T(8,128)(2,1)S(1)} %bitcast.157), channel_id=1, source_target_pairs={{0,1},{1,2},{2,3},{3,4},{4,5},{5,6},{6,7},{7,8},{8,9},{9,10},{10,1... | collective-permute-start | bytes 393224 | tf_op jit(solution)/shard_map/ppermute | solution.py:18
  202.6 17.1 %collective-permute-start.6 = (bf16[1024,64]{1,0:T(8,128)(2,1)S(1)}, bf16[1024,64]{1,0:T(8,128)(2,1)S(1)}, u32[]{:S(2)}, u32[]{:S(2)}) collective-permute-start(bf16[1024,64]{1,0:T(8,128)(2,1)S(1)} %bitcast.158), channel_id=1, source_target_pairs={{1,0},{2,1},{3,2},{4,3},{5,4},{6,5},{7,6},{8,7},{9,8},{10,9},{11,1... | collective-permute-start | bytes 393224 | tf_op jit(solution)/shard_map/ppermute | solution.py:20
  207.9 15.1 %collective-permute-start.7 = (bf16[1024,64]{1,0:T(8,128)(2,1)S(1)}, bf16[1024,64]{1,0:T(8,128)(2,1)S(1)}, u32[]{:S(2)}, u32[]{:S(2)}) collective-permute-start(bf16[1024,64]{1,0:T(8,128)(2,1)S(1)} %bitcast.159), channel_id=1, source_target_pairs={{0,30},{1,31},{2,0},{3,1},{4,2},{5,3},{6,4},{7,5},{8,6},{9,7},{10,... | collective-permute-start | bytes 393224 | tf_op jit(solution)/shard_map/ppermute | solution.py:30
  224.4 184.7 %copy-start.7 = (f32[64]{0:T(128)S(1)}, f32[64]{0:T(128)}, u32[]{:S(2)}) copy-start(f32[64]{0:T(128)} %param.25) | copy-start | bytes 772
where the time goes:
time: 457 us; the launch traced here: 453 us
  matrix products  172 us (38%)
  local copies, waits for them, and re-layouts  108 us (24%)
  other arithmetic  67.7 us (15%)
  blocking collectives  38.6 us (8%)
  loops' own time  29 us (6%)
  waiting for transfers between devices  19.1 us (4%)
  starting transfers between devices  16.2 us (4%)
    dot_general x16, matrix products, block_step(): picked = jnp.dot(one_hot, window_rows, preferred_element_type=jnp.float32)  137 us
    dynamic_slice x72, local copies, waits for them, and re-layouts, per_device(): lax.map(block_step, (starts, own_rows.reshape(number, block_rows, -1), bo...  54.6 us
    reduce_sum x16, other arithmetic, interact(): jnp.sum(jax.nn.silu(angle_input) * pair_mask[..., None], axis=2)  47.2 us
    psum x1, blocking collectives, per_device(): energy_sum = lax.psum(jnp.sum(own_rows * weight_energy), ('space', 'rep'))  38.6 us
    another operation x2, loops' own time, per_device(): lax.map(block_step, (starts, own_rows.reshape(number, block_rows, -1), bo...  29 us
    dot_general x16, matrix products, interact(): jnp.dot(summed, weight_atom, preferred_element_type=jnp.float32)  19.1 us
    ppermute x4, waiting for transfers between devices, passed_along(): return lax.ppermute(value, axis, pairs)  19 us
    dynamic_update_slice x24, local copies, waits for them, and re-layouts, per_device(): lax.map(block_step, (starts, own_rows.reshape(number, block_rows, -1), bo...  12.7 us
  transfers between devices with their start and end apart: 8, of which 4 were waited for; matrix products, arithmetic and copies ran while one was open for 2% of the time, Pallas kernels for 0%

commit v1 on v0

v1 whole, which is shorter than its diff:
```python
import functools
import math

import jax
import jax.numpy as jnp
from jax import lax
from jax.experimental import pallas as pl
from jax.experimental.pallas import tpu as pltpu
from jax.sharding import PartitionSpec as P

LAYERS = 2
LANES = 256
DEAD = -1e30
VMEM = pl.BlockSpec(memory_space=pltpu.VMEM)


def tree_push(stack, term):
    level = 0
    while stack and stack[-1][0] == level:
        term = term + stack.pop()[1]
        level += 1
    stack.append((level, term))


def tree_total(stack):
    total = stack.pop()[1]
    while stack:
        total = total + stack.pop()[1]
    return total


def layer_kernel(
    first,
    last,
    slots,
    channels,
    pieces,
    *refs,
):
    piece_refs = refs[:pieces]
    (state_ref, bond_ref, off_ref, cnt_ref, cos_ref, core_ref, atom_ref, pair_ref, wcos_ref, wbond_ref) = refs[
        pieces : pieces + 10
    ]
    rest = refs[pieces + 10 :]
    if last:
        energy_ref, atoms_out, bonds_out, energy_out = rest[:4]
        rest = rest[4:]
    else:
        atoms_out, table_out, bonds_out, cos_out = rest[:4]
        rest = rest[4:]
    tab, core_t, pair_t, atom_t, bond_t, wc, p_s, q_s, n_s, msg_s, new_s, cos_s, bond_s = rest
    blocks = off_ref.shape[0]
    per_piece = blocks
    reach = tab.shape[0] - blocks + 1
    bf = jnp.bfloat16
    f32 = jnp.float32
    for index in range(pieces):
        tab[index * per_piece : (index + 1) * per_piece] = piece_refs[index][...]
    core_t[...] = (core_ref[...].astype(f32).T * 0.5).astype(bf)
    pair_t[...] = (pair_ref[...].astype(f32).T * 0.5).astype(bf)
    atom_t[...] = atom_ref[...].astype(f32).T.astype(bf)
    bond_t[...] = (wbond_ref[...].astype(f32).T * 0.5).astype(bf)
    wc[...] = jnp.broadcast_to((wcos_ref[...] * 0.5).T, wc.shape).astype(bf)
    columns = lax.broadcasted_iota(jnp.int32, (LANES, LANES), 0)
    lane = lax.broadcasted_iota(jnp.int32, (1, LANES), 1)
    centre = pieces // 2 * per_piece

    def block(b, carry):
        rows = pl.ds(pl.multiple_of(b * LANES, LANES), LANES)
        count = cnt_ref[b]
        own = tab[centre + b]

        if first:
            cos_s[...] = cos_ref[rows, :].T
            cos_out[b] = cos_s[...].astype(cos_out.dtype)
            for pair in range(slots // 2):
                both = bond_ref[rows, pair * 2 * channels : (pair + 1) * 2 * channels].astype(f32).T.astype(bf)
                bond_s[2 * pair] = both[:channels]
                bond_s[2 * pair + 1] = both[channels:]
        else:
            cos_s[...] = cos_ref[b]

        def bond_at(k):
            return bond_s[k] if first else bond_ref[b, k]

        def project(k, carry):
            both = jnp.dot(pair_t[...], bond_at(k), preferred_element_type=f32)
            p_s[k] = both[:channels].astype(bf)
            q_s[k] = jnp.where(k < count, both[channels:], DEAD).astype(bf)
            return carry

        lax.fori_loop(0, slots, project, 0, unroll=4)

        def gather(k):
            index = off_ref[b, pl.ds(k, 1), :] + (lane + (reach - 1) // 2 * LANES)
            low = index % LANES
            high = index // LANES
            chosen = jnp.where(columns == low, 1.0, 0.0).astype(bf)
            lhs = tab[pl.ds(b, reach)].reshape(reach * channels, LANES)
            picked = jnp.dot(lhs, chosen, preferred_element_type=f32)
            result = picked[:channels]
            for h in range(1, reach):
                result = jnp.where(high == h, picked[h * channels : (h + 1) * channels], result)
            return result.astype(bf)

        n_s[0] = gather(0)
        msg_s[...] = jnp.zeros_like(msg_s)

        def slot(j, carry):
            live = jnp.where(j < count, 1.0, 0.0)
            here = bond_at(j)
            joined = jnp.concatenate([own, n_s[j % 2], here], axis=0)
            mixed = jnp.dot(core_t[...], joined, preferred_element_type=f32)
            n_s[(j + 1) % 2] = gather(jnp.minimum(j + 1, slots - 1))
            gates = jnp.tanh(mixed)
            cores = mixed[channels : 2 * channels]
            msg_s[...] += (1.0 + gates[:channels]) * (cores + cores * gates[channels : 2 * channels]) * live
            p = p_s[j]
            stack = []
            for m in range(1, slots):
                k = (j + m) % slots
                cosine = jnp.broadcast_to(cos_s[pl.ds(j * slots + k, 1), :], (8, LANES)).astype(bf)
                cosine = jnp.concatenate([cosine] * (channels // 8), axis=0)
                y = p + (q_s[k] + cosine * wc[...])
                tree_push(stack, y + y * jnp.tanh(y))
            angular = (tree_total(stack).astype(f32) * (1.0 / count.astype(f32))).astype(bf)
            update = jnp.dot(bond_t[...], angular, preferred_element_type=f32)
            update = update * (1.0 + gates[2 * channels :]) * live
            fresh = (here.astype(f32) + update).astype(bf)
            if last:
                new_s[j] = fresh
            else:
                bonds_out[b, j] = fresh
            return carry

        lax.fori_loop(0, slots, slot, 0)
        summed = (msg_s[...] * (0.5 / count.astype(f32))).astype(bf)
        state = (state_ref[b]) + jnp.dot(atom_t[...], summed, preferred_element_type=f32)
        if last:
            atoms_out[rows, :] = state.T
            energy_out[b] = jnp.sum(state * energy_ref[...].T, axis=0, keepdims=True)
            for pair in range(slots // 2):
                both = jnp.concatenate([new_s[2 * pair], new_s[2 * pair + 1]], axis=0)
                bonds_out[rows, pair * 2 * channels : (pair + 1) * 2 * channels] = both.astype(f32).T.astype(bf)
        else:
            atoms_out[b] = state
            table_out[b] = state.astype(bf)
        return carry

    lax.fori_loop(0, blocks, block, 0)


def run_layer(first, last, tables, state, bonds, offs, counts, cosines, weights, energy):
    blocks, slots = offs.shape[:2]
    channels = state.shape[1]
    quarter = blocks * LANES
    bf = jnp.bfloat16
    f32 = jnp.float32
    sds = jax.ShapeDtypeStruct
    if last:
        outs = [
            sds((quarter, channels), f32),
            sds((quarter, slots * channels), bf),
            sds((blocks, 1, LANES), f32),
        ]
    else:
        outs = [
            sds((blocks, channels, LANES), f32),
            sds((blocks, channels, LANES), bf),
            sds((blocks, slots, channels, LANES), bf),
            sds((blocks, slots * slots, LANES), f32),
        ]
    operands = [*tables, state, bonds, offs, counts, cosines, *weights]
    if last:
        operands.append(energy)
    return pl.pallas_call(
        functools.partial(layer_kernel, first, last, slots, channels, len(tables)),
        out_shape=outs,
        in_specs=[VMEM] * len(operands),
        out_specs=[VMEM] * len(outs),
        scratch_shapes=[
            pltpu.VMEM((blocks * len(tables), channels, LANES), bf),
            pltpu.VMEM((3 * channels, 3 * channels), bf),
            pltpu.VMEM((2 * channels, channels), bf),
            pltpu.VMEM((channels, channels), bf),
            pltpu.VMEM((channels, channels), bf),
            pltpu.VMEM((channels, LANES), bf),
            pltpu.VMEM((slots, channels, LANES), bf),
            pltpu.VMEM((slots, channels, LANES), bf),
            pltpu.VMEM((2, channels, LANES), bf),
            pltpu.VMEM((channels, LANES), f32),
            pltpu.VMEM((slots, channels, LANES), bf),
            pltpu.VMEM((slots * slots, LANES), f32),
            pltpu.VMEM((slots, channels, LANES), bf),
        ],
        compiler_params=pltpu.CompilerParams(vmem_limit_bytes=56 * 2**20),
    )(*operands)


def passed_along(value, axis, steps):
    count = lax.axis_size(axis)
    return lax.ppermute(value, axis, [(source, (source + steps) % count) for source in range(count)])


def around(table):
    return [table if steps == 0 else passed_along(table, ("space", "rep"), steps) for steps in (2, 1, 0, -1, -2)]


def per_device(
    atom_features,
    bond_features,
    offsets,
    counts,
    cosines,
    weight_core,
    weight_atom,
    weight_pair,
    weight_cosine,
    weight_bond,
    weight_energy,
):
    quarter, slots = offsets.shape
    domain, channels = atom_features.shape
    blocks = quarter // LANES
    own = lax.dynamic_slice_in_dim(atom_features, lax.axis_index("rep") * quarter, quarter, 0)
    state = own.reshape(blocks, LANES, channels).transpose(0, 2, 1)
    table = state.astype(jnp.bfloat16)
    offs = offsets.reshape(blocks, LANES, slots).transpose(0, 2, 1)
    cnts = counts.reshape(blocks, 1, LANES)
    bonds = bond_features
    energy = None
    for layer in range(LAYERS):
        weights = (
            weight_core[layer],
            weight_atom[layer],
            weight_pair[layer],
            weight_cosine[layer : layer + 1],
            weight_bond[layer],
        )
        last = layer == LAYERS - 1
        outs = run_layer(
            layer == 0, last, around(table), state, bonds, offs, cnts, cosines, weights, weight_energy[None, :]
        )
        if last:
            state, bonds, energy = outs
        else:
            state, table, bonds, cosines = outs
    total = lax.psum(jnp.sum(energy), ("space", "rep"))
    return (state, bonds, total / math.sqrt(lax.axis_size("space") * domain))


def solution(mesh):
    return jax.shard_map(
        per_device,
        mesh=mesh,
        in_specs=(
            P("space", None),
            P(("space", "rep"), None),
            P(("space", "rep"), None),
            P(("space", "rep")),
            P(("space", "rep"), None),
            P(),
            P(),
            P(),
            P(),
            P(),
            P(),
        ),
        out_specs=(P(("space", "rep"), None), P(("space", "rep"), None), P()),
        check_vma=False,
    )
```

time: 457 us -> 147 us (0.32)
  matrix products: 172 us -> 0 us
  local copies, waits for them, and re-layouts: 108 us -> 11.6 us
  Pallas kernels: 0 us -> 69.4 us
  other arithmetic: 67.7 us -> 1.3 us
  loops' own time: 29 us -> 0 us
  waiting for transfers between devices: 19.1 us -> 11 us
    dot_general x80 -> x0, matrix products: 172 us -> none  [the longest x16 137 us: block_step(): picked = jnp.dot(one_hot, window_rows, preferred_element_type=jnp.float32)]
    pallas_call x0 -> x2, Pallas kernels: none -> 69.4 us  [run_layer(): pl.pallas_call(functools.partial(layer_kernel, first, last, slots, channe...]
    dynamic_slice x73 -> x1, local copies, waits for them, and re-layouts: 54.6 us -> 0.02 us  [per_device(): lax.dynamic_slice_in_dim(atom_features, lax.axis_index('rep') * quarter,...]
    reduce_sum x33 -> x1, other arithmetic: 53.5 us -> 1.3 us  [per_device(): total = lax.psum(jnp.sum(energy), ('space', 'rep'))]
    another operation x2 -> x0, loops' own time: 29 us -> none  [per_device(): lax.map(block_step, (starts, own_rows.reshape(number, block_rows, -1), bo...]
    dynamic_update_slice x24 -> x0, local copies, waits for them, and re-layouts: 12.7 us -> none  [per_device(): lax.map(block_step, (starts, own_rows.reshape(number, block_rows, -1), bo...]
    div x16 -> x0, other arithmetic: 11.2 us -> none  [interact(): inverse_count = 1.0 / cnt_rows.astype(jnp.float32)]
    convert_element_type x33 -> x0, local copies, waits for them, and re-layouts: 10.8 us -> none  [the longest x16 6.24 us: interact(): h_rows.astype(jnp.bfloat16)[:, None, :]]
  transfers between devices with their start and end apart: 8 -> 8, of which waited for: 4 -> 5; matrix products, arithmetic and copies ran while one was open for 2% -> 5% of each run, Pallas kernels for 0% -> 0%
where the time goes in v1:
time: 147 us; the launch traced here: 146 us
  Pallas kernels  69.4 us (47%)
  blocking collectives  37.1 us (25%)
  starting transfers between devices  13 us (9%)
  local copies, waits for them, and re-layouts  11.6 us (8%)
  waiting for transfers between devices  11 us (7%)
  between operations  2.51 us (2%)
    pallas_call x2, Pallas kernels, run_layer(): pl.pallas_call(functools.partial(layer_kernel, first, last, slots, channe...  69.4 us
    psum x1, blocking collectives, per_device(): total = lax.psum(jnp.sum(energy), ('space', 'rep'))  37.1 us
    ppermute x8, starting transfers between devices, passed_along(): lax.ppermute(value, axis, [(source, (source + steps) % count) for source...  13 us
    ppermute x8, waiting for transfers between devices, passed_along(): lax.ppermute(value, axis, [(source, (source + steps) % count) for source...  11 us
    unnamed x23, local copies, waits for them, and re-layouts  4.45 us
  transfers between devices with their start and end apart: 8, of which 5 were waited for; matrix products, arithmetic and copies ran while one was open for 5% of the time, Pallas kernels for 0%

profile of v1, /device:TPU:0, one launch (start us, length us, event | category | flops | bytes accessed | tf_op | source)
XLA Modules:
  0.0 146.0 jit_solution(3705758750391398549)
XLA Ops:
  0.6 0.0 copy-start
  0.6 0.0 copy-start.10
  0.7 1.2 copy-done
  1.9 0.0 copy-start.1
  1.9 7.0 %collective-permute-start.3 = (bf16[4,64,256]{2,1,0:T(8,128)(2,1)S(1)}, bf16[4,64,256]{2,1,0:T(8,128)(2,1)S(1)}, u32[]{:S(2)}, u32[]{:S(2)}) collective-permute-start(bf16[4,64,256]{2,1,0:T(8,128)(2,1)S(1)} %bitcast.43), channel_id=1, source_target_pairs={{0,30},{1,31},{2,0},{3,1},{4,2},{5,3},{6,4},{7,5},{8,6},{9,7},{10,... | collective-permute-start | bytes 393224 | tf_op jit(solution)/shard_map/ppermute | solution.py:202
  8.9 0.0 collective-permute-start.2
  8.9 0.5 collective-permute-start.1
  9.4 0.7 collective-permute-start
  10.1 0.7 copy.24
  10.8 1.3 slice_bitcast_fusion.3
  12.2 1.5 copy.25
  13.7 1.6 %slice_bitcast_fusion = (bf16[192,192]{1,0:T(8,128)(2,1)}, bf16[192,192]{1,0:T(8,128)(2,1)}) fusion(bf16[2,192,192]{2,1,0:T(8,128)(2,1)} %param.16), kind=kLoop, calls=%fused_computation.1 | loop fusion | bytes 294912 | tf_op jit(solution)/shard_map/squeeze | solution.py:234
  15.3 1.4 slice_bitcast_fusion.2
  16.7 0.0 copy-done.10
  16.7 0.6 fusion.1
  17.3 0.0 collective-permute-done.3.refs_4_
  17.3 0.0 copy-start.6
  17.3 0.0 collective-permute-done.2.refs_3_
  17.3 0.0 copy-start.7
  17.3 0.0 collective-permute-done.1.refs_1_
  17.3 0.0 copy-start.8
  17.3 2.1 %collective-permute-done.refs_0_ = bf16[4,64,256]{2,1,0:T(8,128)(2,1)S(1)} collective-permute-done((bf16[4,64,256]{2,1,0:T(8,128)(2,1)S(1)}, bf16[4,64,256]{2,1,0:T(8,128)(2,1)S(1)}, u32[]{:S(2)}, u32[]{:S(2)}) %collective-permute-start) | collective-permute-done | bytes 131104 | tf_op jit(solution)/shard_map/ppermute | solution.py:202
  19.4 0.0 copy-start.9
  19.4 0.0 copy-done.1
  19.4 0.0 copy-done.6
  19.4 0.0 copy-done.7
  19.4 0.0 copy-done.8
  19.4 0.6 copy-done.9
  20.0 35.0 %shard_map.130 = (f32[4,64,256]{2,1,0:T(8,128)}, bf16[4,64,256]{2,1,0:T(8,128)(2,1)}, bf16[4,16,64,256]{3,2,1,0:T(8,128)(2,1)}, f32[4,256,256]{2,1,0:T(8,128)}) custom-call(bf16[4,64,256]{2,1,0:T(8,128)(2,1)} %copy-done.9, bf16[4,64,256]{2,1,0:T(8,128)(2,1)} %copy-done.8, bf16[4,64,256]{2,1,0:T(8,128)(2,1)} %bitcast.47, bf16[4,64,256]{2,1,0:T(8,128)(2,1)} %copy-done.7, ...), custom_call_target="tpu_custom_call" | custom-call | tf_op jit(solution)/shard_map/pallas_call | solution.py:176
  55.1 2.9 %collective-permute-start.7 = (bf16[4,64,256]{2,1,0:T(8,128)(2,1)}, bf16[4,64,256]{2,1,0:T(8,128)(2,1)S(1)}, u32[]{:S(2)}, u32[]{:S(2)}) collective-permute-start(bf16[4,64,256]{2,1,0:T(8,128)(2,1)} %get-tuple-element.10.refs_2_), channel_id=1, source_target_pairs={{0,30},{1,31},{2,0},{3,1},{4,2},{5,3},{6,4},{7,5},{8,6},{9,7},{10,... | collective-permute-start | bytes 393224 | tf_op jit(solution)/shard_map/ppermute | solution.py:202
  58.0 0.7 collective-permute-start.6
  58.6 0.0 collective-permute-start.5
  58.6 1.2 collective-permute-start.4
  59.9 1.9 %collective-permute-done.7.refs_4_ = bf16[4,64,256]{2,1,0:T(8,128)(2,1)S(1)} collective-permute-done((bf16[4,64,256]{2,1,0:T(8,128)(2,1)}, bf16[4,64,256]{2,1,0:T(8,128)(2,1)S(1)}, u32[]{:S(2)}, u32[]{:S(2)}) %collective-permute-start.7) | collective-permute-done | bytes 131104 | tf_op jit(solution)/shard_map/ppermute | solution.py:202
  61.7 0.0 copy-start.2
  61.7 1.4 collective-permute-done.6.refs_3_
  63.1 0.0 copy-start.3
  63.1 4.6 %collective-permute-done.5.refs_1_ = bf16[4,64,256]{2,1,0:T(8,128)(2,1)S(1)} collective-permute-done((bf16[4,64,256]{2,1,0:T(8,128)(2,1)}, bf16[4,64,256]{2,1,0:T(8,128)(2,1)S(1)}, u32[]{:S(2)}, u32[]{:S(2)}) %collective-permute-start.5) | collective-permute-done | bytes 131104 | tf_op jit(solution)/shard_map/ppermute | solution.py:202
  67.7 0.0 copy-start.4
  67.7 1.1 collective-permute-done.4.refs_0_
  68.8 0.0 copy-start.5
  68.8 0.0 copy-done.2
  68.8 0.0 copy-done.3
  68.8 0.0 copy-done.4
  68.8 0.6 copy-done.5
  69.4 34.4 %shard_map.131 = (f32[1024,64]{1,0:T(8,128)}, bf16[1024,1024]{1,0:T(8,128)(2,1)}, f32[4,1,256]{2,1,0:T(1,128)}) custom-call(bf16[4,64,256]{2,1,0:T(8,128)(2,1)} %copy-done.5, bf16[4,64,256]{2,1,0:T(8,128)(2,1)} %copy-done.4, bf16[4,64,256]{2,1,0:T(8,128)(2,1)} %get-tuple-element.10.refs_2_, bf16[4,64,256]{2,1,0:T(8,128)(2,1)} %copy-done.3, ...), custom_call_target="tpu_custom_call" | custom-call | tf_op jit(solution)/shard_map/pallas_call | solution.py:176
  103.9 1.3 reduce_sum.9
  105.2 37.1 %psum.7 = f32[]{:T(128)} all-reduce(f32[]{:T(128)} %reduce_sum.9), channel_id=1, replica_groups=mesh['space'=8,'rep'=4] {'space','rep'}, use_global_device_ids=true, to_apply=%region_1.0 | all-reduce | flops 1 | bytes 8 | tf_op jit(solution)/shard_map/psum | solution.py:248
  142.2 1.9 %copy.17 = f32[1024,64]{0,1:T(8,128)} copy(f32[1024,64]{1,0:T(8,128)} %get-tuple-element.20) | data formatting | bytes 524288
  (2 shorter events, 0.0 us)
Async XLA Ops:
  0.6 1.2 copy-start
  0.6 16.0 %copy-start.10 = (f32[2,64]{1,0:T(2,128)S(1)}, f32[2,64]{1,0:T(2,128)}, u32[]{:S(2)}) copy-start(f32[2,64]{1,0:T(2,128)} %param.19) | copy-start | bytes 1540
  1.9 17.5 %copy-start.1 = (bf16[8,4,8,256]{3,2,0,1:T(8,128)(2,1)}, bf16[8,4,8,256]{3,2,0,1:T(8,128)(2,1)S(1)}, u32[]{:S(2)}) copy-start(bf16[8,4,8,256]{3,2,0,1:T(8,128)(2,1)S(1)} %copy.26) | copy-start | bytes 393220
  1.9 15.4 %collective-permute-start.3 = (bf16[4,64,256]{2,1,0:T(8,128)(2,1)S(1)}, bf16[4,64,256]{2,1,0:T(8,128)(2,1)S(1)}, u32[]{:S(2)}, u32[]{:S(2)}) collective-permute-start(bf16[4,64,256]{2,1,0:T(8,128)(2,1)S(1)} %bitcast.43), channel_id=1, source_target_pairs={{0,30},{1,31},{2,0},{3,1},{4,2},{5,3},{6,4},{7,5},{8,6},{9,7},{10,... | collective-permute-start | bytes 393224 | tf_op jit(solution)/shard_map/ppermute | solution.py:202
  8.9 8.4 %collective-permute-start.2 = (bf16[4,64,256]{2,1,0:T(8,128)(2,1)S(1)}, bf16[4,64,256]{2,1,0:T(8,128)(2,1)S(1)}, u32[]{:S(2)}, u32[]{:S(2)}) collective-permute-start(bf16[4,64,256]{2,1,0:T(8,128)(2,1)S(1)} %bitcast.44), channel_id=1, source_target_pairs={{0,31},{1,0},{2,1},{3,2},{4,3},{5,4},{6,5},{7,6},{8,7},{9,8},{10,9... | collective-permute-start | bytes 393224 | tf_op jit(solution)/shard_map/ppermute | solution.py:202
  8.9 8.4 %collective-permute-start.1 = (bf16[4,64,256]{2,1,0:T(8,128)(2,1)S(1)}, bf16[4,64,256]{2,1,0:T(8,128)(2,1)S(1)}, u32[]{:S(2)}, u32[]{:S(2)}) collective-permute-start(bf16[4,64,256]{2,1,0:T(8,128)(2,1)S(1)} %bitcast.45), channel_id=1, source_target_pairs={{0,1},{1,2},{2,3},{3,4},{4,5},{5,6},{6,7},{7,8},{8,9},{9,10},{10,1... | collective-permute-start | bytes 393224 | tf_op jit(solution)/shard_map/ppermute | solution.py:202
  9.4 10.0 %collective-permute-start = (bf16[4,64,256]{2,1,0:T(8,128)(2,1)S(1)}, bf16[4,64,256]{2,1,0:T(8,128)(2,1)S(1)}, u32[]{:S(2)}, u32[]{:S(2)}) collective-permute-start(bf16[4,64,256]{2,1,0:T(8,128)(2,1)S(1)} %bitcast.46), channel_id=1, source_target_pairs={{0,2},{1,3},{2,4},{3,5},{4,6},{5,7},{6,8},{7,9},{8,10},{9,11},{10,... | collective-permute-start | bytes 393224 | tf_op jit(solution)/shard_map/ppermute | solution.py:202
  17.3 2.1 %copy-start.6 = (bf16[4,64,256]{2,1,0:T(8,128)(2,1)}, bf16[4,64,256]{2,1,0:T(8,128)(2,1)S(1)}, u32[]{:S(2)}) copy-start(bf16[4,64,256]{2,1,0:T(8,128)(2,1)S(1)} %collective-permute-done.3.refs_4_) | copy-start | bytes 393220
  17.3 2.1 %copy-start.7 = (bf16[4,64,256]{2,1,0:T(8,128)(2,1)}, bf16[4,64,256]{2,1,0:T(8,128)(2,1)S(1)}, u32[]{:S(2)}) copy-start(bf16[4,64,256]{2,1,0:T(8,128)(2,1)S(1)} %collective-permute-done.2.refs_3_) | copy-start | bytes 393220
  17.3 2.1 %copy-start.8 = (bf16[4,64,256]{2,1,0:T(8,128)(2,1)}, bf16[4,64,256]{2,1,0:T(8,128)(2,1)S(1)}, u32[]{:S(2)}) copy-start(bf16[4,64,256]{2,1,0:T(8,128)(2,1)S(1)} %collective-permute-done.1.refs_1_) | copy-start | bytes 393220
  19.4 0.7 copy-start.9
  55.1 6.7 %collective-permute-start.7 = (bf16[4,64,256]{2,1,0:T(8,128)(2,1)}, bf16[4,64,256]{2,1,0:T(8,128)(2,1)S(1)}, u32[]{:S(2)}, u32[]{:S(2)}) collective-permute-start(bf16[4,64,256]{2,1,0:T(8,128)(2,1)} %get-tuple-element.10.refs_2_), channel_id=1, source_target_pairs={{0,30},{1,31},{2,0},{3,1},{4,2},{5,3},{6,4},{7,5},{8,6},{9,7},{10,... | collective-permute-start | bytes 393224 | tf_op jit(solution)/shard_map/ppermute | solution.py:202
  58.0 5.2 %collective-permute-start.6 = (bf16[4,64,256]{2,1,0:T(8,128)(2,1)}, bf16[4,64,256]{2,1,0:T(8,128)(2,1)S(1)}, u32[]{:S(2)}, u32[]{:S(2)}) collective-permute-start(bf16[4,64,256]{2,1,0:T(8,128)(2,1)} %get-tuple-element.10.refs_2_), channel_id=1, source_target_pairs={{0,31},{1,0},{2,1},{3,2},{4,3},{5,4},{6,5},{7,6},{8,7},{9,8},{10,9... | collective-permute-start | bytes 393224 | tf_op jit(solution)/shard_map/ppermute | solution.py:202
  58.6 9.1 %collective-permute-start.5 = (bf16[4,64,256]{2,1,0:T(8,128)(2,1)}, bf16[4,64,256]{2,1,0:T(8,128)(2,1)S(1)}, u32[]{:S(2)}, u32[]{:S(2)}) collective-permute-start(bf16[4,64,256]{2,1,0:T(8,128)(2,1)} %get-tuple-element.10.refs_2_), channel_id=1, source_target_pairs={{0,1},{1,2},{2,3},{3,4},{4,5},{5,6},{6,7},{7,8},{8,9},{9,10},{10,1... | collective-permute-start | bytes 393224 | tf_op jit(solution)/shard_map/ppermute | solution.py:202
  58.6 10.1 %collective-permute-start.4 = (bf16[4,64,256]{2,1,0:T(8,128)(2,1)}, bf16[4,64,256]{2,1,0:T(8,128)(2,1)S(1)}, u32[]{:S(2)}, u32[]{:S(2)}) collective-permute-start(bf16[4,64,256]{2,1,0:T(8,128)(2,1)} %get-tuple-element.10.refs_2_), channel_id=1, source_target_pairs={{0,2},{1,3},{2,4},{3,5},{4,6},{5,7},{6,8},{7,9},{8,10},{9,11},{10,... | collective-permute-start | bytes 393224 | tf_op jit(solution)/shard_map/ppermute | solution.py:202
  61.7 7.1 %copy-start.2 = (bf16[4,64,256]{2,1,0:T(8,128)(2,1)}, bf16[4,64,256]{2,1,0:T(8,128)(2,1)S(1)}, u32[]{:S(2)}) copy-start(bf16[4,64,256]{2,1,0:T(8,128)(2,1)S(1)} %collective-permute-done.7.refs_4_) | copy-start | bytes 393220
  63.1 5.7 %copy-start.3 = (bf16[4,64,256]{2,1,0:T(8,128)(2,1)}, bf16[4,64,256]{2,1,0:T(8,128)(2,1)S(1)}, u32[]{:S(2)}) copy-start(bf16[4,64,256]{2,1,0:T(8,128)(2,1)S(1)} %collective-permute-done.6.refs_3_) | copy-start | bytes 393220
  67.7 1.1 copy-start.4
  68.8 0.7 copy-start.5

commit v2 on v1

v2 whole, which is shorter than its diff:
```python
import functools
import math

import jax
import jax.numpy as jnp
from jax import lax
from jax.experimental import pallas as pl
from jax.experimental.pallas import tpu as pltpu
from jax.sharding import PartitionSpec as P

LAYERS = 2
LANES = 256
DEAD = -1e30
BATCH = 4
BF = jnp.bfloat16
F32 = jnp.float32
AXES = ("space", "rep")
PARAMS = pltpu.CompilerParams(vmem_limit_bytes=56 * 2**20, dimension_semantics=("arbitrary",))


def tree_push(stack, term):
    level = 0
    while stack and stack[-1][0] == level:
        term = term + stack.pop()[1]
        level += 1
    stack.append((level, term))


def tree_total(stack):
    total = stack.pop()[1]
    while stack:
        total = total + stack.pop()[1]
    return total


def gather_kernel(layer, first, last, slots, channels, quarter, *refs):
    refs = list(refs)
    b = pl.program_id(0)
    per = quarter // LANES
    rim = 2 * per
    reach = 2 * rim + 1
    if first:
        domain_ref, far_ref = refs[:2]
        refs = refs[2:]
    else:
        piece_refs = refs[:5]
        state_ref = refs[5]
        refs = refs[6:]
    bond_ref, off_ref, cnt_ref, core_ref, atom_ref = refs[:5]
    refs = refs[5:]
    if last:
        energy_w_ref = refs.pop(0)
    state_out, gate_out = refs[:2]
    refs = refs[2:]
    if not last:
        table_out = refs.pop(0)
    if first:
        bonds_out = refs.pop(0)
    if last:
        energy_out = refs.pop(0)
    tab, core_t, atom_t, n_s, msg_s = refs

    @pl.when(b == 0)
    def _():
        core_t[...] = (core_ref[layer].astype(F32).T * 0.5).astype(BF)
        atom_t[...] = atom_ref[layer].astype(F32).T.astype(BF)
        if first:
            inner = domain_ref.shape[1] // LANES
            for i in range(inner):
                tab[rim + i] = domain_ref[:, i * LANES : (i + 1) * LANES].astype(BF)
            for i in range(rim):
                part = far_ref[:, i * LANES : (i + 1) * LANES]
                tab[i] = part
                tab[rim + inner + i] = part
        else:
            for piece, ref in enumerate(piece_refs):
                for i in range(per):
                    tab[piece * per + i] = ref[:, i * LANES : (i + 1) * LANES]
        if last:
            energy_out[...] = jnp.zeros_like(energy_out)

    if first:
        base = lax.axis_index("rep") * per + b
        state = domain_ref[:, pl.ds(pl.multiple_of(base * LANES, LANES), LANES)]
        for pair in range(slots // 2):
            both = bond_ref[:, pair * 2 * channels : (pair + 1) * 2 * channels].astype(F32).T.astype(BF)
            bonds_out[2 * pair] = both[:channels]
            bonds_out[2 * pair + 1] = both[channels:]
        bonds = bonds_out
    else:
        base = b
        state = state_ref[...]
        bonds = bond_ref

    own = tab[base + rim]
    count = cnt_ref[...]
    columns = lax.broadcasted_iota(jnp.int32, (LANES, LANES), 0)
    lane = lax.broadcasted_iota(jnp.int32, (1, LANES), 1) + rim * LANES

    def gather(group):
        for u in range(BATCH):
            index = off_ref[pl.ds(group * BATCH + u, 1), :] + lane
            low = index % LANES
            high = index // LANES
            chosen = jnp.where(columns == low, 1.0, 0.0).astype(BF)
            lhs = tab[pl.ds(base, reach)].reshape(reach * channels, LANES)
            picked = jnp.dot(lhs, chosen, preferred_element_type=F32)
            result = picked[:channels]
            for h in range(1, reach):
                result = jnp.where(high == h, picked[h * channels : (h + 1) * channels], result)
            n_s[group * BATCH + u] = result.astype(BF)

    def gates(group):
        total = msg_s[...] if group else None
        for u in range(BATCH):
            j = group * BATCH + u
            live = jnp.where(j < count, 1.0, 0.0)
            joined = jnp.concatenate([own, n_s[j], bonds[j]], axis=0)
            mixed = jnp.dot(core_t[...], joined, preferred_element_type=F32)
            gate = jnp.tanh(mixed)
            cores = mixed[channels : 2 * channels]
            message = (1.0 + gate[:channels]) * (cores + cores * gate[channels : 2 * channels]) * live
            total = message if total is None else total + message
            gate_out[j] = ((1.0 + gate[2 * channels :]) * live).astype(BF)
        msg_s[...] = total

    groups = slots // BATCH
    gather(0)
    for group in range(1, groups):
        gather(group)
        gates(group - 1)
    gates(groups - 1)
    summed = (msg_s[...] * (0.5 / count.astype(F32))).astype(BF)
    state = state + jnp.dot(atom_t[...], summed, preferred_element_type=F32)
    state_out[...] = state
    if not last:
        table_out[...] = state.astype(BF)
    if last:
        energy_out[...] += jnp.sum(state * energy_w_ref[...].T, axis=0, keepdims=True)


def whole(array):
    return pl.BlockSpec(array.shape, lambda b: (0,) * len(array.shape))


def run_gather(layer, tables, state, bonds, offs, counts, weights, energy):
    first, last = layer == 0, layer == LAYERS - 1
    slots, quarter = offs.shape
    channels = weights[1].shape[1]
    per = quarter // LANES
    column = pl.BlockSpec((channels, LANES), lambda b: (0, b))
    slab = pl.BlockSpec((None, slots, channels, LANES), lambda b: (b, 0, 0, 0))
    sds = jax.ShapeDtypeStruct
    operands = list(tables)
    specs = [whole(x) for x in tables]
    if not first:
        operands.append(state)
        specs.append(column)
    operands += [bonds, offs, counts, *weights]
    specs += [
        pl.BlockSpec((LANES, slots * channels), lambda b: (b, 0)) if first else slab,
        pl.BlockSpec((slots, LANES), lambda b: (0, b)),
        pl.BlockSpec((1, LANES), lambda b: (0, b)),
        *[whole(x) for x in weights],
    ]
    outs = [sds((channels, quarter), F32), sds((per, slots, channels, LANES), BF)]
    out_specs = [column, slab]
    if last:
        operands.append(energy)
        specs.append(whole(energy))
    if not last:
        outs.append(sds((channels, quarter), BF))
        out_specs.append(column)
    if first:
        outs.append(sds((per, slots, channels, LANES), BF))
        out_specs.append(slab)
    if last:
        outs.append(sds((1, LANES), F32))
        out_specs.append(pl.BlockSpec((1, LANES), lambda b: (0, 0)))
    rows = (tables[0].shape[1] // LANES + 4 * per) if first else 5 * per
    return pl.pallas_call(
        functools.partial(gather_kernel, layer, first, last, slots, channels, quarter),
        grid=(per,),
        out_shape=outs,
        in_specs=specs,
        out_specs=out_specs,
        scratch_shapes=[
            pltpu.VMEM((rows, channels, LANES), BF),
            pltpu.VMEM((3 * channels, 3 * channels), BF),
            pltpu.VMEM((channels, channels), BF),
            pltpu.VMEM((slots, channels, LANES), BF),
            pltpu.VMEM((channels, LANES), F32),
        ],
        compiler_params=PARAMS,
        cost_estimate=pl.CostEstimate(flops=10 * 2**30, bytes_accessed=2**23, transcendentals=2**22),
    )(*operands)


def angle_kernel(layer, first, last, slots, channels, *refs):
    refs = list(refs)
    bond_ref, gate_ref, cnt_ref, cos_ref, pair_ref, wcos_ref, wbond_ref = refs[:7]
    refs = refs[7:]
    if last:
        refs.pop(0)
    bonds_out = refs.pop(0)
    if first:
        cos_out = refs.pop(0)
    pair_t, bond_t, wc, p_s, q_s, a_s, new_s = refs

    @pl.when(pl.program_id(0) == 0)
    def _():
        pair_t[...] = (pair_ref[layer].astype(F32).T * 0.5).astype(BF)
        bond_t[...] = (wbond_ref[layer].astype(F32).T * 0.5).astype(BF)
        wc[...] = jnp.broadcast_to((wcos_ref[layer : layer + 1] * 0.5).T, wc.shape).astype(BF)

    count = cnt_ref[...]
    inverse = 1.0 / count.astype(F32)
    if first:
        cos_out[...] = cos_ref[...].T
        cosines = cos_out
    else:
        cosines = cos_ref

    for k in range(slots):
        both = jnp.dot(pair_t[...], bond_ref[k], preferred_element_type=F32)
        p_s[k] = both[:channels].astype(BF)
        q_s[k] = jnp.where(k < count, both[channels:], DEAD).astype(BF)

    fresh = new_s if last else bonds_out

    def update(j):
        change = jnp.dot(bond_t[...], a_s[j], preferred_element_type=F32)
        fresh[j] = (bond_ref[j].astype(F32) + change * gate_ref[j].astype(F32)).astype(BF)

    def slot(j, carry):
        p = p_s[j]
        stack = []
        for m in range(1, slots):
            k = (j + m) % slots
            cosine = jnp.broadcast_to(cosines[pl.ds(j * slots + k, 1), :], (8, LANES)).astype(BF)
            cosine = jnp.concatenate([cosine] * (channels // 8), axis=0)
            y = p + (q_s[k] + cosine * wc[...])
            tree_push(stack, y + y * jnp.tanh(y))
        a_s[j] = (tree_total(stack).astype(F32) * inverse).astype(BF)
        return carry

    lax.fori_loop(0, slots, slot, 0)
    for j in range(slots):
        update(j)
    if last:
        for pair in range(slots // 2):
            both = jnp.concatenate([new_s[2 * pair], new_s[2 * pair + 1]], axis=0)
            bonds_out[:, pair * 2 * channels : (pair + 1) * 2 * channels] = both.astype(F32).T.astype(BF)


def run_angle(layer, part, buffer, bonds, gates, counts, cosines, weights):
    first, last = layer == 0, layer == LAYERS - 1
    per, slots, channels = bonds.shape[:3]
    at = (lambda b: b) if part is None else (lambda b: b + part)
    steps = per if part is None else 1
    slab = pl.BlockSpec((None, slots, channels, LANES), lambda b: (at(b), 0, 0, 0))
    tile = pl.BlockSpec((None, slots * slots, LANES), lambda b: (at(b), 0, 0))
    sds = jax.ShapeDtypeStruct
    operands = [bonds, gates, counts, cosines, *weights]
    specs = [
        slab,
        slab,
        pl.BlockSpec((1, LANES), lambda b: (0, at(b))),
        pl.BlockSpec((LANES, slots * slots), lambda b: (at(b), 0)) if first else tile,
        *[whole(x) for x in weights],
    ]
    aliases = {}
    if last:
        outs = [sds((per * LANES, slots * channels), BF)]
        out_specs = [pl.BlockSpec((LANES, slots * channels), lambda b: (at(b), 0))]
        if buffer is None:
            buffer = jnp.zeros((8, 128), F32)
        else:
            aliases = {len(operands): 0}
        operands.append(buffer)
        specs.append(pl.BlockSpec(memory_space=pl.ANY))
    else:
        outs = [sds((per, slots, channels, LANES), BF), sds((per, slots * slots, LANES), F32)]
        out_specs = [slab, tile]
    return pl.pallas_call(
        functools.partial(angle_kernel, layer, first, last, slots, channels),
        grid=(steps,),
        out_shape=outs,
        in_specs=specs,
        out_specs=out_specs,
        input_output_aliases=aliases,
        scratch_shapes=[
            pltpu.VMEM((2 * channels, channels), BF),
            pltpu.VMEM((channels, channels), BF),
            pltpu.VMEM((channels, LANES), BF),
            pltpu.VMEM((slots, channels, LANES), BF),
            pltpu.VMEM((slots, channels, LANES), BF),
            pltpu.VMEM((slots, channels, LANES), BF),
            pltpu.VMEM((slots, channels, LANES), BF),
        ],
        compiler_params=PARAMS,
        cost_estimate=pl.CostEstimate(flops=2**30 * steps, bytes_accessed=2**21 * steps, transcendentals=2**22 * steps),
    )(*operands)


def passed_along(value, steps):
    count = lax.axis_size(AXES)
    return lax.ppermute(value, AXES, [(source, (source + steps) % count) for source in range(count)])


def far_side(domain, quarter):
    rim = 2 * quarter
    rep = lax.axis_size("rep")
    total = lax.axis_size(AXES)
    payload = jnp.where(lax.axis_index("rep") < 2, domain[:, :rim], domain[:, -rim:]).astype(BF)
    pairs = []
    for start in range(0, total, rep):
        for d in range(2):
            pairs.append(((start + d - 2) % total, start + d))
            pairs.append(((start + rep + d) % total, start + rep - 2 + d))
    return lax.ppermute(payload, AXES, pairs)


def sum_stages():
    rep, space = lax.axis_size("rep"), lax.axis_size("space")

    def over_rep(value):
        moved = [
            lax.ppermute(value, "rep", [(i, (i + s) % rep) for i in range(rep)]) for s in range(1, rep)
        ]
        return sum(moved, value)

    def over_space(step):
        return lambda value: value + lax.ppermute(value, "space", [(i, i ^ step) for i in range(space)])

    return [over_rep] + [over_space(1 << s) for s in range(space.bit_length() - 1)]


def per_device(
    atom_features,
    bond_features,
    offsets,
    counts,
    cosines,
    weight_core,
    weight_atom,
    weight_pair,
    weight_cosine,
    weight_bond,
    weight_energy,
):
    quarter = offsets.shape[0]
    per = quarter // LANES
    domain = atom_features.T
    offs = offsets.T
    cnts = counts[None, :]
    into_atoms = (weight_core, weight_atom)
    into_bonds = (weight_pair, weight_cosine, weight_bond)
    far = far_side(domain, quarter)
    state, gates, table, bonds = run_gather(
        0, [domain, far], None, bond_features, offs, cnts, into_atoms, None
    )
    pieces = [table if s == 0 else passed_along(table, s) for s in (2, 1, 0, -1, -2)]
    bonds, tiles = run_angle(0, None, None, bonds, gates, cnts, cosines, into_bonds)
    state, gates, energy = run_gather(1, pieces, state, bonds, offs, cnts, into_atoms, weight_energy[None, :])
    stages = sum_stages()
    out = None
    for part in range(per):
        if stages:
            energy = stages.pop(0)(energy)
        (out,) = run_angle(1, part, out, bonds, gates, cnts, tiles, into_bonds)
    for stage in stages:
        energy = stage(energy)
    scale = math.sqrt(lax.axis_size("space") * domain.shape[1])
    return (state.T, out, jnp.sum(energy) / scale)


def solution(mesh):
    return jax.shard_map(
        per_device,
        mesh=mesh,
        in_specs=(
            P("space", None),
            P(("space", "rep"), None),
            P(("space", "rep"), None),
            P(("space", "rep")),
            P(("space", "rep"), None),
            P(),
            P(),
            P(),
            P(),
            P(),
            P(),
        ),
        out_specs=(P(("space", "rep"), None), P(("space", "rep"), None), P()),
        check_vma=False,
    )
```

time: 147 us -> 105 us (0.71)
  blocking collectives: 37.1 us -> 0 us
  local copies, waits for them, and re-layouts: 11.6 us -> 2.01 us
  starting transfers between devices: 13 us -> 21.4 us
  waiting for transfers between devices: 11 us -> 6.33 us
  Pallas kernels: 69.4 us -> 70.9 us
    psum x1 -> x0, blocking collectives: 37.1 us -> none  [per_device(): total = lax.psum(jnp.sum(energy), ('space', 'rep'))]
    ppermute x8 -> x11, starting transfers between devices: 13 us -> 21.4 us  [the longest x1 7 us: far_side(): return lax.ppermute(payload, AXES, pairs)]
    ppermute x8 -> x11, waiting for transfers between devices: 11 us -> 6.33 us  [the longest x1 6.31 us: far_side(): return lax.ppermute(payload, AXES, pairs)]
    squeeze x3 -> x0, local copies, waits for them, and re-layouts: 4.38 us -> none  [the longest x1 1.63 us: per_device(): weight_core[layer]]
    unnamed x23 -> x12, local copies, waits for them, and re-layouts: 4.45 us -> 1.42 us
    reshape x3 -> x0, local copies, waits for them, and re-layouts: 2.2 us -> none  [the longest x1 1.46 us: per_device(): offs = offsets.reshape(blocks, LANES, slots).transpose(0, 2, 1)]
    pallas_call x2 -> x7, Pallas kernels: 69.4 us -> 70.9 us  [the longest x5 39.3 us: run_angle(): pl.pallas_call(functools.partial(angle_kernel, layer, first, last, slots,...]
  transfers between devices with their start and end apart: 8 -> 11, of which waited for: 5 -> 1; matrix products, arithmetic and copies ran while one was open for 5% -> 1% of each run, Pallas kernels for 0% -> 37%
where the time goes in v2:
time: 105 us
  Pallas kernels  70.9 us (68%)
  starting transfers between devices  21.4 us (20%)
  waiting for transfers between devices  6.33 us (6%)
  between operations  2.54 us (2%)
  local copies, waits for them, and re-layouts  2.01 us (2%)
  other arithmetic  1.87 us (2%)
    pallas_call x5, Pallas kernels, run_angle(): pl.pallas_call(functools.partial(angle_kernel, layer, first, last, slots,...  39.3 us
    pallas_call x2, Pallas kernels, run_gather(): pl.pallas_call(functools.partial(gather_kernel, layer, first, last, slots...  31.6 us
    ppermute x1, starting transfers between devices, far_side(): return lax.ppermute(payload, AXES, pairs)  7 us
    ppermute x3, starting transfers between devices, over_space(): lax.ppermute(value, 'space', [(i, i ^ step) for i in range(space)])  6.81 us
    ppermute x1, waiting for transfers between devices, far_side(): return lax.ppermute(payload, AXES, pairs)  6.31 us
    ppermute x4, starting transfers between devices, passed_along(): lax.ppermute(value, AXES, [(source, (source + steps) % count) for source...  5.89 us
  transfers between devices with their start and end apart: 11, of which 1 were waited for; matrix products, arithmetic and copies ran while one was open for 1% of the time, Pallas kernels for 37%

profile of v2, /device:TPU:0, one launch (start us, length us, event | category | flops | bytes accessed | tf_op | source)
XLA Modules:
  0.0 105.0 jit_solution(11177627654549692937)
XLA Ops:
  0.6 1.3 %fusion = bf16[64,2048]{1,0:T(8,128)(2,1)S(1)} fusion(f32[64,4096]{1,0:T(8,128)} %bitcast.5, pred[]{:T(512)S(6)} %lt.3), kind=kLoop, calls=%fused_computation.1 | loop fusion | flops 131072 | bytes 786433 | tf_op jit(solution)/shard_map/convert_element_type | solution.py:315
  1.9 7.0 %collective-permute-start = (bf16[64,2048]{1,0:T(8,128)(2,1)S(1)}, bf16[64,2048]{1,0:T(8,128)(2,1)S(1)}, u32[]{:S(2)}, u32[]{:S(2)}) collective-permute-start(bf16[64,2048]{1,0:T(8,128)(2,1)S(1)} %fusion), channel_id=1, source_target_pairs={{30,0},{4,2},{31,1},{5,3},{2,4},{8,6},{3,5},{9,7},{6,8},{12,10},{7... | collective-permute-start | bytes 786440 | tf_op jit(solution)/shard_map/ppermute | solution.py:321
  8.9 6.3 %collective-permute-done.refs_1_ = bf16[64,2048]{1,0:T(8,128)(2,1)S(1)} collective-permute-done((bf16[64,2048]{1,0:T(8,128)(2,1)S(1)}, bf16[64,2048]{1,0:T(8,128)(2,1)S(1)}, u32[]{:S(2)}, u32[]{:S(2)}) %collective-permute-start) | collective-permute-done | bytes 262176 | tf_op jit(solution)/shard_map/ppermute | solution.py:321
  15.2 0.0 copy-start.1
  15.2 0.7 copy-done.1
  15.9 15.8 %shard_map.130 = (f32[64,1024]{1,0:T(8,128)}, bf16[4,16,64,256]{3,2,1,0:T(8,128)(2,1)}, bf16[64,1024]{1,0:T(8,128)(2,1)}, bf16[4,16,64,256]{3,2,1,0:T(8,128)(2,1)}) custom-call(f32[64,4096]{1,0:T(8,128)} %bitcast.6, bf16[64,2048]{1,0:T(8,128)(2,1)} %copy-done.1, bf16[1024,1024]{1,0:T(8,128)(2,1)} %refs_2_.1, s32[16,1024]{1,0:T(8,128)} %bitcast.14, ...), custom_call_target="tpu_custom_call" | custom-call | flops 10737418240 | bytes 8388608 | tf_op jit(solution)/shard_map/pallas_call | solution.py:181
  31.7 5.4 %collective-permute-start.4 = (bf16[64,1024]{1,0:T(8,128)(2,1)}, bf16[64,1024]{1,0:T(8,128)(2,1)S(1)}, u32[]{:S(2)}, u32[]{:S(2)}) collective-permute-start(bf16[64,1024]{1,0:T(8,128)(2,1)} %get-tuple-element.12.refs_2_), channel_id=1, source_target_pairs={{0,30},{1,31},{2,0},{3,1},{4,2},{5,3},{6,4},{7,5},{8,6},{9,7},{10,... | collective-permute-start | bytes 393224 | tf_op jit(solution)/shard_map/ppermute | solution.py:308
  37.1 0.0 collective-permute-start.3
  37.1 0.5 collective-permute-start.2
  37.6 0.0 collective-permute-start.1
  37.6 16.4 %shard_map.131 = (bf16[4,16,64,256]{3,2,1,0:T(8,128)(2,1)}, f32[4,256,256]{2,1,0:T(8,128)}) custom-call(bf16[4,16,64,256]{3,2,1,0:T(8,128)(2,1)} %get-tuple-element.14.refs_0_, bf16[4,16,64,256]{3,2,1,0:T(8,128)(2,1)} %get-tuple-element.15.refs_1_, s32[1,1024]{1,0:T(1,128)} %bitcast.8, f32[1024,256]{1,0:T(8,128)} %refs_3_.1, bf16[2,64,128]{2,1,0:T(8,128)(2,1)} %refs_4_.9, ...), custom_call_target="tpu_custom_call" | custom-call | flops 4294967296 | bytes 8388608 | tf_op jit(solution)/shard_map/pallas_call | solution.py:285
  54.0 0.0 collective-permute-done.4.refs_4_
  54.0 0.0 copy-start.2
  54.0 0.0 collective-permute-done.3.refs_3_
  54.0 0.0 copy-start.3
  54.0 0.0 collective-permute-done.2.refs_1_
  54.1 0.0 copy-start.4
  54.1 0.0 collective-permute-done.1.refs_0_
  54.1 0.0 copy-start.5
  54.1 0.6 copy-done.2
  54.7 0.1 copy-done.3
  54.7 0.0 copy-done.4
  54.7 0.0 copy-done.5
  54.8 15.8 %shard_map.132 = (f32[64,1024]{1,0:T(8,128)}, bf16[4,16,64,256]{3,2,1,0:T(8,128)(2,1)}, f32[1,256]{1,0:T(1,128)}) custom-call(bf16[64,1024]{1,0:T(8,128)(2,1)} %copy-done.5, bf16[64,1024]{1,0:T(8,128)(2,1)} %copy-done.4, bf16[64,1024]{1,0:T(8,128)(2,1)} %get-tuple-element.12.refs_2_, bf16[64,1024]{1,0:T(8,128)(2,1)} %copy-done.3, ...), custom_call_target="tpu_custom_call" | custom-call | flops 10737418240 | bytes 8388608 | tf_op jit(solution)/shard_map/pallas_call | solution.py:181
  70.6 0.1 collective-permute-start.7
  70.6 1.6 %collective-permute-start.6 = (f32[1,256]{1,0:T(1,128)}, f32[1,256]{1,0:T(1,128)S(1)}, u32[]{:S(2)}, u32[]{:S(2)}) collective-permute-start(f32[1,256]{1,0:T(1,128)} %get-tuple-element.20), channel_id=1, source_target_pairs={{0,2},{1,3},{2,0},{3,1},{4,6},{5,7},{6,4},{7,5},{8,10},{9,11},{10,... | collective-permute-start | bytes 3080 | tf_op jit(solution)/shard_map/ppermute | solution.py:329
  72.3 0.0 collective-permute-start.5
  72.3 0.6 broadcast_in_dim.11.refs_7_
  72.8 0.0 copy-start
  72.9 5.7 %shard_map.133.refs_7_ = bf16[1024,1024]{1,0:T(8,128)(2,1)} custom-call(bf16[4,16,64,256]{3,2,1,0:T(8,128)(2,1)} %get-tuple-element.16.refs_6_.refs_0_, bf16[4,16,64,256]{3,2,1,0:T(8,128)(2,1)} %get-tuple-element.18.refs_1_, s32[1,1024]{1,0:T(1,128)} %bitcast.10, f32[4,256,256]{2,1,0:T(8,128)} %get-tuple-element.19.refs_3_, bf16[2,64,128]{2,1,0:T(8,128)(2,1)} %refs_4_.9, ...), custom_call_target="tpu_custom_call" | custom-call | flops 1073741824 | bytes 2097152 | tf_op jit(solution)/shard_map/pallas_call | solution.py:285
  78.6 0.0 collective-permute-done.7
  78.6 0.0 collective-permute-done.6
  78.6 0.0 collective-permute-done.5
  78.6 0.0 copy-done
  78.6 0.1 collective-permute-start.8
  78.7 5.7 %shard_map.134.refs_7_ = bf16[1024,1024]{1,0:T(8,128)(2,1)} custom-call(bf16[4,16,64,256]{3,2,1,0:T(8,128)(2,1)} %get-tuple-element.16.refs_6_.refs_0_, bf16[4,16,64,256]{3,2,1,0:T(8,128)(2,1)} %get-tuple-element.18.refs_1_, s32[1,1024]{1,0:T(1,128)} %bitcast.11, f32[4,256,256]{2,1,0:T(8,128)} %get-tuple-element.19.refs_3_, ...), custom_call_target="tpu_custom_call", output_to_operand_aliasing={{}: (7, {})} | custom-call | flops 1073741824 | bytes 2097152 | tf_op jit(solution)/shard_map/pallas_call | solution.py:285
  84.4 0.0 collective-permute-done.8
  84.4 0.5 collective-permute-start.9
  84.9 5.7 %shard_map.135.refs_7_ = bf16[1024,1024]{1,0:T(8,128)(2,1)} custom-call(bf16[4,16,64,256]{3,2,1,0:T(8,128)(2,1)} %get-tuple-element.16.refs_6_.refs_0_, bf16[4,16,64,256]{3,2,1,0:T(8,128)(2,1)} %get-tuple-element.18.refs_1_, s32[1,1024]{1,0:T(1,128)} %bitcast.12, f32[4,256,256]{2,1,0:T(8,128)} %get-tuple-element.19.refs_3_, ...), custom_call_target="tpu_custom_call", output_to_operand_aliasing={{}: (7, {})} | custom-call | flops 1073741824 | bytes 2097152 | tf_op jit(solution)/shard_map/pallas_call | solution.py:285
  90.7 0.0 collective-permute-done.9
  90.7 6.2 %collective-permute-start.10 = (f32[1,256]{1,0:T(1,128)S(1)}, f32[1,256]{1,0:T(1,128)S(1)}, u32[]{:S(2)}, u32[]{:S(2)}) collective-permute-start(f32[1,256]{1,0:T(1,128)S(1)} %add.22), channel_id=1, source_target_pairs={{0,16},{4,20},{8,24},{12,28},{16,0},{20,4},{24,8},{28,12},{1,17},{... | collective-permute-start | bytes 3080 | tf_op jit(solution)/shard_map/ppermute | solution.py:334
  96.9 5.7 %shard_map.136 = bf16[1024,1024]{1,0:T(8,128)(2,1)} custom-call(bf16[4,16,64,256]{3,2,1,0:T(8,128)(2,1)} %get-tuple-element.16.refs_6_.refs_0_, bf16[4,16,64,256]{3,2,1,0:T(8,128)(2,1)} %get-tuple-element.18.refs_1_, s32[1,1024]{1,0:T(1,128)} %bitcast.13, f32[4,256,256]{2,1,0:T(8,128)} %get-tuple-element.19.refs_3_, ...), custom_call_target="tpu_custom_call", output_to_operand_aliasing={{}: (7, {})} | custom-call | flops 1073741824 | bytes 2097152 | tf_op jit(solution)/shard_map/pallas_call | solution.py:285
  102.6 0.0 collective-permute-done.10
  102.6 0.6 add_reduce_fusion
  (3 shorter events, 0.0 us)
Async XLA Ops:
  1.9 13.3 %collective-permute-start = (bf16[64,2048]{1,0:T(8,128)(2,1)S(1)}, bf16[64,2048]{1,0:T(8,128)(2,1)S(1)}, u32[]{:S(2)}, u32[]{:S(2)}) collective-permute-start(bf16[64,2048]{1,0:T(8,128)(2,1)S(1)} %fusion), channel_id=1, source_target_pairs={{30,0},{4,2},{31,1},{5,3},{2,4},{8,6},{3,5},{9,7},{6,8},{12,10},{7... | collective-permute-start | bytes 786440 | tf_op jit(solution)/shard_map/ppermute | solution.py:321
  15.2 0.7 copy-start.1
  31.7 22.3 %collective-permute-start.4 = (bf16[64,1024]{1,0:T(8,128)(2,1)}, bf16[64,1024]{1,0:T(8,128)(2,1)S(1)}, u32[]{:S(2)}, u32[]{:S(2)}) collective-permute-start(bf16[64,1024]{1,0:T(8,128)(2,1)} %get-tuple-element.12.refs_2_), channel_id=1, source_target_pairs={{0,30},{1,31},{2,0},{3,1},{4,2},{5,3},{6,4},{7,5},{8,6},{9,7},{10,... | collective-permute-start | bytes 393224 | tf_op jit(solution)/shard_map/ppermute | solution.py:308
  37.1 16.9 %collective-permute-start.3 = (bf16[64,1024]{1,0:T(8,128)(2,1)}, bf16[64,1024]{1,0:T(8,128)(2,1)S(1)}, u32[]{:S(2)}, u32[]{:S(2)}) collective-permute-start(bf16[64,1024]{1,0:T(8,128)(2,1)} %get-tuple-element.12.refs_2_), channel_id=1, source_target_pairs={{0,31},{1,0},{2,1},{3,2},{4,3},{5,4},{6,5},{7,6},{8,7},{9,8},{10,9... | collective-permute-start | bytes 393224 | tf_op jit(solution)/shard_map/ppermute | solution.py:308
  37.1 16.9 %collective-permute-start.2 = (bf16[64,1024]{1,0:T(8,128)(2,1)}, bf16[64,1024]{1,0:T(8,128)(2,1)S(1)}, u32[]{:S(2)}, u32[]{:S(2)}) collective-permute-start(bf16[64,1024]{1,0:T(8,128)(2,1)} %get-tuple-element.12.refs_2_), channel_id=1, source_target_pairs={{0,1},{1,2},{2,3},{3,4},{4,5},{5,6},{6,7},{7,8},{8,9},{9,10},{10,1... | collective-permute-start | bytes 393224 | tf_op jit(solution)/shard_map/ppermute | solution.py:308
  37.6 16.4 %collective-permute-start.1 = (bf16[64,1024]{1,0:T(8,128)(2,1)}, bf16[64,1024]{1,0:T(8,128)(2,1)S(1)}, u32[]{:S(2)}, u32[]{:S(2)}) collective-permute-start(bf16[64,1024]{1,0:T(8,128)(2,1)} %get-tuple-element.12.refs_2_), channel_id=1, source_target_pairs={{0,2},{1,3},{2,4},{3,5},{4,6},{5,7},{6,8},{7,9},{8,10},{9,11},{10,... | collective-permute-start | bytes 393224 | tf_op jit(solution)/shard_map/ppermute | solution.py:308
  54.0 0.6 copy-start.2
  54.0 0.7 copy-start.3
  54.1 0.7 copy-start.4
  54.1 0.7 copy-start.5
  70.6 8.0 %collective-permute-start.7 = (f32[1,256]{1,0:T(1,128)}, f32[1,256]{1,0:T(1,128)S(1)}, u32[]{:S(2)}, u32[]{:S(2)}) collective-permute-start(f32[1,256]{1,0:T(1,128)} %get-tuple-element.20), channel_id=1, source_target_pairs={{0,3},{1,0},{2,1},{3,2},{4,7},{5,4},{6,5},{7,6},{8,11},{9,8},{10,9... | collective-permute-start | bytes 3080 | tf_op jit(solution)/shard_map/ppermute | solution.py:329
  70.6 7.9 %collective-permute-start.6 = (f32[1,256]{1,0:T(1,128)}, f32[1,256]{1,0:T(1,128)S(1)}, u32[]{:S(2)}, u32[]{:S(2)}) collective-permute-start(f32[1,256]{1,0:T(1,128)} %get-tuple-element.20), channel_id=1, source_target_pairs={{0,2},{1,3},{2,0},{3,1},{4,6},{5,7},{6,4},{7,5},{8,10},{9,11},{10,... | collective-permute-start | bytes 3080 | tf_op jit(solution)/shard_map/ppermute | solution.py:329
  72.3 6.3 %collective-permute-start.5 = (f32[1,256]{1,0:T(1,128)}, f32[1,256]{1,0:T(1,128)S(1)}, u32[]{:S(2)}, u32[]{:S(2)}) collective-permute-start(f32[1,256]{1,0:T(1,128)} %get-tuple-element.20), channel_id=1, source_target_pairs={{0,1},{1,2},{2,3},{3,0},{4,5},{5,6},{6,7},{7,4},{8,9},{9,10},{10,1... | collective-permute-start | bytes 3080 | tf_op jit(solution)/shard_map/ppermute | solution.py:329
  72.8 5.7 %copy-start = (f32[1,256]{1,0:T(1,128)S(1)}, f32[1,256]{1,0:T(1,128)}, u32[]{:S(2)}) copy-start(f32[1,256]{1,0:T(1,128)} %get-tuple-element.20) | copy-start | bytes 3076
  78.6 5.8 %collective-permute-start.8 = (f32[1,256]{1,0:T(1,128)S(1)}, f32[1,256]{1,0:T(1,128)S(1)}, u32[]{:S(2)}, u32[]{:S(2)}) collective-permute-start(f32[1,256]{1,0:T(1,128)S(1)} %add_add_fusion), channel_id=1, source_target_pairs={{0,4},{4,0},{8,12},{12,8},{16,20},{20,16},{24,28},{28,24},{1,5},{5... | collective-permute-start | bytes 3080 | tf_op jit(solution)/shard_map/ppermute | solution.py:334
  84.4 6.2 %collective-permute-start.9 = (f32[1,256]{1,0:T(1,128)S(1)}, f32[1,256]{1,0:T(1,128)S(1)}, u32[]{:S(2)}, u32[]{:S(2)}) collective-permute-start(f32[1,256]{1,0:T(1,128)S(1)} %add.21), channel_id=1, source_target_pairs={{0,8},{4,12},{8,0},{12,4},{16,24},{20,28},{24,16},{28,20},{1,9},{5... | collective-permute-start | bytes 3080 | tf_op jit(solution)/shard_map/ppermute | solution.py:334
  90.7 12.0 %collective-permute-start.10 = (f32[1,256]{1,0:T(1,128)S(1)}, f32[1,256]{1,0:T(1,128)S(1)}, u32[]{:S(2)}, u32[]{:S(2)}) collective-permute-start(f32[1,256]{1,0:T(1,128)S(1)} %add.22), channel_id=1, source_target_pairs={{0,16},{4,20},{8,24},{12,28},{16,0},{20,4},{24,8},{28,12},{1,17},{... | collective-permute-start | bytes 3080 | tf_op jit(solution)/shard_map/ppermute | solution.py:334

commit v3 on v2

v3 whole, which is shorter than its diff:
```python
import functools
import math

import jax
import jax.numpy as jnp
from jax import lax
from jax.experimental import pallas as pl
from jax.experimental.pallas import tpu as pltpu
from jax.sharding import PartitionSpec as P

LAYERS = 2
LANES = 256
DEAD = -1e30
BATCH = 4
BF = jnp.bfloat16
F32 = jnp.float32
AXES = ("space", "rep")
PARAMS = pltpu.CompilerParams(vmem_limit_bytes=24 * 2**20)
VMEM = pl.BlockSpec(memory_space=pltpu.VMEM)
ANY = pl.BlockSpec(memory_space=pl.ANY)


def tree_push(stack, term):
    level = 0
    while stack and stack[-1][0] == level:
        term = term + stack.pop()[1]
        level += 1
    stack.append((level, term))


def tree_total(stack):
    total = stack.pop()[1]
    while stack:
        total = total + stack.pop()[1]
    return total


def bond_update(weight, angular, bond, gate):
    change = jnp.dot(weight, angular, preferred_element_type=F32)
    return (bond.astype(F32) + change * gate).astype(BF)


def block_lanes(b):
    return pl.ds(pl.multiple_of(b * LANES, LANES), LANES)


def gather_kernel(layer, first, last, slots, channels, quarter, *refs):
    refs = list(refs)
    per = quarter // LANES
    rim = 2 * per
    reach = 2 * rim + 1
    if first:
        state_ref, far_ref = refs[:2]
        refs = refs[2:]
    else:
        piece_refs = refs[:5]
        state_ref = refs[5]
        refs = refs[6:]
    bond_ref, off_ref, cnt_ref, core_ref, atom_ref = refs[:5]
    refs = refs[5:]
    if last:
        energy_w_ref = refs.pop(0)
        refs.pop(0)
    else:
        angular_ref, wbond_ref = refs[:2]
        refs = refs[2:]
    state_out = refs.pop(0)
    if last:
        gate_out, energy_out = refs[:2]
        energy_out[...] = jnp.zeros_like(energy_out)
        energy_w = energy_w_ref[...].T
    else:
        table_out, bonds_out = refs[:2]
    refs = refs[2:]
    tab, core_t, atom_t, bond_t, n_s, msg_s = refs
    core_t[...] = (core_ref[layer].astype(F32).T * 0.5).astype(BF)
    atom_t[...] = atom_ref[layer].astype(F32).T.astype(BF)
    if not last:
        bond_t[...] = (wbond_ref[layer].astype(F32).T * 0.5).astype(BF)
    skip = lax.axis_index("rep") * per if first else 0
    if first:
        inner = state_ref.shape[1] // LANES
        for i in range(inner):
            tab[rim + i] = state_ref[:, i * LANES : (i + 1) * LANES].astype(BF)
        for i in range(rim):
            part = far_ref[:, i * LANES : (i + 1) * LANES]
            tab[i] = part
            tab[rim + inner + i] = part
    else:
        for piece, ref in enumerate(piece_refs):
            for i in range(per):
                tab[piece * per + i] = ref[:, i * LANES : (i + 1) * LANES]
    columns = lax.broadcasted_iota(jnp.int32, (LANES, LANES), 0)
    lane = lax.broadcasted_iota(jnp.int32, (1, LANES), 1) + rim * LANES

    def block(b, carry):
        base = skip + b
        here = block_lanes(b)
        own = tab[base + rim]
        count = cnt_ref[:, here]

        def gather(group):
            for j in range(group * BATCH, (group + 1) * BATCH):
                index = off_ref[j : j + 1, here] + lane
                low = index % LANES
                high = index // LANES
                chosen = jnp.where(columns == low, 1.0, 0.0).astype(BF)
                lhs = tab[pl.ds(base, reach)].reshape(reach * channels, LANES)
                picked = jnp.dot(lhs, chosen, preferred_element_type=F32)
                result = picked[:channels]
                for h in range(1, reach):
                    result = jnp.where(high == h, picked[h * channels : (h + 1) * channels], result)
                n_s[j] = result.astype(BF)

        def gates(group):
            total = msg_s[...] if group else None
            for u in range(BATCH):
                j = group * BATCH + u
                live = jnp.where(j < count, 1.0, 0.0)
                bond = bond_ref[b, j]
                joined = jnp.concatenate([own, n_s[j], bond], axis=0)
                mixed = jnp.dot(core_t[...], joined, preferred_element_type=F32)
                gate = jnp.tanh(mixed)
                cores = mixed[channels : 2 * channels]
                message = (1.0 + gate[:channels]) * (cores + cores * gate[channels : 2 * channels]) * live
                total = message if total is None else total + message
                bond_gate = (1.0 + gate[2 * channels :]) * live
                if last:
                    gate_out[b, j] = bond_gate.astype(BF)
                else:
                    bonds_out[b, j] = bond_update(bond_t[...], angular_ref[b, j], bond, bond_gate)
            msg_s[...] = total

        groups = slots // BATCH
        gather(0)
        for group in range(1, groups):
            gather(group)
            gates(group - 1)
        gates(groups - 1)
        summed = (msg_s[...] * (0.5 / count.astype(F32))).astype(BF)
        state = state_ref[:, block_lanes(base) if first else here]
        state = state + jnp.dot(atom_t[...], summed, preferred_element_type=F32)
        state_out[:, here] = state
        if last:
            energy_out[...] += jnp.sum(state * energy_w, axis=0, keepdims=True)
        else:
            table_out[:, here] = state.astype(BF)
        return carry

    lax.fori_loop(0, per, block, 0)


def run_gather(layer, tables, state, bonds, offs, counts, weights, extra):
    first, last = layer == 0, layer == LAYERS - 1
    slots, quarter = offs.shape
    channels = weights[1].shape[1]
    per = quarter // LANES
    sds = jax.ShapeDtypeStruct
    operands = list(tables)
    if not first:
        operands.append(state)
    operands += [bonds, offs, counts, *weights, *extra]
    specs = [VMEM] * len(operands)
    slab = sds((per, slots, channels, LANES), BF)
    if last:
        specs[-1] = ANY
        outs = [sds((channels, quarter), F32), slab, sds((1, LANES), F32)]
    else:
        outs = [sds((channels, quarter), F32), sds((channels, quarter), BF), slab]
    rows = (tables[0].shape[1] // LANES + 4 * per) if first else 5 * per
    return pl.pallas_call(
        functools.partial(gather_kernel, layer, first, last, slots, channels, quarter),
        out_shape=outs,
        in_specs=specs,
        out_specs=[VMEM] * len(outs),
        scratch_shapes=[
            pltpu.VMEM((rows, channels, LANES), BF),
            pltpu.VMEM((3 * channels, 3 * channels), BF),
            pltpu.VMEM((channels, channels), BF),
            pltpu.VMEM((channels, channels), BF),
            pltpu.VMEM((slots, channels, LANES), BF),
            pltpu.VMEM((channels, LANES), F32),
        ],
        compiler_params=PARAMS,
        cost_estimate=pl.CostEstimate(flops=10 * 2**30, bytes_accessed=2**23, transcendentals=2**22),
    )(*operands)


def angle_kernel(layer, first, start, steps, slots, channels, *refs):
    bond_ref, cnt_ref, cos_ref, pair_ref, wcos_ref, angular_out = refs[:6]
    refs = refs[6:]
    if first:
        bonds, cosines, pair_t, wc, p_s, q_s = refs
    else:
        pair_t, wc, p_s, q_s = refs
        bonds, cosines = bond_ref, cos_ref
    pair_t[...] = (pair_ref[layer].astype(F32).T * 0.5).astype(BF)
    wc[...] = jnp.broadcast_to((wcos_ref[layer : layer + 1] * 0.5).T, wc.shape).astype(BF)

    def block(step, carry):
        b = start + step
        count = cnt_ref[:, block_lanes(b)]
        inverse = 1.0 / count.astype(F32)
        if first:
            rows = block_lanes(b)
            cosines[b] = cos_ref[rows, :].T
            for pair in range(slots // 2):
                both = bond_ref[rows, pair * 2 * channels : (pair + 1) * 2 * channels].astype(F32).T.astype(BF)
                bonds[b, 2 * pair] = both[:channels]
                bonds[b, 2 * pair + 1] = both[channels:]

        for k in range(slots):
            both = jnp.dot(pair_t[...], bonds[b, k], preferred_element_type=F32)
            p_s[k] = both[:channels].astype(BF)
            q_s[k] = jnp.where(k < count, both[channels:], DEAD).astype(BF)

        def slot(j, inner):
            p = p_s[j]
            stack = []
            for m in range(1, slots):
                k = (j + m) % slots
                cosine = jnp.broadcast_to(cosines[b, pl.ds(j * slots + k, 1), :], (8, LANES)).astype(BF)
                cosine = jnp.concatenate([cosine] * (channels // 8), axis=0)
                y = p + (q_s[k] + cosine * wc[...])
                tree_push(stack, y + y * jnp.tanh(y))
            angular_out[step, j] = (tree_total(stack).astype(F32) * inverse).astype(BF)
            return inner

        lax.fori_loop(0, slots, slot, 0)
        return carry

    lax.fori_loop(0, steps, block, 0)


def run_angle(layer, start, steps, bonds, counts, cosines, weights, shape):
    first = layer == 0
    per, slots, channels, _ = shape
    sds = jax.ShapeDtypeStruct
    outs = [sds((steps, slots, channels, LANES), BF)]
    scratch = [
        pltpu.VMEM((2 * channels, channels), BF),
        pltpu.VMEM((channels, LANES), BF),
        pltpu.VMEM((slots, channels, LANES), BF),
        pltpu.VMEM((slots, channels, LANES), BF),
    ]
    if first:
        outs += [sds(shape, BF), sds((per, slots * slots, LANES), F32)]
    return pl.pallas_call(
        functools.partial(angle_kernel, layer, first, start, steps, slots, channels),
        out_shape=outs,
        in_specs=[VMEM] * 5,
        out_specs=[VMEM] * len(outs),
        scratch_shapes=scratch,
        compiler_params=PARAMS,
        cost_estimate=pl.CostEstimate(flops=2**30 * steps, bytes_accessed=2**21 * steps, transcendentals=2**22 * steps),
    )(bonds, counts, cosines, *weights)


def update_kernel(layer, slots, channels, parts, *refs):
    angular_refs = refs[:parts]
    bond_ref, gate_ref, wbond_ref, bonds_out, bond_t, done, sems = refs[parts:]
    bond_t[...] = (wbond_ref[layer].astype(F32).T * 0.5).astype(BF)
    copies = []
    b = 0
    for angular_ref in angular_refs:
        for step in range(angular_ref.shape[0]):
            for pair in range(slots // 2):
                both = [
                    bond_update(bond_t[...], angular_ref[step, j], bond_ref[b, j], gate_ref[b, j].astype(F32))
                    for j in (2 * pair, 2 * pair + 1)
                ]
                both = jnp.concatenate(both, axis=0).astype(F32).T.astype(BF)
                done[b, :, pair * 2 * channels : (pair + 1) * 2 * channels] = both
            copies.append(
                pltpu.make_async_copy(done.at[b], bonds_out.at[pl.ds(b * LANES, LANES)], sems.at[b])
            )
            copies[-1].start()
            b += 1
    for copy in copies:
        copy.wait()


def run_update(layer, angulars, bonds, gates, weight):
    per, slots, channels, _ = bonds.shape
    return pl.pallas_call(
        functools.partial(update_kernel, layer, slots, channels, len(angulars)),
        out_shape=jax.ShapeDtypeStruct((per * LANES, slots * channels), BF),
        in_specs=[VMEM] * (len(angulars) + 3),
        out_specs=ANY,
        scratch_shapes=[
            pltpu.VMEM((channels, channels), BF),
            pltpu.VMEM((per, LANES, slots * channels), BF),
            pltpu.SemaphoreType.DMA((per,)),
        ],
        compiler_params=PARAMS,
        cost_estimate=pl.CostEstimate(flops=2**30, bytes_accessed=2**23, transcendentals=0),
    )(*angulars, bonds, gates, weight)


def passed_along(value, steps):
    count = lax.axis_size(AXES)
    return lax.ppermute(value, AXES, [(source, (source + steps) % count) for source in range(count)])


def far_side(domain, quarter):
    rim = 2 * quarter
    rep = lax.axis_size("rep")
    total = lax.axis_size(AXES)
    payload = jnp.where(lax.axis_index("rep") < 2, domain[:, :rim], domain[:, -rim:]).astype(BF)
    pairs = []
    for start in range(0, total, rep):
        for d in range(2):
            pairs.append(((start + d - 2) % total, start + d))
            pairs.append(((start + rep + d) % total, start + rep - 2 + d))
    return lax.ppermute(payload, AXES, pairs)


def sum_stages():
    rep, space = lax.axis_size("rep"), lax.axis_size("space")

    def over_rep(value):
        moved = [
            lax.ppermute(value, "rep", [(i, (i + s) % rep) for i in range(rep)]) for s in range(1, rep)
        ]
        return sum(moved, value)

    def over_space(step):
        return lambda value: value + lax.ppermute(value, "space", [(i, i ^ step) for i in range(space)])

    return [over_rep] + [over_space(1 << s) for s in range(space.bit_length() - 1)]


def per_device(
    atom_features,
    bond_features,
    offsets,
    counts,
    cosines,
    weight_core,
    weight_atom,
    weight_pair,
    weight_cosine,
    weight_bond,
    weight_energy,
):
    quarter = offsets.shape[0]
    per = quarter // LANES
    domain = atom_features.T
    offs = offsets.T
    cnts = counts[None, :]
    into_atoms = (weight_core, weight_atom)
    into_angles = (weight_pair, weight_cosine)
    shape = (per, offsets.shape[1], domain.shape[0], LANES)
    far = far_side(domain, quarter)
    angular, bonds, tiles = run_angle(0, 0, per, bond_features, cnts, cosines, into_angles, shape)
    state, table, bonds = run_gather(
        0, [domain, far], None, bonds, offs, cnts, into_atoms, [angular, weight_bond]
    )
    pieces = [table if s == 0 else passed_along(table, s) for s in (2, 1, 0, -1, -2)]
    half = per // 2
    angulars = list(run_angle(1, 0, half, bonds, cnts, tiles, into_angles, shape))
    state, gates, energy = run_gather(
        1, pieces, state, bonds, offs, cnts, into_atoms, [weight_energy[None, :], angulars[0]]
    )
    stages = sum_stages()
    for part in range(half, per):
        if stages:
            energy = stages.pop(0)(energy)
        angulars += run_angle(1, part, 1, bonds, cnts, tiles, into_angles, shape)
    if stages:
        energy = stages.pop(0)(energy)
    out = run_update(1, angulars, bonds, gates, weight_bond)
    for stage in stages:
        energy = stage(energy)
    scale = math.sqrt(lax.axis_size("space") * domain.shape[1])
    return (state.T, out, jnp.sum(energy) / scale)


def solution(mesh):
    return jax.shard_map(
        per_device,
        mesh=mesh,
        in_specs=(
            P("space", None),
            P(("space", "rep"), None),
            P(("space", "rep"), None),
            P(("space", "rep")),
            P(("space", "rep"), None),
            P(),
            P(),
            P(),
            P(),
            P(),
            P(),
        ),
        out_specs=(P(("space", "rep"), None), P(("space", "rep"), None), P()),
        check_vma=False,
    )
```

time: 105 us -> 88.2 us (0.84)
  Pallas kernels: 70.9 us -> 56.8 us
  waiting for transfers between devices: 6.33 us -> 2.4 us
  local copies, waits for them, and re-layouts: 2.01 us -> 4.98 us
  starting transfers between devices: 21.4 us -> 19.2 us
    pallas_call x5, Pallas kernels: 39.3 us -> 28.8 us  [the longest x4 26.5 us: run_angle(): pl.pallas_call(functools.partial(angle_kernel, layer, first, start, steps...]
    ppermute x1, waiting for transfers between devices: 6.31 us -> 0.01 us  [far_side(): return lax.ppermute(payload, AXES, pairs)]
    ppermute x3, starting transfers between devices: 6.81 us -> 3.04 us  [over_space(): lax.ppermute(value, 'space', [(i, i ^ step) for i in range(space)])]
    pallas_call x2, Pallas kernels: 31.6 us -> 28 us  [run_gather(): pl.pallas_call(functools.partial(gather_kernel, layer, first, last, slots...]
    unnamed x12 -> x28, local copies, waits for them, and re-layouts: 1.42 us -> 4.98 us
    ppermute x3, waiting for transfers between devices: 0.01 us -> 1.82 us  [over_rep(): lax.ppermute(value, 'rep', [(i, (i + s) % rep) for i in range(rep)])]
    ppermute x4, starting transfers between devices: 5.89 us -> 7.41 us  [passed_along(): lax.ppermute(value, AXES, [(source, (source + steps) % count) for source...]
  transfers between devices with their start and end apart: 11 -> 11, of which waited for: 1 -> 4; matrix products, arithmetic and copies ran while one was open for 1% -> 0% of each run, Pallas kernels for 37% -> 33%
where the time goes in v3:
time: 88.2 us; the launch traced here: 87.9 us
  Pallas kernels  56.8 us (64%)
  starting transfers between devices  19.2 us (22%)
  local copies, waits for them, and re-layouts  4.98 us (6%)
  between operations  2.63 us (3%)
  waiting for transfers between devices  2.4 us (3%)
  other arithmetic  1.86 us (2%)
    pallas_call x2, Pallas kernels, run_gather(): pl.pallas_call(functools.partial(gather_kernel, layer, first, last, slots...  28 us
    pallas_call x4, Pallas kernels, run_angle(): pl.pallas_call(functools.partial(angle_kernel, layer, first, start, steps...  26.5 us
    ppermute x4, starting transfers between devices, passed_along(): lax.ppermute(value, AXES, [(source, (source + steps) % count) for source...  7.41 us
    ppermute x1, starting transfers between devices, far_side(): return lax.ppermute(payload, AXES, pairs)  7 us
    unnamed x28, local copies, waits for them, and re-layouts  4.98 us
    ppermute x3, starting transfers between devices, over_space(): lax.ppermute(value, 'space', [(i, i ^ step) for i in range(space)])  3.04 us
    pallas_call x1, Pallas kernels, run_update(): pl.pallas_call(functools.partial(update_kernel, layer, slots, channels, l...  2.31 us
    ppermute x3, waiting for transfers between devices, over_rep(): lax.ppermute(value, 'rep', [(i, (i + s) % rep) for i in range(rep)])  1.82 us
  transfers between devices with their start and end apart: 11, of which 4 were waited for; matrix products, arithmetic and copies ran while one was open for 0% of the time, Pallas kernels for 33%

profile of v3, /device:TPU:0, one launch (start us, length us, event | category | flops | bytes accessed | tf_op | source)
XLA Modules:
  0.0 87.9 jit_solution(11714040289418154643)
XLA Ops:
  0.6 1.3 %fusion = bf16[64,2048]{1,0:T(8,128)(2,1)S(1)} fusion(f32[64,4096]{1,0:T(8,128)} %bitcast.5, pred[]{:T(512)S(6)} %lt.3), kind=kLoop, calls=%fused_computation.1 | loop fusion | flops 131072 | bytes 786433 | tf_op jit(solution)/shard_map/convert_element_type | solution.py:309
  1.9 7.0 %collective-permute-start = (bf16[64,2048]{1,0:T(8,128)(2,1)S(1)}, bf16[64,2048]{1,0:T(8,128)(2,1)S(1)}, u32[]{:S(2)}, u32[]{:S(2)}) collective-permute-start(bf16[64,2048]{1,0:T(8,128)(2,1)S(1)} %fusion), channel_id=1, source_target_pairs={{30,0},{4,2},{31,1},{5,3},{2,4},{8,6},{3,5},{9,7},{6,8},{12,10},{7... | collective-permute-start | bytes 786440 | tf_op jit(solution)/shard_map/ppermute | solution.py:315
  8.9 0.0 copy-start.2
  8.9 1.6 %copy-done.2 = bf16[1024,1024]{1,0:T(8,128)(2,1)S(1)} copy-done((bf16[1024,1024]{1,0:T(8,128)(2,1)S(1)}, bf16[1024,1024]{1,0:T(8,128)(2,1)}, u32[]{:S(2)}) %copy-start.2) | copy-done | bytes 2097176
  10.5 0.0 copy-start.3
  10.5 1.2 %copy-done.3 = f32[1024,256]{1,0:T(8,128)S(1)} copy-done((f32[1024,256]{1,0:T(8,128)S(1)}, f32[1024,256]{1,0:T(8,128)}, u32[]{:S(2)}) %copy-start.3) | copy-done | bytes 1048600
  11.7 0.0 copy-start.7
  11.7 0.8 copy-done.7
  12.5 0.0 copy-start.9
  12.5 0.7 copy-done.9
  13.1 0.0 copy-start.11
  13.1 0.7 copy-done.11
  13.8 0.0 copy-start
  13.8 0.0 copy-start.1
  13.8 0.0 copy-start.4
  13.8 0.0 copy-start.5
  13.8 0.0 copy-start.6
  13.8 0.0 copy-start.10
  13.9 13.4 %shard_map.130 = (bf16[4,16,64,256]{3,2,1,0:T(8,128)(2,1)S(1)}, bf16[4,16,64,256]{3,2,1,0:T(8,128)(2,1)S(1)}, f32[4,256,256]{2,1,0:T(8,128)S(1)}) custom-call(bf16[1024,1024]{1,0:T(8,128)(2,1)S(1)} %copy-done.2, s32[1,1024]{1,0:T(1,128)S(1)} %bitcast.9, f32[1024,256]{1,0:T(8,128)S(1)} %copy-done.3, bf16[2,64,128]{2,1,0:T(8,128)(2,1)S(1)} %copy-done.7, ...), custom_call_target="tpu_custom_call" | custom-call | flops 4294967296 | bytes 8388608 | tf_op jit(solution)/shard_map/pallas_call | solution.py:248
  27.3 0.0 collective-permute-done.refs_1_
  27.3 0.0 copy-done
  27.3 0.0 copy-done.1
  27.3 0.0 copy-done.4
  27.3 0.0 copy-done.5
  27.3 0.0 copy-done.6
  27.3 0.0 copy-done.10
  27.3 0.0 copy-start.8
  27.4 0.0 copy-start.12
  27.4 13.9 %shard_map.131 = (f32[64,1024]{1,0:T(8,128)S(1)}, bf16[64,1024]{1,0:T(8,128)(2,1)S(1)}, bf16[4,16,64,256]{3,2,1,0:T(8,128)(2,1)S(1)}) custom-call(f32[64,4096]{1,0:T(8,128)S(1)} %bitcast.6, bf16[64,2048]{1,0:T(8,128)(2,1)S(1)} %collective-permute-done.refs_1_, bf16[4,16,64,256]{3,2,1,0:T(8,128)(2,1)S(1)} %get-tuple-element.12.refs_2_, ...), custom_call_target="tpu_custom_call" | custom-call | flops 10737418240 | bytes 8388608 | tf_op jit(solution)/shard_map/pallas_call | solution.py:171
  41.3 0.1 collective-permute-start.1
  41.4 0.1 collective-permute-start.2
  41.5 5.3 %collective-permute-start.3 = (bf16[64,1024]{1,0:T(8,128)(2,1)S(1)}, bf16[64,1024]{1,0:T(8,128)(2,1)S(1)}, u32[]{:S(2)}, u32[]{:S(2)}) collective-permute-start(bf16[64,1024]{1,0:T(8,128)(2,1)S(1)} %get-tuple-element.14.refs_2_), channel_id=1, source_target_pairs={{0,31},{1,0},{2,1},{3,2},{4,3},{5,4},{6,5},{7,6},{8,7},{9,8},{10,9... | collective-permute-start | bytes 393224 | tf_op jit(solution)/shard_map/ppermute | solution.py:302
  46.8 2.0 %collective-permute-start.4 = (bf16[64,1024]{1,0:T(8,128)(2,1)S(1)}, bf16[64,1024]{1,0:T(8,128)(2,1)S(1)}, u32[]{:S(2)}, u32[]{:S(2)}) collective-permute-start(bf16[64,1024]{1,0:T(8,128)(2,1)S(1)} %get-tuple-element.14.refs_2_), channel_id=1, source_target_pairs={{0,30},{1,31},{2,0},{3,1},{4,2},{5,3},{6,4},{7,5},{8,6},{9,7},{10,... | collective-permute-start | bytes 393224 | tf_op jit(solution)/shard_map/ppermute | solution.py:302
  48.7 0.0 copy-done.8
  48.7 0.0 copy-done.12
  48.7 0.0 copy-start.13
  48.7 6.5 %shard_map.132.refs_12_.refs_0_ = bf16[2,16,64,256]{3,2,1,0:T(8,128)(2,1)S(1)} custom-call(bf16[4,16,64,256]{3,2,1,0:T(8,128)(2,1)S(1)} %get-tuple-element.16.refs_0_.refs_6_.refs_3_, s32[1,1024]{1,0:T(1,128)S(1)} %bitcast.11, f32[4,256,256]{2,1,0:T(8,128)S(1)} %get-tuple-element.17.refs_2_, bf16[2,64,128]{2,1,0:T(8,128)(2,1)S(1)} %copy-done.8, ...), custom_call_target="tpu_custom_call" | custom-call | flops 2147483648 | bytes 4194304 | tf_op jit(solution)/shard_map/pallas_call | solution.py:248
  55.3 0.0 collective-permute-done.1.refs_0_
  55.3 0.0 collective-permute-done.2.refs_1_
  55.3 0.0 collective-permute-done.3.refs_3_
  55.3 0.0 collective-permute-done.4.refs_4_
  55.3 0.0 copy-done.13
  55.3 14.1 %shard_map.133 = (f32[64,1024]{1,0:T(8,128)}, bf16[4,16,64,256]{3,2,1,0:T(8,128)(2,1)S(1)}, f32[1,256]{1,0:T(1,128)S(1)}) custom-call(bf16[64,1024]{1,0:T(8,128)(2,1)S(1)} %collective-permute-done.1.refs_0_, bf16[64,1024]{1,0:T(8,128)(2,1)S(1)} %collective-permute-done.2.refs_1_, bf16[64,1024]{1,0:T(8,128)(2,1)S(1)} %get-tuple-element.14.refs_2_, ...), custom_call_target="tpu_custom_call" | custom-call | flops 10737418240 | bytes 8388608 | tf_op jit(solution)/shard_map/pallas_call | solution.py:171
  69.4 0.0 collective-permute-start.5
  69.4 0.1 collective-permute-start.6
  69.5 1.7 %collective-permute-start.7 = (f32[1,256]{1,0:T(1,128)S(1)}, f32[1,256]{1,0:T(1,128)S(1)}, u32[]{:S(2)}, u32[]{:S(2)}) collective-permute-start(f32[1,256]{1,0:T(1,128)S(1)} %get-tuple-element.20), channel_id=1, source_target_pairs={{0,3},{1,0},{2,1},{3,2},{4,7},{5,4},{6,5},{7,6},{8,11},{9,8},{10,9... | collective-permute-start | bytes 3080 | tf_op jit(solution)/shard_map/ppermute | solution.py:323
  71.2 1.2 %collective-permute-done.5 = f32[1,256]{1,0:T(1,128)S(1)} collective-permute-done((f32[1,256]{1,0:T(1,128)S(1)}, f32[1,256]{1,0:T(1,128)S(1)}, u32[]{:S(2)}, u32[]{:S(2)}) %collective-permute-start.5) | collective-permute-done | bytes 1056 | tf_op jit(solution)/shard_map/ppermute | solution.py:323
  72.4 0.6 collective-permute-done.6
  73.0 0.0 collective-permute-done.7
  73.0 0.1 collective-permute-start.8
  73.1 3.3 %shard_map.135.refs_2_ = bf16[1,16,64,256]{3,2,1,0:T(8,128)(2,1)S(1)} custom-call(bf16[4,16,64,256]{3,2,1,0:T(8,128)(2,1)S(1)} %get-tuple-element.16.refs_0_.refs_6_.refs_3_, s32[1,1024]{1,0:T(1,128)S(1)} %bitcast.13, f32[4,256,256]{2,1,0:T(8,128)S(1)} %get-tuple-element.17.refs_2_, bf16[2,64,128]{2,1,0:T(8,128)(2,1)S(1)} %copy-done.8, f32[2,64]{1,0:T(2,128)S(1)} %copy-done.12), custom_call_target="tpu_custom_call" | custom-call | flops 1073741824 | bytes 2097152 | tf_op jit(solution)/shard_map/pallas_call | solution.py:248
  76.4 0.3 collective-permute-done.8
  76.7 0.0 collective-permute-start.9
  76.7 3.3 %shard_map.134.refs_1_ = bf16[1,16,64,256]{3,2,1,0:T(8,128)(2,1)S(1)} custom-call(bf16[4,16,64,256]{3,2,1,0:T(8,128)(2,1)S(1)} %get-tuple-element.16.refs_0_.refs_6_.refs_3_, s32[1,1024]{1,0:T(1,128)S(1)} %bitcast.14, f32[4,256,256]{2,1,0:T(8,128)S(1)} %get-tuple-element.17.refs_2_, bf16[2,64,128]{2,1,0:T(8,128)(2,1)S(1)} %copy-done.8, f32[2,64]{1,0:T(2,128)S(1)} %copy-done.12), custom_call_target="tpu_custom_call" | custom-call | flops 1073741824 | bytes 2097152 | tf_op jit(solution)/shard_map/pallas_call | solution.py:248
  79.9 0.3 collective-permute-done.9
  80.2 3.0 %collective-permute-start.10 = (f32[1,256]{1,0:T(1,128)S(1)}, f32[1,256]{1,0:T(1,128)S(1)}, u32[]{:S(2)}, u32[]{:S(2)}) collective-permute-start(f32[1,256]{1,0:T(1,128)S(1)} %add.22), channel_id=1, source_target_pairs={{0,16},{4,20},{8,24},{12,28},{16,0},{20,4},{24,8},{28,12},{1,17},{... | collective-permute-start | bytes 3080 | tf_op jit(solution)/shard_map/ppermute | solution.py:328
  83.2 2.3 %shard_map.136 = bf16[1024,1024]{1,0:T(8,128)(2,1)} custom-call(bf16[2,16,64,256]{3,2,1,0:T(8,128)(2,1)S(1)} %shard_map.132.refs_12_.refs_0_, bf16[1,16,64,256]{3,2,1,0:T(8,128)(2,1)S(1)} %shard_map.134.refs_1_, bf16[1,16,64,256]{3,2,1,0:T(8,128)(2,1)S(1)} %shard_map.135.refs_2_, bf16[4,16,64,256]{3,2,1,0:T(8,128)(2,1)S(1)} %get-tuple-element.16.refs_0_.refs_6_.refs_3_, ...), custom_call_target="tpu_custom_call" | custom-call | flops 1073741824 | bytes 8388608 | tf_op jit(solution)/shard_map/pallas_call | solution.py:285
  85.5 0.0 collective-permute-done.10
  85.5 0.6 add_reduce_fusion
  (3 shorter events, 0.0 us)
Async XLA Ops:
  1.9 25.4 %collective-permute-start = (bf16[64,2048]{1,0:T(8,128)(2,1)S(1)}, bf16[64,2048]{1,0:T(8,128)(2,1)S(1)}, u32[]{:S(2)}, u32[]{:S(2)}) collective-permute-start(bf16[64,2048]{1,0:T(8,128)(2,1)S(1)} %fusion), channel_id=1, source_target_pairs={{30,0},{4,2},{31,1},{5,3},{2,4},{8,6},{3,5},{9,7},{6,8},{12,10},{7... | collective-permute-start | bytes 786440 | tf_op jit(solution)/shard_map/ppermute | solution.py:315
  8.9 1.6 %copy-start.2 = (bf16[1024,1024]{1,0:T(8,128)(2,1)S(1)}, bf16[1024,1024]{1,0:T(8,128)(2,1)}, u32[]{:S(2)}) copy-start(bf16[1024,1024]{1,0:T(8,128)(2,1)} %refs_0_.1) | copy-start | bytes 6291460
  10.5 1.2 %copy-start.3 = (f32[1024,256]{1,0:T(8,128)S(1)}, f32[1024,256]{1,0:T(8,128)}, u32[]{:S(2)}) copy-start(f32[1024,256]{1,0:T(8,128)} %refs_2_.1) | copy-start | bytes 3145732
  11.7 0.8 copy-start.7
  12.5 0.7 copy-start.9
  13.1 0.7 copy-start.11
  13.8 13.5 %copy-start = (f32[4096,64]{0,1:T(8,128)S(1)}, f32[4096,64]{0,1:T(8,128)}, u32[]{:S(2)}) copy-start(f32[4096,64]{0,1:T(8,128)} %param.11) | copy-start | bytes 3145732
  13.8 13.5 %copy-start.1 = (bf16[2,64,64]{2,1,0:T(8,128)(2,1)S(1)}, bf16[2,64,64]{2,1,0:T(8,128)(2,1)}, u32[]{:S(2)}) copy-start(bf16[2,64,64]{2,1,0:T(8,128)(2,1)} %refs_5_.3) | copy-start | bytes 49156
  13.8 13.5 %copy-start.4 = (bf16[2,192,192]{2,1,0:T(8,128)(2,1)S(1)}, bf16[2,192,192]{2,1,0:T(8,128)(2,1)}, u32[]{:S(2)}) copy-start(bf16[2,192,192]{2,1,0:T(8,128)(2,1)} %refs_9_.1) | copy-start | bytes 442372
  13.8 13.5 %copy-start.5 = (s32[1024,16]{0,1:T(8,128)S(1)}, s32[1024,16]{0,1:T(8,128)}, u32[]{:S(2)}) copy-start(s32[1024,16]{0,1:T(8,128)} %param.13) | copy-start | bytes 196612
  13.8 13.5 %copy-start.6 = (bf16[2,64,64]{2,1,0:T(8,128)(2,1)S(1)}, bf16[2,64,64]{2,1,0:T(8,128)(2,1)}, u32[]{:S(2)}) copy-start(bf16[2,64,64]{2,1,0:T(8,128)(2,1)} %refs_10_.1) | copy-start | bytes 49156
  13.8 13.5 %copy-start.10 = (s32[1024]{0:T(1024)S(1)}, s32[1024]{0:T(1024)}, u32[]{:S(2)}) copy-start(s32[1024]{0:T(1024)} %param.14) | copy-start | bytes 12292
  27.3 21.4 %copy-start.8 = (bf16[2,64,128]{2,1,0:T(8,128)(2,1)S(1)}, bf16[2,64,128]{2,1,0:T(8,128)(2,1)}, u32[]{:S(2)}) copy-start(bf16[2,64,128]{2,1,0:T(8,128)(2,1)} %refs_3_.7) | copy-start | bytes 98308
  27.4 21.4 %copy-start.12 = (f32[2,64]{1,0:T(2,128)S(1)}, f32[2,64]{1,0:T(2,128)}, u32[]{:S(2)}) copy-start(f32[2,64]{1,0:T(2,128)} %refs_4_.7) | copy-start | bytes 1540
  41.3 14.0 %collective-permute-start.1 = (bf16[64,1024]{1,0:T(8,128)(2,1)S(1)}, bf16[64,1024]{1,0:T(8,128)(2,1)S(1)}, u32[]{:S(2)}, u32[]{:S(2)}) collective-permute-start(bf16[64,1024]{1,0:T(8,128)(2,1)S(1)} %get-tuple-element.14.refs_2_), channel_id=1, source_target_pairs={{0,2},{1,3},{2,4},{3,5},{4,6},{5,7},{6,8},{7,9},{8,10},{9,11},{10,... | collective-permute-start | bytes 393224 | tf_op jit(solution)/shard_map/ppermute | solution.py:302
  41.4 13.9 %collective-permute-start.2 = (bf16[64,1024]{1,0:T(8,128)(2,1)S(1)}, bf16[64,1024]{1,0:T(8,128)(2,1)S(1)}, u32[]{:S(2)}, u32[]{:S(2)}) collective-permute-start(bf16[64,1024]{1,0:T(8,128)(2,1)S(1)} %get-tuple-element.14.refs_2_), channel_id=1, source_target_pairs={{0,1},{1,2},{2,3},{3,4},{4,5},{5,6},{6,7},{7,8},{8,9},{9,10},{10,1... | collective-permute-start | bytes 393224 | tf_op jit(solution)/shard_map/ppermute | solution.py:302
  41.5 13.9 %collective-permute-start.3 = (bf16[64,1024]{1,0:T(8,128)(2,1)S(1)}, bf16[64,1024]{1,0:T(8,128)(2,1)S(1)}, u32[]{:S(2)}, u32[]{:S(2)}) collective-permute-start(bf16[64,1024]{1,0:T(8,128)(2,1)S(1)} %get-tuple-element.14.refs_2_), channel_id=1, source_target_pairs={{0,31},{1,0},{2,1},{3,2},{4,3},{5,4},{6,5},{7,6},{8,7},{9,8},{10,9... | collective-permute-start | bytes 393224 | tf_op jit(solution)/shard_map/ppermute | solution.py:302
  46.8 8.5 %collective-permute-start.4 = (bf16[64,1024]{1,0:T(8,128)(2,1)S(1)}, bf16[64,1024]{1,0:T(8,128)(2,1)S(1)}, u32[]{:S(2)}, u32[]{:S(2)}) collective-permute-start(bf16[64,1024]{1,0:T(8,128)(2,1)S(1)} %get-tuple-element.14.refs_2_), channel_id=1, source_target_pairs={{0,30},{1,31},{2,0},{3,1},{4,2},{5,3},{6,4},{7,5},{8,6},{9,7},{10,... | collective-permute-start | bytes 393224 | tf_op jit(solution)/shard_map/ppermute | solution.py:302
  48.7 6.6 %copy-start.13 = (f32[64]{0:T(128)S(1)}, f32[64]{0:T(128)}, u32[]{:S(2)}) copy-start(f32[64]{0:T(128)} %param.21) | copy-start | bytes 772
  69.4 3.0 %collective-permute-start.5 = (f32[1,256]{1,0:T(1,128)S(1)}, f32[1,256]{1,0:T(1,128)S(1)}, u32[]{:S(2)}, u32[]{:S(2)}) collective-permute-start(f32[1,256]{1,0:T(1,128)S(1)} %get-tuple-element.20), channel_id=1, source_target_pairs={{0,1},{1,2},{2,3},{3,0},{4,5},{5,6},{6,7},{7,4},{8,9},{9,10},{10,1... | collective-permute-start | bytes 3080 | tf_op jit(solution)/shard_map/ppermute | solution.py:323
  69.4 3.6 %collective-permute-start.6 = (f32[1,256]{1,0:T(1,128)S(1)}, f32[1,256]{1,0:T(1,128)S(1)}, u32[]{:S(2)}, u32[]{:S(2)}) collective-permute-start(f32[1,256]{1,0:T(1,128)S(1)} %get-tuple-element.20), channel_id=1, source_target_pairs={{0,2},{1,3},{2,0},{3,1},{4,6},{5,7},{6,4},{7,5},{8,10},{9,11},{10,... | collective-permute-start | bytes 3080 | tf_op jit(solution)/shard_map/ppermute | solution.py:323
  69.5 3.5 %collective-permute-start.7 = (f32[1,256]{1,0:T(1,128)S(1)}, f32[1,256]{1,0:T(1,128)S(1)}, u32[]{:S(2)}, u32[]{:S(2)}) collective-permute-start(f32[1,256]{1,0:T(1,128)S(1)} %get-tuple-element.20), channel_id=1, source_target_pairs={{0,3},{1,0},{2,1},{3,2},{4,7},{5,4},{6,5},{7,6},{8,11},{9,8},{10,9... | collective-permute-start | bytes 3080 | tf_op jit(solution)/shard_map/ppermute | solution.py:323
  73.0 3.6 %collective-permute-start.8 = (f32[1,256]{1,0:T(1,128)S(1)}, f32[1,256]{1,0:T(1,128)S(1)}, u32[]{:S(2)}, u32[]{:S(2)}) collective-permute-start(f32[1,256]{1,0:T(1,128)S(1)} %add_add_fusion), channel_id=1, source_target_pairs={{0,4},{4,0},{8,12},{12,8},{16,20},{20,16},{24,28},{28,24},{1,5},{5... | collective-permute-start | bytes 3080 | tf_op jit(solution)/shard_map/ppermute | solution.py:328
  76.7 3.6 %collective-permute-start.9 = (f32[1,256]{1,0:T(1,128)S(1)}, f32[1,256]{1,0:T(1,128)S(1)}, u32[]{:S(2)}, u32[]{:S(2)}) collective-permute-start(f32[1,256]{1,0:T(1,128)S(1)} %add.21), channel_id=1, source_target_pairs={{0,8},{4,12},{8,0},{12,4},{16,24},{20,28},{24,16},{28,20},{1,9},{5... | collective-permute-start | bytes 3080 | tf_op jit(solution)/shard_map/ppermute | solution.py:328
  80.2 5.3 %collective-permute-start.10 = (f32[1,256]{1,0:T(1,128)S(1)}, f32[1,256]{1,0:T(1,128)S(1)}, u32[]{:S(2)}, u32[]{:S(2)}) collective-permute-start(f32[1,256]{1,0:T(1,128)S(1)} %add.22), channel_id=1, source_target_pairs={{0,16},{4,20},{8,24},{12,28},{16,0},{20,4},{24,8},{28,12},{1,17},{... | collective-permute-start | bytes 3080 | tf_op jit(solution)/shard_map/ppermute | solution.py:328

commit v4 on v3

--- a/solution.py
+++ b/solution.py
@@ -226,7 +226,7 @@
             angular_out[step, j] = (tree_total(stack).astype(F32) * inverse).astype(BF)
             return inner
 
-        lax.fori_loop(0, slots, slot, 0)
+        lax.fori_loop(0, slots, slot, 0, unroll=2)
         return carry
 
     lax.fori_loop(0, steps, block, 0)
@@ -302,16 +302,28 @@
     return lax.ppermute(value, AXES, [(source, (source + steps) % count) for source in range(count)])
 
 
+def edge_kernel(domain_ref, payload_ref):
+    rim = payload_ref.shape[1]
+    start = jnp.where(lax.axis_index("rep") < 2, domain_ref.shape[1] - rim, 0)
+    payload_ref[...] = domain_ref[:, pl.ds(pl.multiple_of(start, LANES), rim)].astype(BF)
+
+
 def far_side(domain, quarter):
     rim = 2 * quarter
     rep = lax.axis_size("rep")
     total = lax.axis_size(AXES)
-    payload = jnp.where(lax.axis_index("rep") < 2, domain[:, :rim], domain[:, -rim:]).astype(BF)
+    payload = pl.pallas_call(
+        edge_kernel,
+        out_shape=jax.ShapeDtypeStruct((domain.shape[0], rim), BF),
+        in_specs=[VMEM],
+        out_specs=VMEM,
+        compiler_params=PARAMS,
+        cost_estimate=pl.CostEstimate(flops=10 * 2**30, bytes_accessed=2**23, transcendentals=2**22),
+    )(domain)
     pairs = []
     for start in range(0, total, rep):
-        for d in range(2):
-            pairs.append(((start + d - 2) % total, start + d))
-            pairs.append(((start + rep + d) % total, start + rep - 2 + d))
+        for d in range(rep):
+            pairs.append(((start + d + (-rep if d < 2 else rep)) % total, start + d))
     return lax.ppermute(payload, AXES, pairs)
 
 

time: 88.2 us -> 82.1 us (0.931)
  local copies, waits for them, and re-layouts: 4.98 us -> 1.27 us
  Pallas kernels: 56.8 us -> 55.3 us
  other arithmetic: 1.86 us -> 0.61 us
    ppermute x1, starting transfers between devices: 7 us -> 2.99 us  [far_side(): return lax.ppermute(payload, AXES, pairs)]
    unnamed x28 -> x22, local copies, waits for them, and re-layouts: 4.98 us -> 1.27 us
    ppermute x4, starting transfers between devices: 7.41 us -> 9.96 us  [passed_along(): lax.ppermute(value, AXES, [(source, (source + steps) % count) for source...]
    ppermute x3, starting transfers between devices: 1.78 us -> 3.49 us  [over_rep(): lax.ppermute(value, 'rep', [(i, (i + s) % rep) for i in range(rep)])]
    pallas_call x4, Pallas kernels: 26.5 us -> 24.9 us  [run_angle(): pl.pallas_call(functools.partial(angle_kernel, layer, first, start, steps...]
    convert_element_type x1 -> x0, other arithmetic: 1.25 us -> none  [far_side(): jnp.where(lax.axis_index('rep') < 2, domain[:, :rim], domain[:, -rim:])]
where the time goes in v4:
time: 82.1 us; the launch traced here: 82 us
  Pallas kernels  55.3 us (67%)
  starting transfers between devices  19.9 us (24%)
  between operations  2.62 us (3%)
  waiting for transfers between devices  2.3 us (3%)
  local copies, waits for them, and re-layouts  1.27 us (2%)
    pallas_call x2, Pallas kernels, run_gather(): pl.pallas_call(functools.partial(gather_kernel, layer, first, last, slots...  28 us
    pallas_call x4, Pallas kernels, run_angle(): pl.pallas_call(functools.partial(angle_kernel, layer, first, start, steps...  24.9 us
    ppermute x4, starting transfers between devices, passed_along(): lax.ppermute(value, AXES, [(source, (source + steps) % count) for source...  9.96 us
    ppermute x3, starting transfers between devices, over_rep(): lax.ppermute(value, 'rep', [(i, (i + s) % rep) for i in range(rep)])  3.49 us
    ppermute x3, starting transfers between devices, over_space(): lax.ppermute(value, 'space', [(i, i ^ step) for i in range(space)])  3.47 us
    ppermute x1, starting transfers between devices, far_side(): return lax.ppermute(payload, AXES, pairs)  2.99 us
    pallas_call x1, Pallas kernels, run_update(): pl.pallas_call(functools.partial(update_kernel, layer, slots, channels, l...  2.31 us
  transfers between devices with their start and end apart: 11, of which 4 were waited for; matrix products, arithmetic and copies ran while one was open for 0% of the time, Pallas kernels for 33%

profile of v4, /device:TPU:0, one launch (start us, length us, event | category | flops | bytes accessed | tf_op | source)
XLA Modules:
  0.0 82.0 jit_solution(348157771067403671)
XLA Ops:
  0.6 0.0 copy-start.3
  0.6 1.2 %copy-done.3 = f32[4096,64]{0,1:T(8,128)S(1)} copy-done((f32[4096,64]{0,1:T(8,128)S(1)}, f32[4096,64]{0,1:T(8,128)}, u32[]{:S(2)}) %copy-start.3) | copy-done | bytes 1048600
  1.9 0.0 copy-start.1
  1.9 0.0 copy-start.2
  1.9 0.0 copy-start.7
  1.9 0.0 copy-start.8
  1.9 0.0 copy-start.9
  1.9 3.0 %collective-permute-start = (bf16[64,2048]{1,0:T(8,128)(2,1)S(1)}, bf16[64,2048]{1,0:T(8,128)(2,1)S(1)}, u32[]{:S(2)}, u32[]{:S(2)}) collective-permute-start(bf16[64,2048]{1,0:T(8,128)(2,1)S(1)} %shard_map.130), channel_id=1, source_target_pairs={{28,0},{29,1},{6,2},{7,3},{0,4},{1,5},{10,6},{11,7},{4,8},{5,9},{1... | collective-permute-start | bytes 786440 | tf_op jit(solution)/shard_map/ppermute | solution.py:327
  4.9 0.0 copy-done.1
  4.9 0.0 copy-done.2
  4.9 0.0 copy-done.7
  4.9 0.0 copy-done.8
  4.9 0.0 copy-done.9
  4.9 0.0 copy-start
  5.0 0.0 copy-start.4
  5.0 0.0 copy-start.5
  5.0 0.0 copy-start.6
  5.0 12.6 %shard_map.131 = (bf16[4,16,64,256]{3,2,1,0:T(8,128)(2,1)S(1)}, bf16[4,16,64,256]{3,2,1,0:T(8,128)(2,1)S(1)}, f32[4,256,256]{2,1,0:T(8,128)S(1)}) custom-call(bf16[1024,1024]{1,0:T(8,128)(2,1)S(1)} %copy-done.1, s32[1,1024]{1,0:T(1,128)S(1)} %bitcast.9, f32[1024,256]{1,0:T(8,128)S(1)} %copy-done.2, bf16[2,64,128]{2,1,0:T(8,128)(2,1)S(1)} %copy-done.7, ...), custom_call_target="tpu_custom_call" | custom-call | flops 4294967296 | bytes 8388608 | tf_op jit(solution)/shard_map/pallas_call | solution.py:248
  17.6 0.0 collective-permute-done.refs_1_
  17.6 0.0 copy-done
  17.6 0.0 copy-done.4
  17.6 0.0 copy-done.5
  17.6 0.0 copy-done.6
  17.7 13.9 %shard_map.132 = (f32[64,1024]{1,0:T(8,128)S(1)}, bf16[64,1024]{1,0:T(8,128)(2,1)S(1)}, bf16[4,16,64,256]{3,2,1,0:T(8,128)(2,1)S(1)}) custom-call(f32[64,4096]{1,0:T(8,128)S(1)} %bitcast.6, bf16[64,2048]{1,0:T(8,128)(2,1)S(1)} %collective-permute-done.refs_1_, bf16[4,16,64,256]{3,2,1,0:T(8,128)(2,1)S(1)} %get-tuple-element.12.refs_2_, ...), custom_call_target="tpu_custom_call" | custom-call | flops 10737418240 | bytes 8388608 | tf_op jit(solution)/shard_map/pallas_call | solution.py:171
  31.6 4.6 %collective-permute-start.1 = (bf16[64,1024]{1,0:T(8,128)(2,1)S(1)}, bf16[64,1024]{1,0:T(8,128)(2,1)S(1)}, u32[]{:S(2)}, u32[]{:S(2)}) collective-permute-start(bf16[64,1024]{1,0:T(8,128)(2,1)S(1)} %get-tuple-element.14.refs_2_), channel_id=1, source_target_pairs={{0,2},{1,3},{2,4},{3,5},{4,6},{5,7},{6,8},{7,9},{8,10},{9,11},{10,... | collective-permute-start | bytes 393224 | tf_op jit(solution)/shard_map/ppermute | solution.py:302
  36.2 0.0 collective-permute-start.2
  36.2 5.3 %collective-permute-start.3 = (bf16[64,1024]{1,0:T(8,128)(2,1)S(1)}, bf16[64,1024]{1,0:T(8,128)(2,1)S(1)}, u32[]{:S(2)}, u32[]{:S(2)}) collective-permute-start(bf16[64,1024]{1,0:T(8,128)(2,1)S(1)} %get-tuple-element.14.refs_2_), channel_id=1, source_target_pairs={{0,31},{1,0},{2,1},{3,2},{4,3},{5,4},{6,5},{7,6},{8,7},{9,8},{10,9... | collective-permute-start | bytes 393224 | tf_op jit(solution)/shard_map/ppermute | solution.py:302
  41.5 0.0 collective-permute-start.4
  41.6 0.0 copy-start.10
  41.6 6.2 %shard_map.133.refs_12_.refs_0_ = bf16[2,16,64,256]{3,2,1,0:T(8,128)(2,1)S(1)} custom-call(bf16[4,16,64,256]{3,2,1,0:T(8,128)(2,1)S(1)} %get-tuple-element.16.refs_0_.refs_6_.refs_3_, s32[1,1024]{1,0:T(1,128)S(1)} %bitcast.11, f32[4,256,256]{2,1,0:T(8,128)S(1)} %get-tuple-element.17.refs_2_, bf16[2,64,128]{2,1,0:T(8,128)(2,1)S(1)} %copy-done.7, ...), custom_call_target="tpu_custom_call" | custom-call | flops 2147483648 | bytes 4194304 | tf_op jit(solution)/shard_map/pallas_call | solution.py:248
  47.7 0.0 collective-permute-done.1.refs_0_
  47.7 0.0 collective-permute-done.2.refs_1_
  47.8 0.0 collective-permute-done.3.refs_3_
  47.8 0.0 collective-permute-done.4.refs_4_
  47.8 0.0 copy-done.10
  47.8 14.1 %shard_map.134 = (f32[64,1024]{1,0:T(8,128)}, bf16[4,16,64,256]{3,2,1,0:T(8,128)(2,1)S(1)}, f32[1,256]{1,0:T(1,128)S(1)}) custom-call(bf16[64,1024]{1,0:T(8,128)(2,1)S(1)} %collective-permute-done.1.refs_0_, bf16[64,1024]{1,0:T(8,128)(2,1)S(1)} %collective-permute-done.2.refs_1_, bf16[64,1024]{1,0:T(8,128)(2,1)S(1)} %get-tuple-element.14.refs_2_, ...), custom_call_target="tpu_custom_call" | custom-call | flops 10737418240 | bytes 8388608 | tf_op jit(solution)/shard_map/pallas_call | solution.py:171
  61.8 0.1 collective-permute-start.5
  62.0 1.9 %collective-permute-start.6 = (f32[1,256]{1,0:T(1,128)S(1)}, f32[1,256]{1,0:T(1,128)S(1)}, u32[]{:S(2)}, u32[]{:S(2)}) collective-permute-start(f32[1,256]{1,0:T(1,128)S(1)} %get-tuple-element.20), channel_id=1, source_target_pairs={{0,2},{1,3},{2,0},{3,1},{4,6},{5,7},{6,4},{7,5},{8,10},{9,11},{10,... | collective-permute-start | bytes 3080 | tf_op jit(solution)/shard_map/ppermute | solution.py:335
  63.9 1.4 %collective-permute-start.7 = (f32[1,256]{1,0:T(1,128)S(1)}, f32[1,256]{1,0:T(1,128)S(1)}, u32[]{:S(2)}, u32[]{:S(2)}) collective-permute-start(f32[1,256]{1,0:T(1,128)S(1)} %get-tuple-element.20), channel_id=1, source_target_pairs={{0,3},{1,0},{2,1},{3,2},{4,7},{5,4},{6,5},{7,6},{8,11},{9,8},{10,9... | collective-permute-start | bytes 3080 | tf_op jit(solution)/shard_map/ppermute | solution.py:335
  65.3 0.0 collective-permute-done.5
  65.3 0.2 collective-permute-done.6
  65.6 1.1 %collective-permute-done.7 = f32[1,256]{1,0:T(1,128)S(1)} collective-permute-done((f32[1,256]{1,0:T(1,128)S(1)}, f32[1,256]{1,0:T(1,128)S(1)}, u32[]{:S(2)}, u32[]{:S(2)}) %collective-permute-start.7) | collective-permute-done | bytes 1056 | tf_op jit(solution)/shard_map/ppermute | solution.py:335
  66.6 0.0 collective-permute-start.8
  66.6 3.1 %shard_map.136.refs_2_ = bf16[1,16,64,256]{3,2,1,0:T(8,128)(2,1)S(1)} custom-call(bf16[4,16,64,256]{3,2,1,0:T(8,128)(2,1)S(1)} %get-tuple-element.16.refs_0_.refs_6_.refs_3_, s32[1,1024]{1,0:T(1,128)S(1)} %bitcast.13, f32[4,256,256]{2,1,0:T(8,128)S(1)} %get-tuple-element.17.refs_2_, bf16[2,64,128]{2,1,0:T(8,128)(2,1)S(1)} %copy-done.7, f32[2,64]{1,0:T(2,128)S(1)} %copy-done.9), custom_call_target="tpu_custom_call" | custom-call | flops 1073741824 | bytes 2097152 | tf_op jit(solution)/shard_map/pallas_call | solution.py:248
  69.7 0.5 collective-permute-done.8
  70.2 0.0 collective-permute-start.9
  70.2 3.1 %shard_map.135.refs_1_ = bf16[1,16,64,256]{3,2,1,0:T(8,128)(2,1)S(1)} custom-call(bf16[4,16,64,256]{3,2,1,0:T(8,128)(2,1)S(1)} %get-tuple-element.16.refs_0_.refs_6_.refs_3_, s32[1,1024]{1,0:T(1,128)S(1)} %bitcast.14, f32[4,256,256]{2,1,0:T(8,128)S(1)} %get-tuple-element.17.refs_2_, bf16[2,64,128]{2,1,0:T(8,128)(2,1)S(1)} %copy-done.7, f32[2,64]{1,0:T(2,128)S(1)} %copy-done.9), custom_call_target="tpu_custom_call" | custom-call | flops 1073741824 | bytes 2097152 | tf_op jit(solution)/shard_map/pallas_call | solution.py:248
  73.3 0.5 collective-permute-done.9
  73.8 3.5 %collective-permute-start.10 = (f32[1,256]{1,0:T(1,128)S(1)}, f32[1,256]{1,0:T(1,128)S(1)}, u32[]{:S(2)}, u32[]{:S(2)}) collective-permute-start(f32[1,256]{1,0:T(1,128)S(1)} %add.22), channel_id=1, source_target_pairs={{0,16},{4,20},{8,24},{12,28},{16,0},{20,4},{24,8},{28,12},{1,17},{... | collective-permute-start | bytes 3080 | tf_op jit(solution)/shard_map/ppermute | solution.py:340
  77.3 2.3 %shard_map.137 = bf16[1024,1024]{1,0:T(8,128)(2,1)} custom-call(bf16[2,16,64,256]{3,2,1,0:T(8,128)(2,1)S(1)} %shard_map.133.refs_12_.refs_0_, bf16[1,16,64,256]{3,2,1,0:T(8,128)(2,1)S(1)} %shard_map.135.refs_1_, bf16[1,16,64,256]{3,2,1,0:T(8,128)(2,1)S(1)} %shard_map.136.refs_2_, bf16[4,16,64,256]{3,2,1,0:T(8,128)(2,1)S(1)} %get-tuple-element.16.refs_0_.refs_6_.refs_3_, ...), custom_call_target="tpu_custom_call" | custom-call | flops 1073741824 | bytes 8388608 | tf_op jit(solution)/shard_map/pallas_call | solution.py:285
  79.6 0.0 collective-permute-done.10
  79.6 0.6 add_reduce_fusion
  (4 shorter events, 0.0 us)
Async XLA Ops:
  0.6 1.2 %copy-start.3 = (f32[4096,64]{0,1:T(8,128)S(1)}, f32[4096,64]{0,1:T(8,128)}, u32[]{:S(2)}) copy-start(f32[4096,64]{0,1:T(8,128)} %param.11) | copy-start | bytes 3145732
  1.9 3.1 %copy-start.1 = (bf16[1024,1024]{1,0:T(8,128)(2,1)S(1)}, bf16[1024,1024]{1,0:T(8,128)(2,1)}, u32[]{:S(2)}) copy-start(bf16[1024,1024]{1,0:T(8,128)(2,1)} %refs_0_.1) | copy-start | bytes 6291460
  1.9 3.1 %copy-start.2 = (f32[1024,256]{1,0:T(8,128)S(1)}, f32[1024,256]{1,0:T(8,128)}, u32[]{:S(2)}) copy-start(f32[1024,256]{1,0:T(8,128)} %refs_2_.1) | copy-start | bytes 3145732
  1.9 3.1 %copy-start.7 = (bf16[2,64,128]{2,1,0:T(8,128)(2,1)S(1)}, bf16[2,64,128]{2,1,0:T(8,128)(2,1)}, u32[]{:S(2)}) copy-start(bf16[2,64,128]{2,1,0:T(8,128)(2,1)} %refs_3_.7) | copy-start | bytes 98308
  1.9 3.1 %copy-start.8 = (s32[1024]{0:T(1024)S(1)}, s32[1024]{0:T(1024)}, u32[]{:S(2)}) copy-start(s32[1024]{0:T(1024)} %param.14) | copy-start | bytes 12292
  1.9 3.1 %copy-start.9 = (f32[2,64]{1,0:T(2,128)S(1)}, f32[2,64]{1,0:T(2,128)}, u32[]{:S(2)}) copy-start(f32[2,64]{1,0:T(2,128)} %refs_4_.7) | copy-start | bytes 1540
  1.9 15.7 %collective-permute-start = (bf16[64,2048]{1,0:T(8,128)(2,1)S(1)}, bf16[64,2048]{1,0:T(8,128)(2,1)S(1)}, u32[]{:S(2)}, u32[]{:S(2)}) collective-permute-start(bf16[64,2048]{1,0:T(8,128)(2,1)S(1)} %shard_map.130), channel_id=1, source_target_pairs={{28,0},{29,1},{6,2},{7,3},{0,4},{1,5},{10,6},{11,7},{4,8},{5,9},{1... | collective-permute-start | bytes 786440 | tf_op jit(solution)/shard_map/ppermute | solution.py:327
  4.9 12.7 %copy-start = (bf16[2,64,64]{2,1,0:T(8,128)(2,1)S(1)}, bf16[2,64,64]{2,1,0:T(8,128)(2,1)}, u32[]{:S(2)}) copy-start(bf16[2,64,64]{2,1,0:T(8,128)(2,1)} %refs_5_.3) | copy-start | bytes 49156
  5.0 12.7 %copy-start.4 = (bf16[2,192,192]{2,1,0:T(8,128)(2,1)S(1)}, bf16[2,192,192]{2,1,0:T(8,128)(2,1)}, u32[]{:S(2)}) copy-start(bf16[2,192,192]{2,1,0:T(8,128)(2,1)} %refs_9_.1) | copy-start | bytes 442372
  5.0 12.7 %copy-start.5 = (s32[1024,16]{0,1:T(8,128)S(1)}, s32[1024,16]{0,1:T(8,128)}, u32[]{:S(2)}) copy-start(s32[1024,16]{0,1:T(8,128)} %param.13) | copy-start | bytes 196612
  5.0 12.7 %copy-start.6 = (bf16[2,64,64]{2,1,0:T(8,128)(2,1)S(1)}, bf16[2,64,64]{2,1,0:T(8,128)(2,1)}, u32[]{:S(2)}) copy-start(bf16[2,64,64]{2,1,0:T(8,128)(2,1)} %refs_10_.1) | copy-start | bytes 49156
  31.6 16.1 %collective-permute-start.1 = (bf16[64,1024]{1,0:T(8,128)(2,1)S(1)}, bf16[64,1024]{1,0:T(8,128)(2,1)S(1)}, u32[]{:S(2)}, u32[]{:S(2)}) collective-permute-start(bf16[64,1024]{1,0:T(8,128)(2,1)S(1)} %get-tuple-element.14.refs_2_), channel_id=1, source_target_pairs={{0,2},{1,3},{2,4},{3,5},{4,6},{5,7},{6,8},{7,9},{8,10},{9,11},{10,... | collective-permute-start | bytes 393224 | tf_op jit(solution)/shard_map/ppermute | solution.py:302
  36.2 11.5 %collective-permute-start.2 = (bf16[64,1024]{1,0:T(8,128)(2,1)S(1)}, bf16[64,1024]{1,0:T(8,128)(2,1)S(1)}, u32[]{:S(2)}, u32[]{:S(2)}) collective-permute-start(bf16[64,1024]{1,0:T(8,128)(2,1)S(1)} %get-tuple-element.14.refs_2_), channel_id=1, source_target_pairs={{0,1},{1,2},{2,3},{3,4},{4,5},{5,6},{6,7},{7,8},{8,9},{9,10},{10,1... | collective-permute-start | bytes 393224 | tf_op jit(solution)/shard_map/ppermute | solution.py:302
  36.2 11.5 %collective-permute-start.3 = (bf16[64,1024]{1,0:T(8,128)(2,1)S(1)}, bf16[64,1024]{1,0:T(8,128)(2,1)S(1)}, u32[]{:S(2)}, u32[]{:S(2)}) collective-permute-start(bf16[64,1024]{1,0:T(8,128)(2,1)S(1)} %get-tuple-element.14.refs_2_), channel_id=1, source_target_pairs={{0,31},{1,0},{2,1},{3,2},{4,3},{5,4},{6,5},{7,6},{8,7},{9,8},{10,9... | collective-permute-start | bytes 393224 | tf_op jit(solution)/shard_map/ppermute | solution.py:302
  41.5 6.2 %collective-permute-start.4 = (bf16[64,1024]{1,0:T(8,128)(2,1)S(1)}, bf16[64,1024]{1,0:T(8,128)(2,1)S(1)}, u32[]{:S(2)}, u32[]{:S(2)}) collective-permute-start(bf16[64,1024]{1,0:T(8,128)(2,1)S(1)} %get-tuple-element.14.refs_2_), channel_id=1, source_target_pairs={{0,30},{1,31},{2,0},{3,1},{4,2},{5,3},{6,4},{7,5},{8,6},{9,7},{10,... | collective-permute-start | bytes 393224 | tf_op jit(solution)/shard_map/ppermute | solution.py:302
  41.6 6.2 %copy-start.10 = (f32[64]{0:T(128)S(1)}, f32[64]{0:T(128)}, u32[]{:S(2)}) copy-start(f32[64]{0:T(128)} %param.21) | copy-start | bytes 772
  61.8 3.5 %collective-permute-start.5 = (f32[1,256]{1,0:T(1,128)S(1)}, f32[1,256]{1,0:T(1,128)S(1)}, u32[]{:S(2)}, u32[]{:S(2)}) collective-permute-start(f32[1,256]{1,0:T(1,128)S(1)} %get-tuple-element.20), channel_id=1, source_target_pairs={{0,1},{1,2},{2,3},{3,0},{4,5},{5,6},{6,7},{7,4},{8,9},{9,10},{10,1... | collective-permute-start | bytes 3080 | tf_op jit(solution)/shard_map/ppermute | solution.py:335
  62.0 3.6 %collective-permute-start.6 = (f32[1,256]{1,0:T(1,128)S(1)}, f32[1,256]{1,0:T(1,128)S(1)}, u32[]{:S(2)}, u32[]{:S(2)}) collective-permute-start(f32[1,256]{1,0:T(1,128)S(1)} %get-tuple-element.20), channel_id=1, source_target_pairs={{0,2},{1,3},{2,0},{3,1},{4,6},{5,7},{6,4},{7,5},{8,10},{9,11},{10,... | collective-permute-start | bytes 3080 | tf_op jit(solution)/shard_map/ppermute | solution.py:335
  63.9 2.7 %collective-permute-start.7 = (f32[1,256]{1,0:T(1,128)S(1)}, f32[1,256]{1,0:T(1,128)S(1)}, u32[]{:S(2)}, u32[]{:S(2)}) collective-permute-start(f32[1,256]{1,0:T(1,128)S(1)} %get-tuple-element.20), channel_id=1, source_target_pairs={{0,3},{1,0},{2,1},{3,2},{4,7},{5,4},{6,5},{7,6},{8,11},{9,8},{10,9... | collective-permute-start | bytes 3080 | tf_op jit(solution)/shard_map/ppermute | solution.py:335
  66.6 3.6 %collective-permute-start.8 = (f32[1,256]{1,0:T(1,128)S(1)}, f32[1,256]{1,0:T(1,128)S(1)}, u32[]{:S(2)}, u32[]{:S(2)}) collective-permute-start(f32[1,256]{1,0:T(1,128)S(1)} %add_add_fusion), channel_id=1, source_target_pairs={{0,4},{4,0},{8,12},{12,8},{16,20},{20,16},{24,28},{28,24},{1,5},{5... | collective-permute-start | bytes 3080 | tf_op jit(solution)/shard_map/ppermute | solution.py:340
  70.2 3.6 %collective-permute-start.9 = (f32[1,256]{1,0:T(1,128)S(1)}, f32[1,256]{1,0:T(1,128)S(1)}, u32[]{:S(2)}, u32[]{:S(2)}) collective-permute-start(f32[1,256]{1,0:T(1,128)S(1)} %add.21), channel_id=1, source_target_pairs={{0,8},{4,12},{8,0},{12,4},{16,24},{20,28},{24,16},{28,20},{1,9},{5... | collective-permute-start | bytes 3080 | tf_op jit(solution)/shard_map/ppermute | solution.py:340
  73.8 5.8 %collective-permute-start.10 = (f32[1,256]{1,0:T(1,128)S(1)}, f32[1,256]{1,0:T(1,128)S(1)}, u32[]{:S(2)}, u32[]{:S(2)}) collective-permute-start(f32[1,256]{1,0:T(1,128)S(1)} %add.22), channel_id=1, source_target_pairs={{0,16},{4,20},{8,24},{12,28},{16,0},{20,4},{24,8},{28,12},{1,17},{... | collective-permute-start | bytes 3080 | tf_op jit(solution)/shard_map/ppermute | solution.py:340

commit v5 on v4

--- a/solution.py
+++ b/solution.py
@@ -93,51 +93,47 @@
     columns = lax.broadcasted_iota(jnp.int32, (LANES, LANES), 0)
     lane = lax.broadcasted_iota(jnp.int32, (1, LANES), 1) + rim * LANES
 
-    def block(b, carry):
+    def gather(b, group):
         base = skip + b
-        here = block_lanes(b)
+        here = slice(b * LANES, (b + 1) * LANES)
+        for u in range(BATCH):
+            j = group * BATCH + u
+            index = off_ref[j : j + 1, here] + lane
+            low = index % LANES
+            high = index // LANES
+            chosen = jnp.where(columns == low, 1.0, 0.0).astype(BF)
+            lhs = tab[pl.ds(base, reach)].reshape(reach * channels, LANES)
+            picked = jnp.dot(lhs, chosen, preferred_element_type=F32)
+            result = picked[:channels]
+            for h in range(1, reach):
+                result = jnp.where(high == h, picked[h * channels : (h + 1) * channels], result)
+            n_s[group % 2, u] = result.astype(BF)
+
+    def gates(b, group):
+        base = skip + b
+        here = slice(b * LANES, (b + 1) * LANES)
         own = tab[base + rim]
         count = cnt_ref[:, here]
-
-        def gather(group):
-            for j in range(group * BATCH, (group + 1) * BATCH):
-                index = off_ref[j : j + 1, here] + lane
-                low = index % LANES
-                high = index // LANES
-                chosen = jnp.where(columns == low, 1.0, 0.0).astype(BF)
-                lhs = tab[pl.ds(base, reach)].reshape(reach * channels, LANES)
-                picked = jnp.dot(lhs, chosen, preferred_element_type=F32)
-                result = picked[:channels]
-                for h in range(1, reach):
-                    result = jnp.where(high == h, picked[h * channels : (h + 1) * channels], result)
-                n_s[j] = result.astype(BF)
-
-        def gates(group):
-            total = msg_s[...] if group else None
-            for u in range(BATCH):
-                j = group * BATCH + u
-                live = jnp.where(j < count, 1.0, 0.0)
-                bond = bond_ref[b, j]
-                joined = jnp.concatenate([own, n_s[j], bond], axis=0)
-                mixed = jnp.dot(core_t[...], joined, preferred_element_type=F32)
-                gate = jnp.tanh(mixed)
-                cores = mixed[channels : 2 * channels]
-                message = (1.0 + gate[:channels]) * (cores + cores * gate[channels : 2 * channels]) * live
-                total = message if total is None else total + message
-                bond_gate = (1.0 + gate[2 * channels :]) * live
-                if last:
-                    gate_out[b, j] = bond_gate.astype(BF)
-                else:
-                    bonds_out[b, j] = bond_update(bond_t[...], angular_ref[b, j], bond, bond_gate)
+        total = msg_s[...] if group else None
+        for u in range(BATCH):
+            j = group * BATCH + u
+            live = jnp.where(j < count, 1.0, 0.0)
+            bond = bond_ref[b, j]
+            joined = jnp.concatenate([own, n_s[group % 2, u], bond], axis=0)
+            mixed = jnp.dot(core_t[...], joined, preferred_element_type=F32)
+            gate = jnp.tanh(mixed)
+            cores = mixed[channels : 2 * channels]
+            message = (1.0 + gate[:channels]) * (cores + cores * gate[channels : 2 * channels]) * live
+            total = message if total is None else total + message
+            bond_gate = (1.0 + gate[2 * channels :]) * live
+            if last:
+                gate_out[b, j] = bond_gate.astype(BF)
+            else:
+                bonds_out[b, j] = bond_update(bond_t[...], angular_ref[b, j], bond, bond_gate)
+        if group < slots // BATCH - 1:
             msg_s[...] = total
-
-        groups = slots // BATCH
-        gather(0)
-        for group in range(1, groups):
-            gather(group)
-            gates(group - 1)
-        gates(groups - 1)
-        summed = (msg_s[...] * (0.5 / count.astype(F32))).astype(BF)
+            return
+        summed = (total * (0.5 / count.astype(F32))).astype(BF)
         state = state_ref[:, block_lanes(base) if first else here]
         state = state + jnp.dot(atom_t[...], summed, preferred_element_type=F32)
         state_out[:, here] = state
@@ -145,9 +141,13 @@
             energy_out[...] += jnp.sum(state * energy_w, axis=0, keepdims=True)
         else:
             table_out[:, here] = state.astype(BF)
-        return carry
-
-    lax.fori_loop(0, per, block, 0)
+
+    work = [(b, group) for b in range(per) for group in range(slots // BATCH)]
+    gather(*work[0])
+    for now, before in zip(work[1:], work[:-1]):
+        gather(*now)
+        gates(*before)
+    gates(*work[-1])
 
 
 def run_gather(layer, tables, state, bonds, offs, counts, weights, extra):
@@ -178,7 +178,7 @@
             pltpu.VMEM((3 * channels, 3 * channels), BF),
             pltpu.VMEM((channels, channels), BF),
             pltpu.VMEM((channels, channels), BF),
-            pltpu.VMEM((slots, channels, LANES), BF),
+            pltpu.VMEM((2, BATCH, channels, LANES), BF),
             pltpu.VMEM((channels, LANES), F32),
         ],
         compiler_params=PARAMS,
@@ -256,12 +256,12 @@
     )(bonds, counts, cosines, *weights)
 
 
-def update_kernel(layer, slots, channels, parts, *refs):
+def update_kernel(layer, start, slots, channels, parts, *refs):
     angular_refs = refs[:parts]
-    bond_ref, gate_ref, wbond_ref, bonds_out, bond_t, done, sems = refs[parts:]
+    bond_ref, gate_ref, wbond_ref, _, bonds_out, bond_t, done, sems = refs[parts:]
     bond_t[...] = (wbond_ref[layer].astype(F32).T * 0.5).astype(BF)
     copies = []
-    b = 0
+    b = start
     for angular_ref in angular_refs:
         for step in range(angular_ref.shape[0]):
             for pair in range(slots // 2):
@@ -270,9 +270,9 @@
                     for j in (2 * pair, 2 * pair + 1)
                 ]
                 both = jnp.concatenate(both, axis=0).astype(F32).T.astype(BF)
-                done[b, :, pair * 2 * channels : (pair + 1) * 2 * channels] = both
+                done[b - start, :, pair * 2 * channels : (pair + 1) * 2 * channels] = both
             copies.append(
-                pltpu.make_async_copy(done.at[b], bonds_out.at[pl.ds(b * LANES, LANES)], sems.at[b])
+                pltpu.make_async_copy(done.at[b - start], bonds_out.at[pl.ds(b * LANES, LANES)], sems.at[b - start])
             )
             copies[-1].start()
             b += 1
@@ -280,13 +280,15 @@
         copy.wait()
 
 
-def run_update(layer, angulars, bonds, gates, weight):
+def run_update(layer, start, buffer, angulars, bonds, gates, weight):
     per, slots, channels, _ = bonds.shape
+    parts = len(angulars)
     return pl.pallas_call(
-        functools.partial(update_kernel, layer, slots, channels, len(angulars)),
+        functools.partial(update_kernel, layer, start, slots, channels, parts),
         out_shape=jax.ShapeDtypeStruct((per * LANES, slots * channels), BF),
-        in_specs=[VMEM] * (len(angulars) + 3),
+        in_specs=[VMEM] * (parts + 3) + [ANY],
         out_specs=ANY,
+        input_output_aliases={} if buffer is None else {parts + 3: 0},
         scratch_shapes=[
             pltpu.VMEM((channels, channels), BF),
             pltpu.VMEM((per, LANES, slots * channels), BF),
@@ -294,7 +296,7 @@
         ],
         compiler_params=PARAMS,
         cost_estimate=pl.CostEstimate(flops=2**30, bytes_accessed=2**23, transcendentals=0),
-    )(*angulars, bonds, gates, weight)
+    )(*angulars, bonds, gates, weight, weight if buffer is None else buffer)
 
 
 def passed_along(value, steps):
@@ -328,18 +330,15 @@
 
 
 def sum_stages():
-    rep, space = lax.axis_size("rep"), lax.axis_size("space")
-
-    def over_rep(value):
-        moved = [
-            lax.ppermute(value, "rep", [(i, (i + s) % rep) for i in range(rep)]) for s in range(1, rep)
-        ]
-        return sum(moved, value)
-
-    def over_space(step):
-        return lambda value: value + lax.ppermute(value, "space", [(i, i ^ step) for i in range(space)])
-
-    return [over_rep] + [over_space(1 << s) for s in range(space.bit_length() - 1)]
+    def exchange(axis, step):
+        size = lax.axis_size(axis)
+        return lambda value: value + lax.ppermute(value, axis, [(i, i ^ step) for i in range(size)])
+
+    return [
+        exchange(axis, 1 << bit)
+        for axis in ("rep", "space")
+        for bit in range(lax.axis_size(axis).bit_length() - 1)
+    ]
 
 
 def per_device(
@@ -379,9 +378,12 @@
         if stages:
             energy = stages.pop(0)(energy)
         angulars += run_angle(1, part, 1, bonds, cnts, tiles, into_angles, shape)
-    if stages:
-        energy = stages.pop(0)(energy)
-    out = run_update(1, angulars, bonds, gates, weight_bond)
+    out = None
+    for part in range(2):
+        if stages:
+            energy = stages.pop(0)(energy)
+        mine = angulars[:1] if part == 0 else angulars[1:]
+        out = run_update(1, part * half, out, mine, bonds, gates, weight_bond)
     for stage in stages:
         energy = stage(energy)
     scale = math.sqrt(lax.axis_size("space") * domain.shape[1])

time: 82.1 us -> 79.6 us (0.970)
  starting transfers between devices: 19.9 us -> 11.2 us
  waiting for transfers between devices: 2.3 us -> 8.83 us
    ppermute x6 -> x5, starting transfers between devices: 6.96 us -> 1.19 us  [exchange(): lax.ppermute(value, axis, [(i, i ^ step) for i in range(size)])]
    ppermute x6 -> x5, waiting for transfers between devices: 2.29 us -> 5.74 us  [exchange(): lax.ppermute(value, axis, [(i, i ^ step) for i in range(size)])]
    ppermute x4, waiting for transfers between devices: 0.01 us -> 3.08 us  [passed_along(): lax.ppermute(value, AXES, [(source, (source + steps) % count) for source...]
    ppermute x4, starting transfers between devices: 9.96 us -> 6.98 us  [passed_along(): lax.ppermute(value, AXES, [(source, (source + steps) % count) for source...]
    pallas_call x2, Pallas kernels: 28 us -> 26.8 us  [run_gather(): pl.pallas_call(functools.partial(gather_kernel, layer, first, last, slots...]
    pallas_call x1 -> x2, Pallas kernels: 2.31 us -> 3.2 us  [run_update(): pl.pallas_call(functools.partial(update_kernel, layer, start, slots, chan...]
  transfers between devices with their start and end apart: 11 -> 10, of which waited for: 4 -> 7; matrix products, arithmetic and copies ran while one was open for 0% -> 0% of each run, Pallas kernels for 33% -> 35%
where the time goes in v5:
time: 79.6 us; the launch traced here: 79.4 us
  Pallas kernels  54.9 us (69%)
  starting transfers between devices  11.2 us (14%)
  waiting for transfers between devices  8.83 us (11%)
  between operations  2.6 us (3%)
  local copies, waits for them, and re-layouts  1.27 us (2%)
    pallas_call x2, Pallas kernels, run_gather(): pl.pallas_call(functools.partial(gather_kernel, layer, first, last, slots...  26.8 us
    pallas_call x4, Pallas kernels, run_angle(): pl.pallas_call(functools.partial(angle_kernel, layer, first, start, steps...  24.9 us
    ppermute x4, starting transfers between devices, passed_along(): lax.ppermute(value, AXES, [(source, (source + steps) % count) for source...  6.98 us
    ppermute x5, waiting for transfers between devices, exchange(): lax.ppermute(value, axis, [(i, i ^ step) for i in range(size)])  5.74 us
    pallas_call x2, Pallas kernels, run_update(): pl.pallas_call(functools.partial(update_kernel, layer, start, slots, chan...  3.2 us
    ppermute x4, waiting for transfers between devices, passed_along(): lax.ppermute(value, AXES, [(source, (source + steps) % count) for source...  3.08 us
    ppermute x1, starting transfers between devices, far_side(): return lax.ppermute(payload, AXES, pairs)  2.99 us
  transfers between devices with their start and end apart: 10, of which 7 were waited for; matrix products, arithmetic and copies ran while one was open for 0% of the time, Pallas kernels for 35%

profile of v5, /device:TPU:0, one launch (start us, length us, event | category | flops | bytes accessed | tf_op | source)
XLA Modules:
  0.0 79.4 jit_solution(13319567400799072728)
XLA Ops:
  0.6 0.0 copy-start.3
  0.6 1.2 %copy-done.3 = f32[4096,64]{0,1:T(8,128)S(1)} copy-done((f32[4096,64]{0,1:T(8,128)S(1)}, f32[4096,64]{0,1:T(8,128)}, u32[]{:S(2)}) %copy-start.3) | copy-done | bytes 1048600
  1.9 0.0 copy-start.1
  1.9 0.0 copy-start.2
  1.9 0.0 copy-start.7
  1.9 0.0 copy-start.8
  1.9 0.0 copy-start.9
  1.9 3.0 %collective-permute-start = (bf16[64,2048]{1,0:T(8,128)(2,1)S(1)}, bf16[64,2048]{1,0:T(8,128)(2,1)S(1)}, u32[]{:S(2)}, u32[]{:S(2)}) collective-permute-start(bf16[64,2048]{1,0:T(8,128)(2,1)S(1)} %shard_map.130), channel_id=1, source_target_pairs={{28,0},{29,1},{6,2},{7,3},{0,4},{1,5},{10,6},{11,7},{4,8},{5,9},{1... | collective-permute-start | bytes 786440 | tf_op jit(solution)/shard_map/ppermute | solution.py:329
  4.9 0.0 copy-done.1
  4.9 0.0 copy-done.2
  4.9 0.0 copy-done.7
  4.9 0.0 copy-done.8
  4.9 0.0 copy-done.9
  4.9 0.0 copy-start
  5.0 0.0 copy-start.4
  5.0 0.0 copy-start.5
  5.0 0.0 copy-start.6
  5.0 12.6 %shard_map.131 = (bf16[4,16,64,256]{3,2,1,0:T(8,128)(2,1)S(1)}, bf16[4,16,64,256]{3,2,1,0:T(8,128)(2,1)S(1)}, f32[4,256,256]{2,1,0:T(8,128)S(1)}) custom-call(bf16[1024,1024]{1,0:T(8,128)(2,1)S(1)} %copy-done.1, s32[1,1024]{1,0:T(1,128)S(1)} %bitcast.9, f32[1024,256]{1,0:T(8,128)S(1)} %copy-done.2, bf16[2,64,128]{2,1,0:T(8,128)(2,1)S(1)} %copy-done.7, ...), custom_call_target="tpu_custom_call" | custom-call | flops 4294967296 | bytes 8388608 | tf_op jit(solution)/shard_map/pallas_call | solution.py:248
  17.6 0.0 collective-permute-done.refs_1_
  17.6 0.0 copy-done
  17.6 0.0 copy-done.4
  17.6 0.0 copy-done.5
  17.6 0.0 copy-done.6
  17.7 13.7 %shard_map.132 = (f32[64,1024]{1,0:T(8,128)S(1)}, bf16[64,1024]{1,0:T(8,128)(2,1)S(1)}, bf16[4,16,64,256]{3,2,1,0:T(8,128)(2,1)S(1)}) custom-call(f32[64,4096]{1,0:T(8,128)S(1)} %bitcast.6, bf16[64,2048]{1,0:T(8,128)(2,1)S(1)} %collective-permute-done.refs_1_, bf16[4,16,64,256]{3,2,1,0:T(8,128)(2,1)S(1)} %get-tuple-element.12.refs_2_, ...), custom_call_target="tpu_custom_call" | custom-call | flops 10737418240 | bytes 8388608 | tf_op jit(solution)/shard_map/pallas_call | solution.py:171
  31.3 5.8 %collective-permute-start.4 = (bf16[64,1024]{1,0:T(8,128)(2,1)S(1)}, bf16[64,1024]{1,0:T(8,128)(2,1)S(1)}, u32[]{:S(2)}, u32[]{:S(2)}) collective-permute-start(bf16[64,1024]{1,0:T(8,128)(2,1)S(1)} %get-tuple-element.14.refs_2_), channel_id=1, source_target_pairs={{0,30},{1,31},{2,0},{3,1},{4,2},{5,3},{6,4},{7,5},{8,6},{9,7},{10,... | collective-permute-start | bytes 393224 | tf_op jit(solution)/shard_map/ppermute | solution.py:304
  37.1 0.0 collective-permute-start.3
  37.1 0.5 collective-permute-start.2
  37.6 0.7 collective-permute-start.1
  38.3 0.0 copy-start.10
  38.3 6.2 %shard_map.133.refs_12_.refs_0_ = bf16[2,16,64,256]{3,2,1,0:T(8,128)(2,1)S(1)} custom-call(bf16[4,16,64,256]{3,2,1,0:T(8,128)(2,1)S(1)} %get-tuple-element.16.refs_0_.refs_6_.refs_1_.refs_2_, s32[1,1024]{1,0:T(1,128)S(1)} %bitcast.11, f32[4,256,256]{2,1,0:T(8,128)S(1)} %get-tuple-element.17.refs_2_, bf16[2,64,128]{2,1,0:T(8,128)(2,1)S(1)} %copy-done.7, ...), custom_call_target="tpu_custom_call" | custom-call | flops 2147483648 | bytes 4194304 | tf_op jit(solution)/shard_map/pallas_call | solution.py:248
  44.5 0.0 collective-permute-done.4.refs_4_
  44.5 0.0 collective-permute-done.3.refs_3_
  44.5 0.9 %collective-permute-done.2.refs_1_ = bf16[64,1024]{1,0:T(8,128)(2,1)S(1)} collective-permute-done((bf16[64,1024]{1,0:T(8,128)(2,1)S(1)}, bf16[64,1024]{1,0:T(8,128)(2,1)S(1)}, u32[]{:S(2)}, u32[]{:S(2)}) %collective-permute-start.2) | collective-permute-done | bytes 131104 | tf_op jit(solution)/shard_map/ppermute | solution.py:304
  45.4 2.2 %collective-permute-done.1.refs_0_ = bf16[64,1024]{1,0:T(8,128)(2,1)S(1)} collective-permute-done((bf16[64,1024]{1,0:T(8,128)(2,1)S(1)}, bf16[64,1024]{1,0:T(8,128)(2,1)S(1)}, u32[]{:S(2)}, u32[]{:S(2)}) %collective-permute-start.1) | collective-permute-done | bytes 131104 | tf_op jit(solution)/shard_map/ppermute | solution.py:304
  47.6 0.0 copy-done.10
  47.6 13.1 %shard_map.134 = (f32[64,1024]{1,0:T(8,128)}, bf16[4,16,64,256]{3,2,1,0:T(8,128)(2,1)S(1)}, f32[1,256]{1,0:T(1,128)S(1)}) custom-call(bf16[64,1024]{1,0:T(8,128)(2,1)S(1)} %collective-permute-done.1.refs_0_, bf16[64,1024]{1,0:T(8,128)(2,1)S(1)} %collective-permute-done.2.refs_1_, bf16[64,1024]{1,0:T(8,128)(2,1)S(1)} %get-tuple-element.14.refs_2_, ...), custom_call_target="tpu_custom_call" | custom-call | flops 10737418240 | bytes 8388608 | tf_op jit(solution)/shard_map/pallas_call | solution.py:171
  60.7 0.1 collective-permute-start.5
  60.8 1.0 %collective-permute-done.5 = f32[1,256]{1,0:T(1,128)S(1)} collective-permute-done((f32[1,256]{1,0:T(1,128)S(1)}, f32[1,256]{1,0:T(1,128)S(1)}, u32[]{:S(2)}, u32[]{:S(2)}) %collective-permute-start.5) | collective-permute-done | bytes 1056 | tf_op jit(solution)/shard_map/ppermute | solution.py:335
  61.8 0.0 collective-permute-start.6
  61.8 3.1 %shard_map.136.refs_1_ = bf16[1,16,64,256]{3,2,1,0:T(8,128)(2,1)S(1)} custom-call(bf16[4,16,64,256]{3,2,1,0:T(8,128)(2,1)S(1)} %get-tuple-element.16.refs_0_.refs_6_.refs_1_.refs_2_, s32[1,1024]{1,0:T(1,128)S(1)} %bitcast.13, f32[4,256,256]{2,1,0:T(8,128)S(1)} %get-tuple-element.17.refs_2_, bf16[2,64,128]{2,1,0:T(8,128)(2,1)S(1)} %copy-done.7, ...), custom_call_target="tpu_custom_call" | custom-call | flops 1073741824 | bytes 2097152 | tf_op jit(solution)/shard_map/pallas_call | solution.py:248
  64.9 0.5 collective-permute-done.6
  65.4 0.0 collective-permute-start.7
  65.4 3.1 %shard_map.135.refs_0_ = bf16[1,16,64,256]{3,2,1,0:T(8,128)(2,1)S(1)} custom-call(bf16[4,16,64,256]{3,2,1,0:T(8,128)(2,1)S(1)} %get-tuple-element.16.refs_0_.refs_6_.refs_1_.refs_2_, s32[1,1024]{1,0:T(1,128)S(1)} %bitcast.14, f32[4,256,256]{2,1,0:T(8,128)S(1)} %get-tuple-element.17.refs_2_, bf16[2,64,128]{2,1,0:T(8,128)(2,1)S(1)} %copy-done.7, ...), custom_call_target="tpu_custom_call" | custom-call | flops 1073741824 | bytes 2097152 | tf_op jit(solution)/shard_map/pallas_call | solution.py:248
  68.5 0.5 collective-permute-done.7
  69.0 0.0 collective-permute-start.8
  69.0 1.6 %shard_map.137.refs_5_ = bf16[1024,1024]{1,0:T(8,128)(2,1)} custom-call(bf16[2,16,64,256]{3,2,1,0:T(8,128)(2,1)S(1)} %shard_map.133.refs_12_.refs_0_, bf16[4,16,64,256]{3,2,1,0:T(8,128)(2,1)S(1)} %get-tuple-element.16.refs_0_.refs_6_.refs_1_.refs_2_, bf16[4,16,64,256]{3,2,1,0:T(8,128)(2,1)S(1)} %get-tuple-element.19.refs_2_.refs_3_, ...), custom_call_target="tpu_custom_call" | custom-call | flops 1073741824 | bytes 8388608 | tf_op jit(solution)/shard_map/pallas_call | solution.py:286
  70.6 2.0 %collective-permute-done.8 = f32[1,256]{1,0:T(1,128)S(1)} collective-permute-done((f32[1,256]{1,0:T(1,128)S(1)}, f32[1,256]{1,0:T(1,128)S(1)}, u32[]{:S(2)}, u32[]{:S(2)}) %collective-permute-start.8) | collective-permute-done | bytes 1056 | tf_op jit(solution)/shard_map/ppermute | solution.py:335
  72.6 1.1 %collective-permute-start.9 = (f32[1,256]{1,0:T(1,128)S(1)}, f32[1,256]{1,0:T(1,128)S(1)}, u32[]{:S(2)}, u32[]{:S(2)}) collective-permute-start(f32[1,256]{1,0:T(1,128)S(1)} %add.18), channel_id=1, source_target_pairs={{0,16},{4,20},{8,24},{12,28},{16,0},{20,4},{24,8},{28,12},{1,17},{... | collective-permute-start | bytes 3080 | tf_op jit(solution)/shard_map/ppermute | solution.py:335
  73.6 1.6 %shard_map.138 = bf16[1024,1024]{1,0:T(8,128)(2,1)} custom-call(bf16[1,16,64,256]{3,2,1,0:T(8,128)(2,1)S(1)} %shard_map.135.refs_0_, bf16[1,16,64,256]{3,2,1,0:T(8,128)(2,1)S(1)} %shard_map.136.refs_1_, bf16[4,16,64,256]{3,2,1,0:T(8,128)(2,1)S(1)} %get-tuple-element.16.refs_0_.refs_6_.refs_1_.refs_2_, ...), custom_call_target="tpu_custom_call", output_to_operand_aliasing={{}: (5, {})} | custom-call | flops 1073741824 | bytes 8388608 | tf_op jit(solution)/shard_map/pallas_call | solution.py:286
  75.2 1.8 %collective-permute-done.9 = f32[1,256]{1,0:T(1,128)S(1)} collective-permute-done((f32[1,256]{1,0:T(1,128)S(1)}, f32[1,256]{1,0:T(1,128)S(1)}, u32[]{:S(2)}, u32[]{:S(2)}) %collective-permute-start.9) | collective-permute-done | bytes 1056 | tf_op jit(solution)/shard_map/ppermute | solution.py:335
  77.0 0.6 add_reduce_fusion
  (5 shorter events, 0.1 us)
Async XLA Ops:
  0.6 1.2 %copy-start.3 = (f32[4096,64]{0,1:T(8,128)S(1)}, f32[4096,64]{0,1:T(8,128)}, u32[]{:S(2)}) copy-start(f32[4096,64]{0,1:T(8,128)} %param.11) | copy-start | bytes 3145732
  1.9 3.1 %copy-start.1 = (bf16[1024,1024]{1,0:T(8,128)(2,1)S(1)}, bf16[1024,1024]{1,0:T(8,128)(2,1)}, u32[]{:S(2)}) copy-start(bf16[1024,1024]{1,0:T(8,128)(2,1)} %refs_0_.1) | copy-start | bytes 6291460
  1.9 3.1 %copy-start.2 = (f32[1024,256]{1,0:T(8,128)S(1)}, f32[1024,256]{1,0:T(8,128)}, u32[]{:S(2)}) copy-start(f32[1024,256]{1,0:T(8,128)} %refs_2_.1) | copy-start | bytes 3145732
  1.9 3.1 %copy-start.7 = (bf16[2,64,128]{2,1,0:T(8,128)(2,1)S(1)}, bf16[2,64,128]{2,1,0:T(8,128)(2,1)}, u32[]{:S(2)}) copy-start(bf16[2,64,128]{2,1,0:T(8,128)(2,1)} %refs_3_.8) | copy-start | bytes 98308
  1.9 3.1 %copy-start.8 = (s32[1024]{0:T(1024)S(1)}, s32[1024]{0:T(1024)}, u32[]{:S(2)}) copy-start(s32[1024]{0:T(1024)} %param.14) | copy-start | bytes 12292
  1.9 3.1 %copy-start.9 = (f32[2,64]{1,0:T(2,128)S(1)}, f32[2,64]{1,0:T(2,128)}, u32[]{:S(2)}) copy-start(f32[2,64]{1,0:T(2,128)} %refs_4_.9) | copy-start | bytes 1540
  1.9 15.7 %collective-permute-start = (bf16[64,2048]{1,0:T(8,128)(2,1)S(1)}, bf16[64,2048]{1,0:T(8,128)(2,1)S(1)}, u32[]{:S(2)}, u32[]{:S(2)}) collective-permute-start(bf16[64,2048]{1,0:T(8,128)(2,1)S(1)} %shard_map.130), channel_id=1, source_target_pairs={{28,0},{29,1},{6,2},{7,3},{0,4},{1,5},{10,6},{11,7},{4,8},{5,9},{1... | collective-permute-start | bytes 786440 | tf_op jit(solution)/shard_map/ppermute | solution.py:329
  4.9 12.7 %copy-start = (bf16[2,64,64]{2,1,0:T(8,128)(2,1)S(1)}, bf16[2,64,64]{2,1,0:T(8,128)(2,1)}, u32[]{:S(2)}) copy-start(bf16[2,64,64]{2,1,0:T(8,128)(2,1)} %refs_4_.11) | copy-start | bytes 49156
  5.0 12.7 %copy-start.4 = (bf16[2,192,192]{2,1,0:T(8,128)(2,1)S(1)}, bf16[2,192,192]{2,1,0:T(8,128)(2,1)}, u32[]{:S(2)}) copy-start(bf16[2,192,192]{2,1,0:T(8,128)(2,1)} %refs_9_.1) | copy-start | bytes 442372
  5.0 12.7 %copy-start.5 = (s32[1024,16]{0,1:T(8,128)S(1)}, s32[1024,16]{0,1:T(8,128)}, u32[]{:S(2)}) copy-start(s32[1024,16]{0,1:T(8,128)} %param.13) | copy-start | bytes 196612
  5.0 12.7 %copy-start.6 = (bf16[2,64,64]{2,1,0:T(8,128)(2,1)S(1)}, bf16[2,64,64]{2,1,0:T(8,128)(2,1)}, u32[]{:S(2)}) copy-start(bf16[2,64,64]{2,1,0:T(8,128)(2,1)} %refs_10_.1) | copy-start | bytes 49156
  31.3 13.2 %collective-permute-start.4 = (bf16[64,1024]{1,0:T(8,128)(2,1)S(1)}, bf16[64,1024]{1,0:T(8,128)(2,1)S(1)}, u32[]{:S(2)}, u32[]{:S(2)}) collective-permute-start(bf16[64,1024]{1,0:T(8,128)(2,1)S(1)} %get-tuple-element.14.refs_2_), channel_id=1, source_target_pairs={{0,30},{1,31},{2,0},{3,1},{4,2},{5,3},{6,4},{7,5},{8,6},{9,7},{10,... | collective-permute-start | bytes 393224 | tf_op jit(solution)/shard_map/ppermute | solution.py:304
  37.1 7.4 %collective-permute-start.3 = (bf16[64,1024]{1,0:T(8,128)(2,1)S(1)}, bf16[64,1024]{1,0:T(8,128)(2,1)S(1)}, u32[]{:S(2)}, u32[]{:S(2)}) collective-permute-start(bf16[64,1024]{1,0:T(8,128)(2,1)S(1)} %get-tuple-element.14.refs_2_), channel_id=1, source_target_pairs={{0,31},{1,0},{2,1},{3,2},{4,3},{5,4},{6,5},{7,6},{8,7},{9,8},{10,9... | collective-permute-start | bytes 393224 | tf_op jit(solution)/shard_map/ppermute | solution.py:304
  37.1 8.3 %collective-permute-start.2 = (bf16[64,1024]{1,0:T(8,128)(2,1)S(1)}, bf16[64,1024]{1,0:T(8,128)(2,1)S(1)}, u32[]{:S(2)}, u32[]{:S(2)}) collective-permute-start(bf16[64,1024]{1,0:T(8,128)(2,1)S(1)} %get-tuple-element.14.refs_2_), channel_id=1, source_target_pairs={{0,1},{1,2},{2,3},{3,4},{4,5},{5,6},{6,7},{7,8},{8,9},{9,10},{10,1... | collective-permute-start | bytes 393224 | tf_op jit(solution)/shard_map/ppermute | solution.py:304
  37.6 10.0 %collective-permute-start.1 = (bf16[64,1024]{1,0:T(8,128)(2,1)S(1)}, bf16[64,1024]{1,0:T(8,128)(2,1)S(1)}, u32[]{:S(2)}, u32[]{:S(2)}) collective-permute-start(bf16[64,1024]{1,0:T(8,128)(2,1)S(1)} %get-tuple-element.14.refs_2_), channel_id=1, source_target_pairs={{0,2},{1,3},{2,4},{3,5},{4,6},{5,7},{6,8},{7,9},{8,10},{9,11},{10,... | collective-permute-start | bytes 393224 | tf_op jit(solution)/shard_map/ppermute | solution.py:304
  38.3 9.3 %copy-start.10 = (f32[64]{0:T(128)S(1)}, f32[64]{0:T(128)}, u32[]{:S(2)}) copy-start(f32[64]{0:T(128)} %param.21) | copy-start | bytes 772
  60.7 1.1 %collective-permute-start.5 = (f32[1,256]{1,0:T(1,128)S(1)}, f32[1,256]{1,0:T(1,128)S(1)}, u32[]{:S(2)}, u32[]{:S(2)}) collective-permute-start(f32[1,256]{1,0:T(1,128)S(1)} %get-tuple-element.20), channel_id=1, source_target_pairs={{0,1},{1,0},{2,3},{3,2},{4,5},{5,4},{6,7},{7,6},{8,9},{9,8},{10,11... | collective-permute-start | bytes 3080 | tf_op jit(solution)/shard_map/ppermute | solution.py:335
  61.8 3.6 %collective-permute-start.6 = (f32[1,256]{1,0:T(1,128)S(1)}, f32[1,256]{1,0:T(1,128)S(1)}, u32[]{:S(2)}, u32[]{:S(2)}) collective-permute-start(f32[1,256]{1,0:T(1,128)S(1)} %add.15), channel_id=1, source_target_pairs={{0,2},{1,3},{2,0},{3,1},{4,6},{5,7},{6,4},{7,5},{8,10},{9,11},{10,... | collective-permute-start | bytes 3080 | tf_op jit(solution)/shard_map/ppermute | solution.py:335
  65.4 3.6 %collective-permute-start.7 = (f32[1,256]{1,0:T(1,128)S(1)}, f32[1,256]{1,0:T(1,128)S(1)}, u32[]{:S(2)}, u32[]{:S(2)}) collective-permute-start(f32[1,256]{1,0:T(1,128)S(1)} %add.16), channel_id=1, source_target_pairs={{0,4},{4,0},{8,12},{12,8},{16,20},{20,16},{24,28},{28,24},{1,5},{5... | collective-permute-start | bytes 3080 | tf_op jit(solution)/shard_map/ppermute | solution.py:335
  69.0 3.6 %collective-permute-start.8 = (f32[1,256]{1,0:T(1,128)S(1)}, f32[1,256]{1,0:T(1,128)S(1)}, u32[]{:S(2)}, u32[]{:S(2)}) collective-permute-start(f32[1,256]{1,0:T(1,128)S(1)} %add.17), channel_id=1, source_target_pairs={{0,8},{4,12},{8,0},{12,4},{16,24},{20,28},{24,16},{28,20},{1,9},{5... | collective-permute-start | bytes 3080 | tf_op jit(solution)/shard_map/ppermute | solution.py:335
  72.6 4.5 %collective-permute-start.9 = (f32[1,256]{1,0:T(1,128)S(1)}, f32[1,256]{1,0:T(1,128)S(1)}, u32[]{:S(2)}, u32[]{:S(2)}) collective-permute-start(f32[1,256]{1,0:T(1,128)S(1)} %add.18), channel_id=1, source_target_pairs={{0,16},{4,20},{8,24},{12,28},{16,0},{20,4},{24,8},{28,12},{1,17},{... | collective-permute-start | bytes 3080 | tf_op jit(solution)/shard_map/ppermute | solution.py:335

commit v6 on v5

--- a/solution.py
+++ b/solution.py
@@ -12,6 +12,8 @@
 LANES = 256
 DEAD = -1e30
 BATCH = 4
+EARLY = 3
+HIDING = 2
 BF = jnp.bfloat16
 F32 = jnp.float32
 AXES = ("space", "rep")
@@ -38,6 +40,23 @@
 def bond_update(weight, angular, bond, gate):
     change = jnp.dot(weight, angular, preferred_element_type=F32)
     return (bond.astype(F32) + change * gate).astype(BF)
+
+
+def project(pair_t, bond, live):
+    channels = bond.shape[0]
+    both = jnp.dot(pair_t, bond, preferred_element_type=F32)
+    return both[:channels].astype(BF), jnp.where(live, both[channels:], DEAD).astype(BF)
+
+
+def angle_sum(p, queries, cosine_row, wc, j, slots, inverse):
+    stack = []
+    for m in range(1, slots):
+        k = (j + m) % slots
+        cosine = jnp.broadcast_to(cosine_row(k), (8, LANES)).astype(BF)
+        cosine = jnp.concatenate([cosine] * (p.shape[0] // 8), axis=0)
+        y = p + (queries(k) + cosine * wc[...])
+        tree_push(stack, y + y * jnp.tanh(y))
+    return (tree_total(stack).astype(F32) * inverse).astype(BF)
 
 
 def block_lanes(b):
@@ -62,21 +81,22 @@
         energy_w_ref = refs.pop(0)
         refs.pop(0)
     else:
-        angular_ref, wbond_ref = refs[:2]
-        refs = refs[2:]
-    state_out = refs.pop(0)
+        wcos_ref, cos_ref, p_ref, q_ref = refs[:4]
+        refs = refs[4:]
+        early = bond_ref.shape[0] - p_ref.shape[0]
+    state_out, gate_out, third_out = refs[:3]
+    refs = refs[3:]
+    if not last:
+        late = refs.pop(0)
     if last:
-        gate_out, energy_out = refs[:2]
+        energy_out = third_out
         energy_out[...] = jnp.zeros_like(energy_out)
         energy_w = energy_w_ref[...].T
-    else:
-        table_out, bonds_out = refs[:2]
-    refs = refs[2:]
-    tab, core_t, atom_t, bond_t, n_s, msg_s = refs
+    tab, core_t, atom_t, n_s, msg_s, wc = refs
     core_t[...] = (core_ref[layer].astype(F32).T * 0.5).astype(BF)
     atom_t[...] = atom_ref[layer].astype(F32).T.astype(BF)
     if not last:
-        bond_t[...] = (wbond_ref[layer].astype(F32).T * 0.5).astype(BF)
+        wc[...] = jnp.broadcast_to((wcos_ref[layer : layer + 1] * 0.5).T, wc.shape).astype(BF)
     skip = lax.axis_index("rep") * per if first else 0
     if first:
         inner = state_ref.shape[1] // LANES
@@ -93,7 +113,20 @@
     columns = lax.broadcasted_iota(jnp.int32, (LANES, LANES), 0)
     lane = lax.broadcasted_iota(jnp.int32, (1, LANES), 1) + rim * LANES
 
-    def gather(b, group):
+    def late_angle(b, j):
+        inverse = 1.0 / cnt_ref[:, b * LANES : (b + 1) * LANES].astype(F32)
+        step = b - early
+        late[step, j] = angle_sum(
+            p_ref[step, j],
+            lambda k: q_ref[step, k],
+            lambda k: cos_ref[b, j * slots + k : j * slots + k + 1, :],
+            wc,
+            j,
+            slots,
+            inverse,
+        )
+
+    def gather(b, group, rows):
         base = skip + b
         here = slice(b * LANES, (b + 1) * LANES)
         for u in range(BATCH):
@@ -108,6 +141,8 @@
             for h in range(1, reach):
                 result = jnp.where(high == h, picked[h * channels : (h + 1) * channels], result)
             n_s[group % 2, u] = result.astype(BF)
+            for row in rows[u * len(rows) // BATCH : (u + 1) * len(rows) // BATCH]:
+                late_angle(*row)
 
     def gates(b, group):
         base = skip + b
@@ -126,10 +161,7 @@
             message = (1.0 + gate[:channels]) * (cores + cores * gate[channels : 2 * channels]) * live
             total = message if total is None else total + message
             bond_gate = (1.0 + gate[2 * channels :]) * live
-            if last:
-                gate_out[b, j] = bond_gate.astype(BF)
-            else:
-                bonds_out[b, j] = bond_update(bond_t[...], angular_ref[b, j], bond, bond_gate)
+            gate_out[b, j] = bond_gate.astype(BF)
         if group < slots // BATCH - 1:
             msg_s[...] = total
             return
@@ -140,13 +172,15 @@
         if last:
             energy_out[...] += jnp.sum(state * energy_w, axis=0, keepdims=True)
         else:
-            table_out[:, here] = state.astype(BF)
+            third_out[:, here] = state.astype(BF)
 
     work = [(b, group) for b in range(per) for group in range(slots // BATCH)]
-    gather(*work[0])
-    for now, before in zip(work[1:], work[:-1]):
-        gather(*now)
-        gates(*before)
+    rows = [] if last else [(b, j) for b in range(early, per) for j in range(slots)]
+    share = len(rows) // len(work)
+    gather(*work[0], rows[:share])
+    for at in range(1, len(work)):
+        gather(*work[at], rows[at * share : (at + 1) * share])
+        gates(*work[at - 1])
     gates(*work[-1])
 
 
@@ -166,7 +200,7 @@
         specs[-1] = ANY
         outs = [sds((channels, quarter), F32), slab, sds((1, LANES), F32)]
     else:
-        outs = [sds((channels, quarter), F32), sds((channels, quarter), BF), slab]
+        outs = [sds((channels, quarter), F32), slab, sds((channels, quarter), BF), sds(extra[-1].shape, BF)]
     rows = (tables[0].shape[1] // LANES + 4 * per) if first else 5 * per
     return pl.pallas_call(
         functools.partial(gather_kernel, layer, first, last, slots, channels, quarter),
@@ -177,63 +211,75 @@
             pltpu.VMEM((rows, channels, LANES), BF),
             pltpu.VMEM((3 * channels, 3 * channels), BF),
             pltpu.VMEM((channels, channels), BF),
-            pltpu.VMEM((channels, channels), BF),
             pltpu.VMEM((2, BATCH, channels, LANES), BF),
             pltpu.VMEM((channels, LANES), F32),
+            pltpu.VMEM((channels, LANES), BF),
         ],
         compiler_params=PARAMS,
         cost_estimate=pl.CostEstimate(flops=10 * 2**30, bytes_accessed=2**23, transcendentals=2**22),
     )(*operands)
 
 
-def angle_kernel(layer, first, start, steps, slots, channels, *refs):
-    bond_ref, cnt_ref, cos_ref, pair_ref, wcos_ref, angular_out = refs[:6]
-    refs = refs[6:]
+def angle_kernel(layer, first, start, steps, slots, channels, waits, *refs):
+    bond_ref, cnt_ref, cos_ref, pair_ref, wcos_ref = refs[:5]
+    angular_out = refs[5 + waits]
+    refs = refs[6 + waits :]
     if first:
-        bonds, cosines, pair_t, wc, p_s, q_s = refs
+        bonds, cosines, p_out, q_out, pair_t, wc, p_s, q_s = refs
     else:
         pair_t, wc, p_s, q_s = refs
         bonds, cosines = bond_ref, cos_ref
     pair_t[...] = (pair_ref[layer].astype(F32).T * 0.5).astype(BF)
     wc[...] = jnp.broadcast_to((wcos_ref[layer : layer + 1] * 0.5).T, wc.shape).astype(BF)
 
+    def turn(b):
+        rows = block_lanes(b)
+        cosines[b] = cos_ref[rows, :].T
+        for pair in range(slots // 2):
+            both = bond_ref[rows, pair * 2 * channels : (pair + 1) * 2 * channels].astype(F32).T.astype(BF)
+            bonds[b, 2 * pair] = both[:channels]
+            bonds[b, 2 * pair + 1] = both[channels:]
+
     def block(step, carry):
         b = start + step
         count = cnt_ref[:, block_lanes(b)]
         inverse = 1.0 / count.astype(F32)
         if first:
-            rows = block_lanes(b)
-            cosines[b] = cos_ref[rows, :].T
-            for pair in range(slots // 2):
-                both = bond_ref[rows, pair * 2 * channels : (pair + 1) * 2 * channels].astype(F32).T.astype(BF)
-                bonds[b, 2 * pair] = both[:channels]
-                bonds[b, 2 * pair + 1] = both[channels:]
+            turn(b)
 
         for k in range(slots):
-            both = jnp.dot(pair_t[...], bonds[b, k], preferred_element_type=F32)
-            p_s[k] = both[:channels].astype(BF)
-            q_s[k] = jnp.where(k < count, both[channels:], DEAD).astype(BF)
+            p_s[k], q_s[k] = project(pair_t[...], bonds[b, k], k < count)
 
         def slot(j, inner):
-            p = p_s[j]
-            stack = []
-            for m in range(1, slots):
-                k = (j + m) % slots
-                cosine = jnp.broadcast_to(cosines[b, pl.ds(j * slots + k, 1), :], (8, LANES)).astype(BF)
-                cosine = jnp.concatenate([cosine] * (channels // 8), axis=0)
-                y = p + (q_s[k] + cosine * wc[...])
-                tree_push(stack, y + y * jnp.tanh(y))
-            angular_out[step, j] = (tree_total(stack).astype(F32) * inverse).astype(BF)
+            angular_out[step, j] = angle_sum(
+                p_s[j],
+                lambda k: q_s[k],
+                lambda k: cosines[b, pl.ds(j * slots + k, 1), :],
+                wc,
+                j,
+                slots,
+                inverse,
+            )
             return inner
 
         lax.fori_loop(0, slots, slot, 0, unroll=2)
         return carry
 
     lax.fori_loop(0, steps, block, 0)
-
-
-def run_angle(layer, start, steps, bonds, counts, cosines, weights, shape):
-    first = layer == 0
+    if first:
+
+        def later(step, carry):
+            b = steps + step
+            turn(b)
+            count = cnt_ref[:, block_lanes(b)]
+            for k in range(slots):
+                p_out[step, k], q_out[step, k] = project(pair_t[...], bonds[b, k], k < count)
+            return carry
+
+        lax.fori_loop(0, p_out.shape[0], later, 0)
+
+
+def run_angle(layer, first, start, steps, bonds, counts, cosines, weights, shape, after=()):
     per, slots, channels, _ = shape
     sds = jax.ShapeDtypeStruct
     outs = [sds((steps, slots, channels, LANES), BF)]
@@ -244,16 +290,44 @@
         pltpu.VMEM((slots, channels, LANES), BF),
     ]
     if first:
-        outs += [sds(shape, BF), sds((per, slots * slots, LANES), F32)]
+        later = sds((per - steps, slots, channels, LANES), BF)
+        outs += [sds(shape, BF), sds((per, slots * slots, LANES), F32), later, later]
     return pl.pallas_call(
-        functools.partial(angle_kernel, layer, first, start, steps, slots, channels),
+        functools.partial(angle_kernel, layer, first, start, steps, slots, channels, len(after)),
         out_shape=outs,
-        in_specs=[VMEM] * 5,
+        in_specs=[VMEM] * 5 + [ANY] * len(after),
         out_specs=[VMEM] * len(outs),
         scratch_shapes=scratch,
         compiler_params=PARAMS,
         cost_estimate=pl.CostEstimate(flops=2**30 * steps, bytes_accessed=2**21 * steps, transcendentals=2**22 * steps),
-    )(bonds, counts, cosines, *weights)
+    )(bonds, counts, cosines, *weights, *after)
+
+
+def inner_update_kernel(layer, slots, parts, *refs):
+    bond_ref, gate_ref, wbond_ref, bonds_out, bond_t = refs[parts:]
+    bond_t[...] = (wbond_ref[layer].astype(F32).T * 0.5).astype(BF)
+    b = 0
+    for angular_ref in refs[:parts]:
+        for step in range(angular_ref.shape[0]):
+            for j in range(slots):
+                bonds_out[b, j] = bond_update(
+                    bond_t[...], angular_ref[step, j], bond_ref[b, j], gate_ref[b, j].astype(F32)
+                )
+            b += 1
+
+
+def run_inner_update(layer, angulars, bonds, gates, weight):
+    channels = bonds.shape[2]
+    parts = len(angulars)
+    return pl.pallas_call(
+        functools.partial(inner_update_kernel, layer, bonds.shape[1], parts),
+        out_shape=jax.ShapeDtypeStruct(bonds.shape, BF),
+        in_specs=[VMEM] * (parts + 3),
+        out_specs=VMEM,
+        scratch_shapes=[pltpu.VMEM((channels, channels), BF)],
+        compiler_params=PARAMS,
+        cost_estimate=pl.CostEstimate(flops=2**30, bytes_accessed=2**23, transcendentals=0),
+    )(*angulars, bonds, gates, weight)
 
 
 def update_kernel(layer, start, slots, channels, parts, *refs):
@@ -336,8 +410,8 @@
 
     return [
         exchange(axis, 1 << bit)
-        for axis in ("rep", "space")
-        for bit in range(lax.axis_size(axis).bit_length() - 1)
+        for axis in ("space", "rep")
+        for bit in reversed(range(lax.axis_size(axis).bit_length() - 1))
     ]
 
 
@@ -363,26 +437,27 @@
     into_angles = (weight_pair, weight_cosine)
     shape = (per, offsets.shape[1], domain.shape[0], LANES)
     far = far_side(domain, quarter)
-    angular, bonds, tiles = run_angle(0, 0, per, bond_features, cnts, cosines, into_angles, shape)
-    state, table, bonds = run_gather(
-        0, [domain, far], None, bonds, offs, cnts, into_atoms, [angular, weight_bond]
+    angular, bonds, tiles, later_p, later_q = run_angle(0, True, 0, EARLY, bond_features, cnts, cosines, into_angles, shape)
+    state, gates, table, late = run_gather(
+        0, [domain, far], None, bonds, offs, cnts, into_atoms, [weight_cosine, tiles, later_p, later_q]
     )
     pieces = [table if s == 0 else passed_along(table, s) for s in (2, 1, 0, -1, -2)]
-    half = per // 2
-    angulars = list(run_angle(1, 0, half, bonds, cnts, tiles, into_angles, shape))
+    bonds = run_inner_update(0, [angular, late], bonds, gates, weight_bond)
+    angulars = [run_angle(1, False, b, 1, bonds, cnts, tiles, into_angles, shape)[0] for b in range(HIDING)]
     state, gates, energy = run_gather(
-        1, pieces, state, bonds, offs, cnts, into_atoms, [weight_energy[None, :], angulars[0]]
+        1, pieces, state, bonds, offs, cnts, into_atoms, [weight_energy[None, :], angulars[-1]]
     )
     stages = sum_stages()
-    for part in range(half, per):
+    for part in range(HIDING, per):
         if stages:
             energy = stages.pop(0)(energy)
-        angulars += run_angle(1, part, 1, bonds, cnts, tiles, into_angles, shape)
+        angulars += run_angle(1, False, part, 1, bonds, cnts, tiles, into_angles, shape)
     out = None
+    half = per // 2
     for part in range(2):
         if stages:
             energy = stages.pop(0)(energy)
-        mine = angulars[:1] if part == 0 else angulars[1:]
+        mine = angulars[part * half : (part + 1) * half]
         out = run_update(1, part * half, out, mine, bonds, gates, weight_bond)
     for stage in stages:
         energy = stage(energy)

time: 79.6 us -> 78.6 us (0.987)
    pallas_call x4 -> x5, Pallas kernels: 24.9 us -> 22.3 us  [run_angle(): pl.pallas_call(functools.partial(angle_kernel, layer, first, start, steps...]
    ppermute x5, waiting for transfers between devices: 5.74 us -> 3.55 us  [exchange(): lax.ppermute(value, axis, [(i, i ^ step) for i in range(size)])]
    ppermute x4, waiting for transfers between devices: 3.08 us -> 5.16 us  [passed_along(): lax.ppermute(value, AXES, [(source, (source + steps) % count) for source...]
    pallas_call x2, Pallas kernels: 26.8 us -> 27.9 us  [run_gather(): pl.pallas_call(functools.partial(gather_kernel, layer, first, last, slots...]
    pallas_call x0 -> x1, Pallas kernels: none -> 0.99 us  [run_inner_update(): pl.pallas_call(functools.partial(inner_update_kernel, layer, bonds.shape[...]
  transfers between devices with their start and end apart: 10 -> 10, of which waited for: 7 -> 6; matrix products, arithmetic and copies ran while one was open for 0% -> 0% of each run, Pallas kernels for 35% -> 34%
where the time goes in v6:
time: 78.6 us; the launch traced here: 78.4 us
  Pallas kernels  54.4 us (69%)
  starting transfers between devices  10.8 us (14%)
  waiting for transfers between devices  8.72 us (11%)
  between operations  2.61 us (3%)
  local copies, waits for them, and re-layouts  1.27 us (2%)
    pallas_call x2, Pallas kernels, run_gather(): pl.pallas_call(functools.partial(gather_kernel, layer, first, last, slots...  27.9 us
    pallas_call x5, Pallas kernels, run_angle(): pl.pallas_call(functools.partial(angle_kernel, layer, first, start, steps...  22.3 us
    ppermute x4, starting transfers between devices, passed_along(): lax.ppermute(value, AXES, [(source, (source + steps) % count) for source...  6.96 us
    ppermute x4, waiting for transfers between devices, passed_along(): lax.ppermute(value, AXES, [(source, (source + steps) % count) for source...  5.16 us
    ppermute x5, waiting for transfers between devices, exchange(): lax.ppermute(value, axis, [(i, i ^ step) for i in range(size)])  3.55 us
    pallas_call x2, Pallas kernels, run_update(): pl.pallas_call(functools.partial(update_kernel, layer, start, slots, chan...  3.15 us
    ppermute x1, starting transfers between devices, far_side(): return lax.ppermute(payload, AXES, pairs)  2.99 us
  transfers between devices with their start and end apart: 10, of which 6 were waited for; matrix products, arithmetic and copies ran while one was open for 0% of the time, Pallas kernels for 34%

profile of v6, /device:TPU:0, one launch (start us, length us, event | category | flops | bytes accessed | tf_op | source)
XLA Modules:
  0.0 78.4 jit_solution(11540859518646976844)
XLA Ops:
  0.6 0.0 copy-start.3
  0.6 1.2 %copy-done.3 = f32[4096,64]{0,1:T(8,128)S(1)} copy-done((f32[4096,64]{0,1:T(8,128)S(1)}, f32[4096,64]{0,1:T(8,128)}, u32[]{:S(2)}) %copy-start.3) | copy-done | bytes 1048600
  1.9 0.0 copy-start.1
  1.9 0.0 copy-start.2
  1.9 0.0 copy-start.7
  1.9 0.0 copy-start.8
  1.9 0.0 copy-start.9
  1.9 3.0 %collective-permute-start = (bf16[64,2048]{1,0:T(8,128)(2,1)S(1)}, bf16[64,2048]{1,0:T(8,128)(2,1)S(1)}, u32[]{:S(2)}, u32[]{:S(2)}) collective-permute-start(bf16[64,2048]{1,0:T(8,128)(2,1)S(1)} %shard_map.130), channel_id=1, source_target_pairs={{28,0},{29,1},{6,2},{7,3},{0,4},{1,5},{10,6},{11,7},{4,8},{5,9},{1... | collective-permute-start | bytes 786440 | tf_op jit(solution)/shard_map/ppermute | solution.py:403
  4.9 0.0 copy-done.1
  4.9 0.0 copy-done.2
  4.9 0.0 copy-done.7
  4.9 0.0 copy-done.8
  4.9 0.0 copy-done.9
  4.9 0.0 copy-start.4
  5.0 0.0 copy-start.5
  5.0 0.0 copy-start.6
  5.0 10.0 %shard_map.131 = (bf16[3,16,64,256]{3,2,1,0:T(8,128)(2,1)S(1)}, bf16[4,16,64,256]{3,2,1,0:T(8,128)(2,1)S(1)}, f32[4,256,256]{2,1,0:T(8,128)S(1)}, bf16[1,16,64,2...) custom-call(bf16[1024,1024]{1,0:T(8,128)(2,1)S(1)} %copy-done.1, s32[1,1024]{1,0:T(1,128)S(1)} %bitcast.9, ...), custom_call_target="tpu_custom_call" | custom-call | flops 3221225472 | bytes 6291456 | tf_op jit(solution)/shard_map/pallas_call | solution.py:295
  15.0 0.0 collective-permute-done.refs_1_
  15.0 0.0 copy-done.4
  15.0 0.0 copy-done.5
  15.0 0.0 copy-done.6
  15.0 0.0 copy-start
  15.0 14.8 %shard_map.132 = (f32[64,1024]{1,0:T(8,128)S(1)}, bf16[4,16,64,256]{3,2,1,0:T(8,128)(2,1)S(1)}, bf16[64,1024]{1,0:T(8,128)(2,1)S(1)}, bf16[1,16,64,256]{3,2,1,0:T(8,128)(2,1)S(1)}) custom-call(f32[64,4096]{1,0:T(8,128)S(1)} %bitcast.6, bf16[64,2048]{1,0:T(8,128)(2,1)S(1)} %collective-permute-done.refs_1_, ...), custom_call_target="tpu_custom_call" | custom-call | flops 10737418240 | bytes 8388608 | tf_op jit(solution)/shard_map/pallas_call | solution.py:205
  29.9 5.8 %collective-permute-start.4 = (bf16[64,1024]{1,0:T(8,128)(2,1)S(1)}, bf16[64,1024]{1,0:T(8,128)(2,1)S(1)}, u32[]{:S(2)}, u32[]{:S(2)}) collective-permute-start(bf16[64,1024]{1,0:T(8,128)(2,1)S(1)} %get-tuple-element.19.refs_2_), channel_id=1, source_target_pairs={{0,30},{1,31},{2,0},{3,1},{4,2},{5,3},{6,4},{7,5},{8,6},{9,7},{10,... | collective-permute-start | bytes 393224 | tf_op jit(solution)/shard_map/ppermute | solution.py:378
  35.6 0.0 collective-permute-start.3
  35.6 0.5 collective-permute-start.2
  36.1 0.7 collective-permute-start.1
  36.8 0.0 copy-done
  36.9 1.0 %shard_map.133.refs_0_.refs_6_.refs_2_ = bf16[4,16,64,256]{3,2,1,0:T(8,128)(2,1)S(1)} custom-call(bf16[3,16,64,256]{3,2,1,0:T(8,128)(2,1)S(1)} %get-tuple-element.21.refs_0_, bf16[1,16,64,256]{3,2,1,0:T(8,128)(2,1)S(1)} %get-tuple-element.22.refs_1_, bf16[4,16,64,256]{3,2,1,0:T(8,128)(2,1)S(1)} %get-tuple-element.15.refs_2_, ...), custom_call_target="tpu_custom_call" | custom-call | flops 1073741824 | bytes 8388608 | tf_op jit(solution)/shard_map/pallas_call | solution.py:322
  37.9 0.0 copy-start.10
  37.9 3.1 %shard_map.134.refs_12_.refs_1_ = bf16[1,16,64,256]{3,2,1,0:T(8,128)(2,1)S(1)} custom-call(bf16[4,16,64,256]{3,2,1,0:T(8,128)(2,1)S(1)} %shard_map.133.refs_0_.refs_6_.refs_2_, s32[1,1024]{1,0:T(1,128)S(1)} %bitcast.11, f32[4,256,256]{2,1,0:T(8,128)S(1)} %get-tuple-element.16.refs_8_.refs_2_, bf16[2,64,128]{2,1,0:T(8,128)(2,1)S(1)} %copy-done.7, ...), custom_call_target="tpu_custom_call" | custom-call | flops 1073741824 | bytes 2097152 | tf_op jit(solution)/shard_map/pallas_call | solution.py:295
  40.9 0.0 collective-permute-done.4.refs_4_
  41.0 0.0 collective-permute-done.3.refs_3_
  41.0 3.0 %collective-permute-done.2.refs_1_ = bf16[64,1024]{1,0:T(8,128)(2,1)S(1)} collective-permute-done((bf16[64,1024]{1,0:T(8,128)(2,1)S(1)}, bf16[64,1024]{1,0:T(8,128)(2,1)S(1)}, u32[]{:S(2)}, u32[]{:S(2)}) %collective-permute-start.2) | collective-permute-done | bytes 131104 | tf_op jit(solution)/shard_map/ppermute | solution.py:378
  43.9 2.2 %collective-permute-done.1.refs_0_ = bf16[64,1024]{1,0:T(8,128)(2,1)S(1)} collective-permute-done((bf16[64,1024]{1,0:T(8,128)(2,1)S(1)}, bf16[64,1024]{1,0:T(8,128)(2,1)S(1)}, u32[]{:S(2)}, u32[]{:S(2)}) %collective-permute-start.1) | collective-permute-done | bytes 131104 | tf_op jit(solution)/shard_map/ppermute | solution.py:378
  46.1 0.0 copy-done.10
  46.1 13.1 %shard_map.135 = (f32[64,1024]{1,0:T(8,128)}, bf16[4,16,64,256]{3,2,1,0:T(8,128)(2,1)S(1)}, f32[1,256]{1,0:T(1,128)S(1)}) custom-call(bf16[64,1024]{1,0:T(8,128)(2,1)S(1)} %collective-permute-done.1.refs_0_, bf16[64,1024]{1,0:T(8,128)(2,1)S(1)} %collective-permute-done.2.refs_1_, bf16[64,1024]{1,0:T(8,128)(2,1)S(1)} %get-tuple-element.19.refs_2_, ...), custom_call_target="tpu_custom_call" | custom-call | flops 10737418240 | bytes 8388608 | tf_op jit(solution)/shard_map/pallas_call | solution.py:205
  59.2 0.0 collective-permute-start.5
  59.2 3.1 %shard_map.138.refs_0_ = bf16[1,16,64,256]{3,2,1,0:T(8,128)(2,1)S(1)} custom-call(bf16[4,16,64,256]{3,2,1,0:T(8,128)(2,1)S(1)} %shard_map.133.refs_0_.refs_6_.refs_2_, s32[1,1024]{1,0:T(1,128)S(1)} %bitcast.13, f32[4,256,256]{2,1,0:T(8,128)S(1)} %get-tuple-element.16.refs_8_.refs_2_, bf16[2,64,128]{2,1,0:T(8,128)(2,1)S(1)} %copy-done.7, f32[2,64]{1,0:T(2,128)S(1)} %copy-done.9), custom_call_target="tpu_custom_call" | custom-call | flops 1073741824 | bytes 2097152 | tf_op jit(solution)/shard_map/pallas_call | solution.py:295
  62.3 1.4 %collective-permute-done.5 = f32[1,256]{1,0:T(1,128)S(1)} collective-permute-done((f32[1,256]{1,0:T(1,128)S(1)}, f32[1,256]{1,0:T(1,128)S(1)}, u32[]{:S(2)}, u32[]{:S(2)}) %collective-permute-start.5) | collective-permute-done | bytes 1056 | tf_op jit(solution)/shard_map/ppermute | solution.py:409
  63.7 0.0 collective-permute-start.6
  63.7 3.1 %shard_map.137.refs_1_ = bf16[1,16,64,256]{3,2,1,0:T(8,128)(2,1)S(1)} custom-call(bf16[4,16,64,256]{3,2,1,0:T(8,128)(2,1)S(1)} %shard_map.133.refs_0_.refs_6_.refs_2_, s32[1,1024]{1,0:T(1,128)S(1)} %bitcast.14, f32[4,256,256]{2,1,0:T(8,128)S(1)} %get-tuple-element.16.refs_8_.refs_2_, bf16[2,64,128]{2,1,0:T(8,128)(2,1)S(1)} %copy-done.7, f32[2,64]{1,0:T(2,128)S(1)} %copy-done.9), custom_call_target="tpu_custom_call" | custom-call | flops 1073741824 | bytes 2097152 | tf_op jit(solution)/shard_map/pallas_call | solution.py:295
  66.8 0.5 collective-permute-done.6
  67.3 0.0 collective-permute-start.7
  67.3 3.1 %shard_map.136.refs_0_ = bf16[1,16,64,256]{3,2,1,0:T(8,128)(2,1)S(1)} custom-call(bf16[4,16,64,256]{3,2,1,0:T(8,128)(2,1)S(1)} %shard_map.133.refs_0_.refs_6_.refs_2_, s32[1,1024]{1,0:T(1,128)S(1)} %bitcast.15, f32[4,256,256]{2,1,0:T(8,128)S(1)} %get-tuple-element.16.refs_8_.refs_2_, bf16[2,64,128]{2,1,0:T(8,128)(2,1)S(1)} %copy-done.7, f32[2,64]{1,0:T(2,128)S(1)} %copy-done.9), custom_call_target="tpu_custom_call" | custom-call | flops 1073741824 | bytes 2097152 | tf_op jit(solution)/shard_map/pallas_call | solution.py:295
  70.3 0.5 collective-permute-done.7
  70.8 0.8 %collective-permute-start.8 = (f32[1,256]{1,0:T(1,128)S(1)}, f32[1,256]{1,0:T(1,128)S(1)}, u32[]{:S(2)}, u32[]{:S(2)}) collective-permute-start(f32[1,256]{1,0:T(1,128)S(1)} %add.17), channel_id=1, source_target_pairs={{0,2},{1,3},{2,0},{3,1},{4,6},{5,7},{6,4},{7,5},{8,10},{9,11},{10,... | collective-permute-start | bytes 3080 | tf_op jit(solution)/shard_map/ppermute | solution.py:409
  71.6 1.6 %shard_map.139.refs_5_ = bf16[1024,1024]{1,0:T(8,128)(2,1)} custom-call(bf16[1,16,64,256]{3,2,1,0:T(8,128)(2,1)S(1)} %shard_map.138.refs_0_, bf16[1,16,64,256]{3,2,1,0:T(8,128)(2,1)S(1)} %shard_map.134.refs_12_.refs_1_, bf16[4,16,64,256]{3,2,1,0:T(8,128)(2,1)S(1)} %shard_map.133.refs_0_.refs_6_.refs_2_, ...), custom_call_target="tpu_custom_call" | custom-call | flops 1073741824 | bytes 8388608 | tf_op jit(solution)/shard_map/pallas_call | solution.py:360
  73.2 1.2 %collective-permute-done.8 = f32[1,256]{1,0:T(1,128)S(1)} collective-permute-done((f32[1,256]{1,0:T(1,128)S(1)}, f32[1,256]{1,0:T(1,128)S(1)}, u32[]{:S(2)}, u32[]{:S(2)}) %collective-permute-start.8) | collective-permute-done | bytes 1056 | tf_op jit(solution)/shard_map/ppermute | solution.py:409
  74.4 0.0 collective-permute-start.9
  74.4 1.6 %shard_map.140 = bf16[1024,1024]{1,0:T(8,128)(2,1)} custom-call(bf16[1,16,64,256]{3,2,1,0:T(8,128)(2,1)S(1)} %shard_map.136.refs_0_, bf16[1,16,64,256]{3,2,1,0:T(8,128)(2,1)S(1)} %shard_map.137.refs_1_, bf16[4,16,64,256]{3,2,1,0:T(8,128)(2,1)S(1)} %shard_map.133.refs_0_.refs_6_.refs_2_, ...), custom_call_target="tpu_custom_call", output_to_operand_aliasing={{}: (5, {})} | custom-call | flops 1073741824 | bytes 8388608 | tf_op jit(solution)/shard_map/pallas_call | solution.py:360
  76.0 0.0 collective-permute-done.9
  76.0 0.6 add_reduce_fusion
  (5 shorter events, 0.1 us)
Async XLA Ops:
  0.6 1.2 %copy-start.3 = (f32[4096,64]{0,1:T(8,128)S(1)}, f32[4096,64]{0,1:T(8,128)}, u32[]{:S(2)}) copy-start(f32[4096,64]{0,1:T(8,128)} %param.11) | copy-start | bytes 3145732
  1.9 3.1 %copy-start.1 = (bf16[1024,1024]{1,0:T(8,128)(2,1)S(1)}, bf16[1024,1024]{1,0:T(8,128)(2,1)}, u32[]{:S(2)}) copy-start(bf16[1024,1024]{1,0:T(8,128)(2,1)} %refs_0_.1) | copy-start | bytes 6291460
  1.9 3.1 %copy-start.2 = (f32[1024,256]{1,0:T(8,128)S(1)}, f32[1024,256]{1,0:T(8,128)}, u32[]{:S(2)}) copy-start(f32[1024,256]{1,0:T(8,128)} %refs_2_.1) | copy-start | bytes 3145732
  1.9 3.1 %copy-start.7 = (bf16[2,64,128]{2,1,0:T(8,128)(2,1)S(1)}, bf16[2,64,128]{2,1,0:T(8,128)(2,1)}, u32[]{:S(2)}) copy-start(bf16[2,64,128]{2,1,0:T(8,128)(2,1)} %refs_3_.9) | copy-start | bytes 98308
  1.9 3.1 %copy-start.8 = (s32[1024]{0:T(1024)S(1)}, s32[1024]{0:T(1024)}, u32[]{:S(2)}) copy-start(s32[1024]{0:T(1024)} %param.14) | copy-start | bytes 12292
  1.9 3.1 %copy-start.9 = (f32[2,64]{1,0:T(2,128)S(1)}, f32[2,64]{1,0:T(2,128)}, u32[]{:S(2)}) copy-start(f32[2,64]{1,0:T(2,128)} %refs_4_.13) | copy-start | bytes 1540
  1.9 13.1 %collective-permute-start = (bf16[64,2048]{1,0:T(8,128)(2,1)S(1)}, bf16[64,2048]{1,0:T(8,128)(2,1)S(1)}, u32[]{:S(2)}, u32[]{:S(2)}) collective-permute-start(bf16[64,2048]{1,0:T(8,128)(2,1)S(1)} %shard_map.130), channel_id=1, source_target_pairs={{28,0},{29,1},{6,2},{7,3},{0,4},{1,5},{10,6},{11,7},{4,8},{5,9},{1... | collective-permute-start | bytes 786440 | tf_op jit(solution)/shard_map/ppermute | solution.py:403
  4.9 10.1 %copy-start.4 = (bf16[2,192,192]{2,1,0:T(8,128)(2,1)S(1)}, bf16[2,192,192]{2,1,0:T(8,128)(2,1)}, u32[]{:S(2)}) copy-start(bf16[2,192,192]{2,1,0:T(8,128)(2,1)} %refs_9_.1) | copy-start | bytes 442372
  5.0 10.1 %copy-start.5 = (s32[1024,16]{0,1:T(8,128)S(1)}, s32[1024,16]{0,1:T(8,128)}, u32[]{:S(2)}) copy-start(s32[1024,16]{0,1:T(8,128)} %param.13) | copy-start | bytes 196612
  5.0 10.1 %copy-start.6 = (bf16[2,64,64]{2,1,0:T(8,128)(2,1)S(1)}, bf16[2,64,64]{2,1,0:T(8,128)(2,1)}, u32[]{:S(2)}) copy-start(bf16[2,64,64]{2,1,0:T(8,128)(2,1)} %refs_10_.1) | copy-start | bytes 49156
  15.0 21.8 %copy-start = (bf16[2,64,64]{2,1,0:T(8,128)(2,1)S(1)}, bf16[2,64,64]{2,1,0:T(8,128)(2,1)}, u32[]{:S(2)}) copy-start(bf16[2,64,64]{2,1,0:T(8,128)(2,1)} %refs_4_.15) | copy-start | bytes 49156
  29.9 11.1 %collective-permute-start.4 = (bf16[64,1024]{1,0:T(8,128)(2,1)S(1)}, bf16[64,1024]{1,0:T(8,128)(2,1)S(1)}, u32[]{:S(2)}, u32[]{:S(2)}) collective-permute-start(bf16[64,1024]{1,0:T(8,128)(2,1)S(1)} %get-tuple-element.19.refs_2_), channel_id=1, source_target_pairs={{0,30},{1,31},{2,0},{3,1},{4,2},{5,3},{6,4},{7,5},{8,6},{9,7},{10,... | collective-permute-start | bytes 393224 | tf_op jit(solution)/shard_map/ppermute | solution.py:378
  35.6 5.3 %collective-permute-start.3 = (bf16[64,1024]{1,0:T(8,128)(2,1)S(1)}, bf16[64,1024]{1,0:T(8,128)(2,1)S(1)}, u32[]{:S(2)}, u32[]{:S(2)}) collective-permute-start(bf16[64,1024]{1,0:T(8,128)(2,1)S(1)} %get-tuple-element.19.refs_2_), channel_id=1, source_target_pairs={{0,31},{1,0},{2,1},{3,2},{4,3},{5,4},{6,5},{7,6},{8,7},{9,8},{10,9... | collective-permute-start | bytes 393224 | tf_op jit(solution)/shard_map/ppermute | solution.py:378
  35.6 8.3 %collective-permute-start.2 = (bf16[64,1024]{1,0:T(8,128)(2,1)S(1)}, bf16[64,1024]{1,0:T(8,128)(2,1)S(1)}, u32[]{:S(2)}, u32[]{:S(2)}) collective-permute-start(bf16[64,1024]{1,0:T(8,128)(2,1)S(1)} %get-tuple-element.19.refs_2_), channel_id=1, source_target_pairs={{0,1},{1,2},{2,3},{3,4},{4,5},{5,6},{6,7},{7,8},{8,9},{9,10},{10,1... | collective-permute-start | bytes 393224 | tf_op jit(solution)/shard_map/ppermute | solution.py:378
  36.1 10.0 %collective-permute-start.1 = (bf16[64,1024]{1,0:T(8,128)(2,1)S(1)}, bf16[64,1024]{1,0:T(8,128)(2,1)S(1)}, u32[]{:S(2)}, u32[]{:S(2)}) collective-permute-start(bf16[64,1024]{1,0:T(8,128)(2,1)S(1)} %get-tuple-element.19.refs_2_), channel_id=1, source_target_pairs={{0,2},{1,3},{2,4},{3,5},{4,6},{5,7},{6,8},{7,9},{8,10},{9,11},{10,... | collective-permute-start | bytes 393224 | tf_op jit(solution)/shard_map/ppermute | solution.py:378
  37.9 8.3 %copy-start.10 = (f32[64]{0:T(128)S(1)}, f32[64]{0:T(128)}, u32[]{:S(2)}) copy-start(f32[64]{0:T(128)} %param.21) | copy-start | bytes 772
  59.2 4.5 %collective-permute-start.5 = (f32[1,256]{1,0:T(1,128)S(1)}, f32[1,256]{1,0:T(1,128)S(1)}, u32[]{:S(2)}, u32[]{:S(2)}) collective-permute-start(f32[1,256]{1,0:T(1,128)S(1)} %get-tuple-element.26), channel_id=1, source_target_pairs={{0,16},{4,20},{8,24},{12,28},{16,0},{20,4},{24,8},{28,12},{1,17},{... | collective-permute-start | bytes 3080 | tf_op jit(solution)/shard_map/ppermute | solution.py:409
  63.7 3.6 %collective-permute-start.6 = (f32[1,256]{1,0:T(1,128)S(1)}, f32[1,256]{1,0:T(1,128)S(1)}, u32[]{:S(2)}, u32[]{:S(2)}) collective-permute-start(f32[1,256]{1,0:T(1,128)S(1)} %add.15), channel_id=1, source_target_pairs={{0,8},{4,12},{8,0},{12,4},{16,24},{20,28},{24,16},{28,20},{1,9},{5... | collective-permute-start | bytes 3080 | tf_op jit(solution)/shard_map/ppermute | solution.py:409
  67.3 3.6 %collective-permute-start.7 = (f32[1,256]{1,0:T(1,128)S(1)}, f32[1,256]{1,0:T(1,128)S(1)}, u32[]{:S(2)}, u32[]{:S(2)}) collective-permute-start(f32[1,256]{1,0:T(1,128)S(1)} %add.16), channel_id=1, source_target_pairs={{0,4},{4,0},{8,12},{12,8},{16,20},{20,16},{24,28},{28,24},{1,5},{5... | collective-permute-start | bytes 3080 | tf_op jit(solution)/shard_map/ppermute | solution.py:409
  70.8 3.6 %collective-permute-start.8 = (f32[1,256]{1,0:T(1,128)S(1)}, f32[1,256]{1,0:T(1,128)S(1)}, u32[]{:S(2)}, u32[]{:S(2)}) collective-permute-start(f32[1,256]{1,0:T(1,128)S(1)} %add.17), channel_id=1, source_target_pairs={{0,2},{1,3},{2,0},{3,1},{4,6},{5,7},{6,4},{7,5},{8,10},{9,11},{10,... | collective-permute-start | bytes 3080 | tf_op jit(solution)/shard_map/ppermute | solution.py:409
  74.4 1.6 %collective-permute-start.9 = (f32[1,256]{1,0:T(1,128)S(1)}, f32[1,256]{1,0:T(1,128)S(1)}, u32[]{:S(2)}, u32[]{:S(2)}) collective-permute-start(f32[1,256]{1,0:T(1,128)S(1)} %add.18), channel_id=1, source_target_pairs={{0,1},{1,0},{2,3},{3,2},{4,5},{5,4},{6,7},{7,6},{8,9},{9,8},{10,11... | collective-permute-start | bytes 3080 | tf_op jit(solution)/shard_map/ppermute | solution.py:409
